TPU v7x, 32 devices: a whole 2x2x4 slice. The times are simulated.
32 devices in a mesh: row: 8 (over z, x), col: 4 (over y, core).
Axes of the slice: x: 2, y: 2, z: 4, core: 2. Of those that a mesh axis runs over, the one named last changes fastest.
Arguments:
- eigen_vectors: float32 [8192, 2048], P('row', 'col'), may hold values from -6 to 6
- panel_first: float32 [8192, 512], P('row', 'col'), may hold values from -0.0625 to 0.0625
- panel_second: float32 [8192, 512], P('row', 'col'), may hold values from -0.0625 to 0.0625
- factor_first: float32 [512, 512], replicated, as said below
- factor_second: float32 [512, 512], replicated, as said below
Outputs:
- transformed: float32 [8192, 2048], P('row', 'col')
Inputs may be any that keep to these rules, and one draw needn't show every extreme that they name: factor_first is upper triangular. factor_second is upper triangular.
All inputs are finite; a program needn't handle non-finite values.
Results may differ from a plain program's by a relative error of at most 0.0001.
Values sent between devices are 32-bit elements; how exact they have to be, the bound alone decides.
No kernel may reach another device: no remote copies, remote signals or barrier semaphores. Data moves between devices by JAX's collectives and lax.ppermute only.
A program may use at most 64 MiB of HBM per device.

v0:
```python
import jax
import jax.numpy as jnp
from jax import lax
from jax.sharding import PartitionSpec as P


def local_dot(left, right):
    return jnp.dot(left, right, precision=lax.Precision.HIGHEST, preferred_element_type=jnp.float32)


def on_device(eigen_vectors, panel_first, panel_second, factor_first, factor_second):
    vectors_first, vectors_second = (
        lax.all_gather(panel_first, "col", axis=1, tiled=True),
        lax.all_gather(panel_second, "col", axis=1, tiled=True),
    )
    updated = eigen_vectors
    for vectors, factor in ((vectors_second, factor_second), (vectors_first, factor_first)):
        projected = lax.psum(local_dot(vectors.T, updated), "row")
        updated = updated - local_dot(vectors, local_dot(factor, projected))
    return updated


def solution(mesh):
    return jax.shard_map(
        on_device,
        mesh=mesh,
        in_specs=(P("row", "col"), P("row", "col"), P("row", "col"), P(), P()),
        out_specs=P("row", "col"),
        check_vma=False,
    )
```

profile of v0, /device:TPU:0, one launch (start us, length us, event | category | flops | bytes accessed | tf_op | source)
XLA Modules:
  0.0 245.9 jit_solution(11160234855744080831)
XLA Ops:
  6.5 0.0 copy-start
  6.5 0.0 all-gather.3.cloned.1.call-start
  6.5 0.7 all-gather.3.cloned.1.call-update
  7.3 0.0 all-reduce.3.cloned.1.call-start
  7.3 27.2 %all-gather.3.cloned.1.call-done = f32[1024,512]{1,0:T(8,128)} async-done(((f32[1024,128]{1,0:T(8,128)}), f32[1024,512]{1,0:T(8,128)}) %all-gather.3.cloned.1.call-update) | async-done | bytes 2097168 | tf_op jit(solution)/shard_map/all_gather | solution.py:14
  34.5 0.0 copy-start.3
  34.5 6.9 %fusion = f32[512,512]{1,0:T(8,128)} fusion(f32[1024,512]{1,0:T(8,128)} %all-gather.3.cloned.1.call-done, f32[1024,512]{1,0:T(8,128)} %param.5), kind=kOutput, calls=%fused_computation.3 | convolution fusion | flops 3221225472 | bytes 5242880 | tf_op jit(solution)/shard_map/dot_general | solution.py:8
  41.3 0.0 all-reduce.3.cloned.1.call-update
  41.4 0.0 all-gather.5.cloned.1.call-start
  41.4 0.7 all-gather.5.cloned.1.call-update
  42.1 0.0 all-reduce.5.cloned.1.call-start
  42.2 0.0 copy-done.3
  42.2 1.8 copy.6
  44.0 75.5 %all-reduce.3.cloned.1.call-done = f32[512,512]{1,0:T(8,128)} async-done(((f32[512,512]{1,0:T(8,128)}), f32[512,512]{1,0:T(8,128)}) %all-reduce.3.cloned.1.call-update) | async-done | bytes 1048592 | tf_op jit(solution)/shard_map/psum | solution.py:18
  119.5 0.0 copy-done
  119.5 0.0 copy-start.1
  119.5 4.8 %fusion.1 = f32[512,512]{1,0:T(8,128)S(1)} fusion(f32[512,512]{1,0:T(8,128)} %all-reduce.3.cloned.1.call-done, f32[512,512]{1,0:T(8,128)S(1)} %copy-done), kind=kOutput, calls=%fused_computation.4 | convolution fusion | flops 1610612736 | bytes 3145728 | tf_op jit(solution)/shard_map/dot_general | solution.py:8
  124.4 0.0 copy-done.1
  124.4 5.2 %bitcast_subtract_fusion.1 = f32[1024,512]{0,1:T(8,128)S(1)} fusion(f32[1024,512]{0,1:T(8,128)} %copy.6, f32[512,512]{1,0:T(8,128)S(1)} %fusion.1, f32[1024,512]{1,0:T(8,128)S(1)} %copy-done.1), kind=kOutput, calls=%fused_computation.1 | convolution fusion | flops 3221749760 | bytes 7340032 | tf_op jit(solution)/shard_map/dot_general | solution.py:8
  129.5 14.1 %all-gather.5.cloned.1.call-done = f32[1024,512]{1,0:T(8,128)} async-done(((f32[1024,128]{1,0:T(8,128)}), f32[1024,512]{1,0:T(8,128)}) %all-gather.5.cloned.1.call-update) | async-done | bytes 2097168 | tf_op jit(solution)/shard_map/all_gather | solution.py:13
  143.6 6.1 %convolution_bitcast_fusion = f32[512,512]{0,1:T(8,128)} fusion(f32[1024,512]{0,1:T(8,128)S(1)} %bitcast_subtract_fusion.1, f32[1024,512]{1,0:T(8,128)} %all-gather.5.cloned.1.call-done), kind=kOutput, calls=%fused_computation.2 | convolution fusion | flops 3221225472 | bytes 5242880 | tf_op jit(solution)/shard_map/dot_general | solution.py:8
  149.7 0.0 all-reduce.5.cloned.1.call-update
  149.7 78.1 %all-reduce.5.cloned.1.call-done = f32[512,512]{0,1:T(8,128)} async-done(((f32[512,512]{0,1:T(8,128)}), f32[512,512]{0,1:T(8,128)}) %all-reduce.5.cloned.1.call-update) | async-done | bytes 1048592 | tf_op jit(solution)/shard_map/psum | solution.py:18
  227.8 0.0 copy-start.2
  227.8 3.5 %fusion.2 = f32[512,512]{1,0:T(8,128)S(1)} fusion(f32[512,512]{0,1:T(8,128)} %all-reduce.5.cloned.1.call-done, f32[512,512]{1,0:T(8,128)} %param.8), kind=kOutput, calls=%fused_computation.5 | convolution fusion | flops 1610612736 | bytes 3145728 | tf_op jit(solution)/shard_map/dot_general | solution.py:8
  231.3 0.0 copy-done.2
  231.3 5.1 %bitcast_subtract_fusion = f32[1024,512]{0,1:T(8,128)} fusion(f32[1024,512]{0,1:T(8,128)S(1)} %bitcast_subtract_fusion.1, f32[512,512]{1,0:T(8,128)S(1)} %fusion.2, f32[1024,512]{1,0:T(8,128)S(1)} %copy-done.2), kind=kOutput, calls=%fused_computation | convolution fusion | flops 3221749760 | bytes 7340032 | tf_op jit(solution)/shard_map/dot_general | solution.py:8
  236.5 2.9 %copy.7 = f32[1024,512]{1,0:T(8,128)} copy(f32[1024,512]{0,1:T(8,128)} %bitcast_subtract_fusion) | data formatting | bytes 4194304 | tf_op jit(solution)/shard_map/sub | solution.py:19
Async XLA Ops:
  6.5 113.0 %copy-start = (f32[512,512]{1,0:T(8,128)S(1)}, f32[512,512]{1,0:T(8,128)}, u32[]{:S(2)}) copy-start(f32[512,512]{1,0:T(8,128)} %param.9) | copy-start | bytes 3145732
  6.5 27.9 %all-gather.3.cloned.1.call-start = ((), (), s32[]{:S(2)}) async-start(), calls=%async_computation | async-start | bytes 2621440 | tf_op jit(solution)/shard_map/all_gather | solution.py:14
  7.3 112.2 %all-reduce.3.cloned.1.call-start = ((), (), s32[]{:S(2)}) async-start(), calls=%async_computation.1 | async-start | bytes 2097152 | tf_op jit(solution)/shard_map/psum | solution.py:18
  34.5 7.7 %copy-start.3 = (f32[1024,512]{1,0:T(8,128)S(1)}, f32[1024,512]{1,0:T(8,128)}, u32[]{:S(2)}) copy-start(f32[1024,512]{1,0:T(8,128)} %param.5) | copy-start | bytes 6291460
  41.4 102.2 %all-gather.5.cloned.1.call-start = ((), (), s32[]{:S(2)}) async-start(), calls=%async_computation.2 | async-start | bytes 2621440 | tf_op jit(solution)/shard_map/all_gather | solution.py:13
  42.1 185.6 %all-reduce.5.cloned.1.call-start = ((), (), s32[]{:S(2)}) async-start(), calls=%async_computation.3 | async-start | bytes 2097152 | tf_op jit(solution)/shard_map/psum | solution.py:18
  119.5 4.9 %copy-start.1 = (f32[1024,512]{1,0:T(8,128)S(1)}, f32[1024,512]{1,0:T(8,128)}, u32[]{:S(2)}) copy-start(f32[1024,512]{1,0:T(8,128)} %all-gather.3.cloned.1.call-done) | copy-start | bytes 6291460
  227.8 3.6 %copy-start.2 = (f32[1024,512]{1,0:T(8,128)S(1)}, f32[1024,512]{1,0:T(8,128)}, u32[]{:S(2)}) copy-start(f32[1024,512]{1,0:T(8,128)} %all-gather.5.cloned.1.call-done) | copy-start | bytes 6291460
Sparse Core Ops, SparseCore 0:
  8.9 25.5 all-gather.2
  41.5 77.9 all-reduce.2
  121.1 22.4 all-gather.4
  149.8 77.8 all-reduce.4
where the time goes:
time: 246 us
  waiting for transfers between devices  196 us (80%)
  matrix products  31.6 us (13%)
  between operations  13.2 us (5%)
  local copies, waits for them, and re-layouts  4.71 us (2%)
    psum x2, waiting for transfers between devices, on_device(): projected = lax.psum(local_dot(vectors.T, updated), 'row')  154 us
    dot_general x6, matrix products, local_dot(): jnp.dot(left, right, precision=lax.Precision.HIGHEST, preferred_element_t...  31.6 us
    all_gather x1, waiting for transfers between devices, on_device(): lax.all_gather(panel_second, 'col', axis=1, tiled=True)  27.2 us
    all_gather x1, waiting for transfers between devices, on_device(): lax.all_gather(panel_first, 'col', axis=1, tiled=True)  14.1 us
  transfers between devices with their start and end apart: 4, of which 4 were waited for; matrix products, arithmetic and copies ran while one was open for 5% of the time, Pallas kernels for 0%

commit v1 on v0

v1 whole, which is shorter than its diff:
```python
import functools

import jax
import jax.numpy as jnp
from jax import lax
from jax.experimental import pallas as pl
from jax.experimental.pallas import tpu as pltpu
from jax.sharding import PartitionSpec as P

GROUP = 4
MIB = 1 << 20
NT = (((1,), (1,)), ((), ()))
NN = (((1,), (0,)), ((), ()))


def split(value):
    high = value.astype(jnp.bfloat16)
    return high, (value - high.astype(jnp.float32)).astype(jnp.bfloat16)


def dot3(left, right, dims):
    def one(a, b):
        return lax.dot_general(a, b, dims, preferred_element_type=jnp.float32)

    return one(left[0], right[1]) + one(left[1], right[0]) + one(left[0], right[0])


def joined(refs):
    return jnp.concatenate([ref[...] for ref in refs], axis=1)


def stacked(refs, cols=slice(None)):
    return jnp.concatenate([ref[:, cols] for ref in refs], axis=0)


def block(index, size):
    return pl.ds(pl.multiple_of(index * size, size), size)


def prepare_kernel(place, x, v, lt_high, lt_low, x_in, v_in, v_high, v_low, sems):
    wide, thin = x.shape[1] // GROUP, v.shape[1] // GROUP
    copies = [pltpu.make_async_copy(x.at[:, block(place[p], wide)], x_in.at[p], sems.at[p]) for p in range(GROUP)]
    copies.append(pltpu.make_async_copy(v, v_in, sems.at[GROUP]))
    for copy in copies:
        copy.start()
    for p in range(GROUP):
        copies[p].wait()
        high, rest = split(x_in[p])
        lt_high[p * wide : (p + 1) * wide, :] = high.T
        lt_low[p * wide : (p + 1) * wide, :] = rest.T
    copies[GROUP].wait()
    high, rest = split(v_in[...])
    v_high[...] = high.T
    v_low[...] = rest.T
    for p in range(GROUP):
        rows = slice(x.shape[1] + p * thin, x.shape[1] + (p + 1) * thin)
        lt_high[rows, :] = v_high[block(place[p], thin), :]
        lt_low[rows, :] = v_low[block(place[p], thin), :]


def arrange_kernel(width, place, t, t_high, t_low):
    col = place[GROUP]
    for i in range(t.shape[0] // width):
        for j in range(t.shape[0] // width):
            high, rest = split(t[block(col ^ i, width), block(col ^ j, width)])
            at = (slice(i * width, (i + 1) * width), slice(j * width, (j + 1) * width))
            t_high[at] = high
            t_low[at] = rest


def project_kernel(pairs, lt_high, lt_low, *refs):
    vectors, outs = refs[: 2 * pairs], refs[-2:]
    rows = outs[0].shape[0]
    left = (lt_high[: 2 * rows, :], lt_low[: 2 * rows, :])
    for k in range(pairs):
        total = dot3(left, split(joined(vectors[2 * k : 2 * k + 2])), NN)
        size = total.shape[1]
        for i in range(2):
            outs[i][:, k * size : (k + 1) * size] = total[i * rows : (i + 1) * rows, :]


def project_cross_kernel(lt_high, lt_low, near0, near1, far0, far1, *outs):
    thin = near0.shape[1] // GROUP
    cols = lt_high.shape[0] - GROUP * thin
    wide = cols // GROUP
    total = dot3((lt_high[...], lt_low[...]), split(joined((far0, far1))), NN)
    cross = dot3((lt_high[cols:, :], lt_low[cols:, :]), split(joined((near0, near1))), NN)
    for p in range(GROUP):
        out, at = outs[p // 2], (p % 2) * (wide + 2 * thin)
        out[at : at + wide, :] = total[p * wide : (p + 1) * wide, :]
        out[at + wide : at + wide + thin, :] = cross[p * thin : (p + 1) * thin, :]
        out[at + wide + thin : at + wide + 2 * thin, :] = total[cols + p * thin : cols + (p + 1) * thin, :]


def fold_kernel(keep, got, *refs):
    mine, other = refs[-2:]
    rows = mine.shape[0]
    mine[...] = keep[:rows, :] + got[:rows, :]
    other[...] = keep[rows:, :] + got[rows:, :]


def add_kernel(left, right, *refs):
    refs[-1][...] = left[...] + right[...]


def pile_kernel(count, *refs):
    parts, out = refs[:count], refs[-1]
    at = 0
    for part in parts:
        out[at : at + part.shape[0], :] = part[...]
        at += part.shape[0]


def cross_kernel(wide, place, low, high, out):
    width = out.shape[0] // 2
    half = out.shape[1] // 2
    thin = width // GROUP
    size = low.shape[0] // 2
    for i in range(2):
        for j in range(2):
            for p in range(GROUP):
                at = (p % 2) * size + wide + (2 * i + j) * thin
                to = pl.ds(pl.multiple_of(i * width + place[p] * thin, thin), thin)
                out[to, j * half : (j + 1) * half] = (low, high)[p // 2][at : at + thin, :]


def factor_kernel(t_high, t_low, v0, v1, v2, v3, w_high, w_low):
    tile = v0.shape[0] // 2
    right = (t_high[...], t_low[...])
    for i in range(2):
        at = slice(i * tile, (i + 1) * tile)
        left = split(jnp.concatenate([v[at, :] for v in (v0, v1, v2, v3)], axis=1))
        w_high[at, :], w_low[at, :] = split(dot3(left, right, NN))


def near_kernel(place, x, t_high, t_low, w_high, w_low, low, high, out, c):
    half = low.shape[1] // 2
    wide = low.shape[0] // 2
    p2 = split(stacked((low, high), slice(0, half)))
    c[...] = dot3(p2, (t_high[:, :half], t_low[:, :half]), NT)
    tile = x.shape[0] // 2
    for i in range(2):
        at = slice(i * tile, (i + 1) * tile)
        change = dot3((w_high[at, :half], w_low[at, :half]), p2, NT)
        for p in range(GROUP):
            cols = slice(p * wide, (p + 1) * wide)
            out[at, cols] = x[at, block(place[p], wide)] - change[:, cols]


def middle_kernel(x, t_high, t_low, w2_high, w2_low, w1_high, w1_low, c, g, g_core, n_low, n_high, low, high, out, rest):
    half = rest.shape[1]
    wide = n_low.shape[0] // 2
    width = g.shape[0] // 2
    size = low.shape[0] // 2
    p2 = split(
        jnp.concatenate([(low, high)[p // 2][(p % 2) * size : (p % 2) * size + wide, :] for p in range(GROUP)], axis=0)
    )
    c2 = split(c[...] + dot3(p2, (t_high[:, half:], t_low[:, half:]), NT))
    parts = []
    for i in range(4):
        rows = (g_core if i % 2 else g)[(i // 2) * width : (i // 2 + 1) * width, :]
        parts.append(jnp.concatenate([rows[:, (j ^ i) * width : ((j ^ i) + 1) * width] for j in range(4)], axis=1))
    cross = dot3(c2, split(jnp.concatenate(parts, axis=0)), NT)
    rest[...] = cross[:, half:]
    p1 = split(stacked((n_low, n_high), slice(half, 2 * half)) - cross[:, :half])
    tile = x.shape[0] // 2
    for i in range(2):
        at = slice(i * tile, (i + 1) * tile)
        change = dot3((w2_high[at, half:], w2_low[at, half:]), p2, NT)
        out[at, :] = x[at, :] - (change + dot3((w1_high[at, :half], w1_low[at, :half]), p1, NT))


def last_kernel(place, x, w_high, w_low, rest, low, high, out, tiles, sems):
    wide, half = low.shape[0] // 2, low.shape[1]
    right = split(stacked((low, high)) - rest[...])
    count = tiles.shape[0]
    tile = tiles.shape[1]
    copies = []
    for i in range(count):
        at = slice(i * tile, (i + 1) * tile)
        change = dot3((w_high[at, half:], w_low[at, half:]), right, NT)
        for p in range(GROUP):
            cols = slice(p * wide, (p + 1) * wide)
            tiles[i, :, block(place[p], wide)] = x[at, cols] - change[:, cols]
        copies.append(pltpu.make_async_copy(tiles.at[i], out.at[at, :], sems.at[i]))
        copies[i].start()
    for copy in copies:
        copy.wait()


def call(kernel, outs, operands, macs=0, scalars=0, scratch=(), out_space=pltpu.VMEM):
    specs = [pl.BlockSpec(memory_space=pltpu.SMEM)] * scalars
    values = []
    for value in operands[scalars:]:
        if isinstance(value, InAny):
            specs.append(pl.BlockSpec(memory_space=pl.ANY))
            values.append(value.array)
        elif isinstance(value, InHbm):
            specs.append(pl.BlockSpec(memory_space=pltpu.HBM))
            values.append(pltpu.with_memory_space_constraint(value.array, pltpu.HBM))
        else:
            specs.append(pl.BlockSpec(memory_space=pltpu.VMEM))
            values.append(value)
    return pl.pallas_call(
        kernel,
        out_shape=tuple(jax.ShapeDtypeStruct(shape, dtype) for shape, dtype in outs),
        in_specs=specs,
        out_specs=tuple(pl.BlockSpec(memory_space=out_space) for _ in outs),
        scratch_shapes=list(scratch),
        compiler_params=pltpu.CompilerParams(vmem_limit_bytes=36 * MIB),
        cost_estimate=pl.CostEstimate(flops=6 * macs, bytes_accessed=4096, transcendentals=0),
    )(*operands[:scalars], *values)


class InHbm:
    def __init__(self, array):
        self.array = array


class InAny:
    def __init__(self, array):
        self.array = array


def after(value, *earlier):
    return lax.optimization_barrier((value, earlier))[0]


def on_device(row_size, col_size, x, panel_first, panel_second, factor_first, factor_second):
    f32, bf16 = jnp.float32, jnp.bfloat16
    rows, cols = x.shape
    width = panel_first.shape[1]
    total = factor_first.shape[0]
    half = total // 2
    wide, thin = cols // GROUP, width // GROUP
    tall = cols + width
    col = lax.axis_index("col")
    low = lax.axis_index("row") % GROUP
    one, two = 1 + col % 2, 2 - col % 2
    place = jnp.stack([low, low ^ two, low ^ one, low ^ 3, col]).astype(jnp.int32)

    def permute(value, target):
        pairs = [
            (r * col_size + c, target(r, c)[0] * col_size + target(r, c)[1]) for r in range(row_size) for c in range(col_size)
        ]
        return lax.ppermute(value, ("row", "col"), pairs)

    def to_col(value, flip):
        return permute(value, lambda r, c: (r, c ^ flip))

    def to_one(value):
        return permute(value, lambda r, c: (r ^ (1 + c % 2), c))

    def to_two(value):
        return permute(value, lambda r, c: (r ^ (2 - c % 2), c))

    def add(left, right, *pads):
        return call(add_kernel, [(left.shape, f32)], (left, right, *map(InAny, pads)))[0]

    def across(value, *earlier, pads=()):
        bit = GROUP
        while bit < row_size:
            got = after(permute(value, lambda r, c, bit=bit: (r ^ bit, c)), *earlier)
            value = add(value, got, *pads)
            bit *= 2
        return value

    def pad(value):
        return to_col(value[:wide], 1)

    def fold(keep, sent, *pads):
        shape = (keep.shape[0] // 2, keep.shape[1])
        return call(fold_kernel, [(shape, f32)] * 2, (keep, to_one(sent), *map(InAny, pads)))

    def pile(*parts, pads=()):
        shape = (sum(p.shape[0] for p in parts), parts[0].shape[1])
        return call(functools.partial(pile_kernel, len(parts)), [(shape, f32)], (*parts, *map(InAny, pads)))[0]

    def spread(mine, *earlier):
        pair = pile(mine, after(to_two(mine), *earlier))
        return pair, to_one(pair)

    second_far = to_col(panel_second, 2)
    first_far = to_col(panel_first, 2)
    second_near = (panel_second, to_col(panel_second, 1))
    first_near = (panel_first, to_col(panel_first, 1))

    lt_high, lt_low = call(
        prepare_kernel,
        [((tall, rows), bf16)] * 2,
        (place, InHbm(x), InHbm(panel_first)),
        scalars=1,
        scratch=[
            pltpu.VMEM((GROUP, rows, wide), f32),
            pltpu.VMEM((rows, width), f32),
            pltpu.VMEM((width, rows), bf16),
            pltpu.VMEM((width, rows), bf16),
            pltpu.SemaphoreType.DMA((GROUP + 1,)),
        ],
    )
    near_parts = call(
        functools.partial(project_kernel, 2),
        [((2 * wide, total), f32)] * 2,
        (lt_high, lt_low, *second_near, *first_near),
    )
    second_far = after(second_far, near_parts)
    second_far = (second_far, to_col(second_far, 1))
    second = second_near + second_far
    near_mine, near_other = fold(*near_parts)
    near_sum = near_mine + to_two(near_other)
    second_parts = call(
        project_cross_kernel,
        [((2 * (wide + 2 * thin), half), f32)] * 2,
        (lt_high, lt_low, *second_near, after(second_far[0], near_other), second_far[1]),
    )
    second_mine, second_other = fold(second_parts[0], second_parts[1], pad(near_sum))
    second_sum = second_mine + to_two(second_other)

    near_sum = across(near_sum)
    first_far = after(first_far, second_other)
    first_far = (first_far, to_col(first_far, 1))
    first = first_near + first_far
    first_parts = call(
        functools.partial(project_kernel, 1),
        [((2 * wide, half), f32)] * 2,
        (lt_high, lt_low, *first_far),
    )
    second_sum = across(after(second_sum, near_sum))
    near = spread(near_sum)
    first_mine, first_other = fold(*first_parts)
    first_sum = first_mine + to_two(first_other)

    arrange = functools.partial(call, functools.partial(arrange_kernel, width), [((total, total), bf16)] * 2, scalars=1)
    factor = functools.partial(call, factor_kernel, [((rows, total), bf16)] * 2)
    t1 = arrange((place, factor_first), rows * total // 2)
    t2 = arrange((place, factor_second), rows * total // 2)
    w2 = factor((*t2, *second), rows * total * total)
    w1 = factor((*t1, *first), rows * total * total)
    left, coefficients = call(
        near_kernel,
        [((rows, cols), f32), ((cols, total), f32)],
        (place, x, *t2, *w2, *near),
        (rows + total) * cols * half,
        scalars=1,
    )

    second_sum = pile(second_sum, after(to_col(second_sum[wide:], 2), first_parts))
    second_blocks = spread(second_sum, w1, w2, first_other)
    first_sum = across(first_sum)
    (cross,) = call(
        functools.partial(cross_kernel, wide), [((2 * width, total), f32)], (place, *after(second_blocks, left, first_sum)), scalars=1
    )
    cross_core = to_col(cross, 1)
    first_blocks = spread(first_sum)

    left, rest = call(
        middle_kernel,
        [((rows, cols), f32), ((cols, half), f32)],
        (left, *t2, *w2, *w1, coefficients, cross, cross_core, *near, *second_blocks),
        (2 * rows + 2 * total) * cols * half,
    )
    tiles = 4
    (out,) = call(
        last_kernel,
        [((rows, cols), f32)],
        (place, left, *w1, rest, *first_blocks),
        rows * cols * half,
        scalars=1,
        scratch=[pltpu.VMEM((tiles, rows // tiles, cols), f32), pltpu.SemaphoreType.DMA((tiles,))],
        out_space=pl.ANY,
    )
    return out


def solution(mesh):
    return jax.shard_map(
        functools.partial(on_device, mesh.shape["row"], mesh.shape["col"]),
        mesh=mesh,
        in_specs=(P("row", "col"), P("row", "col"), P("row", "col"), P(), P()),
        out_specs=P("row", "col"),
        check_vma=False,
    )
```

time: 246 us -> 96.9 us (0.39)
  waiting for transfers between devices: 196 us -> 51.6 us
  matrix products: 31.6 us -> 0 us
  starting transfers between devices: 0.12 us -> 24.3 us
  Pallas kernels: 0 us -> 20.4 us
  between operations: 13.2 us -> 0.28 us
  local copies, waits for them, and re-layouts: 4.71 us -> 0.11 us
    psum x2 -> x0, waiting for transfers between devices: 154 us -> none  [on_device(): projected = lax.psum(local_dot(vectors.T, updated), 'row')]
    ppermute x0 -> x24, waiting for transfers between devices: none -> 51.6 us  [permute(): return lax.ppermute(value, ('row', 'col'), pairs)]
    all_gather x2 -> x0, waiting for transfers between devices: 41.2 us -> none  [the longest x1 27.2 us: on_device(): lax.all_gather(panel_second, 'col', axis=1, tiled=True)]
    dot_general x6 -> x0, matrix products: 31.6 us -> none  [local_dot(): jnp.dot(left, right, precision=lax.Precision.HIGHEST, preferred_element_t...]
    ppermute x0 -> x24, starting transfers between devices: none -> 24.3 us  [permute(): return lax.ppermute(value, ('row', 'col'), pairs)]
    pallas_call x0 -> x22, Pallas kernels: none -> 20.4 us  [call(): pl.pallas_call(kernel, out_shape=tuple((jax.ShapeDtypeStruct(shape, dtype...]
    sub x1 -> x0, local copies, waits for them, and re-layouts: 2.88 us -> none  [on_device(): updated = updated - local_dot(vectors, local_dot(factor, projected))]
  transfers between devices with their start and end apart: 4 -> 24, of which waited for: 4 -> 14; matrix products, arithmetic and copies ran while one was open for 5% -> 0% of each run, Pallas kernels for 0% -> 18%
where the time goes in v1:
time: 96.9 us; the launch traced here: 96.7 us
  waiting for transfers between devices  51.6 us (53%)
  starting transfers between devices  24.3 us (25%)
  Pallas kernels  20.4 us (21%)
    ppermute x24, waiting for transfers between devices, permute(): return lax.ppermute(value, ('row', 'col'), pairs)  51.6 us
    ppermute x24, starting transfers between devices, permute(): return lax.ppermute(value, ('row', 'col'), pairs)  24.3 us
    pallas_call x22, Pallas kernels, call(): pl.pallas_call(kernel, out_shape=tuple((jax.ShapeDtypeStruct(shape, dtype...  20.4 us
  transfers between devices with their start and end apart: 24, of which 14 were waited for; matrix products, arithmetic and copies ran while one was open for 0% of the time, Pallas kernels for 18%

profile of v1, /device:TPU:0, one launch (start us, length us, event | category | flops | bytes accessed | tf_op | source)
XLA Modules:
  0.0 96.7 jit_solution(6783178566591191586)
XLA Ops:
  0.5 2.9 %collective-permute-start.1 = (f32[1024,128]{1,0:T(8,128)}, f32[1024,128]{1,0:T(8,128)S(1)}, u32[]{:S(2)}, u32[]{:S(2)}) collective-permute-start(f32[1024,128]{1,0:T(8,128)} %near0.1), channel_id=1, source_target_pairs={{0,2},{1,3},{2,0},{3,1},{4,6},{5,7},{6,4},{7,5},{8,10},{9,11},{10,... | collective-permute-start | bytes 1572872 | tf_op jit(solution)/shard_map/ppermute | solution.py:246
  3.6 2.6 %shard_map.56 = (bf16[640,1024]{1,0:T(8,128)(2,1)S(1)}, bf16[640,1024]{1,0:T(8,128)(2,1)S(1)}) custom-call(s32[5]{0:T(128)S(1)} %stack.23.place, f32[1024,512]{1,0:T(8,128)} %x.3, f32[1024,128]{1,0:T(8,128)} %v0.3), custom_call_target="tpu_custom_call" | custom-call | bytes 4096 | tf_op jit(solution)/shard_map/pallas_call | solution.py:204
  6.2 1.8 %shard_map.57 = (f32[256,512]{1,0:T(8,128)S(1)}, f32[256,512]{1,0:T(8,128)S(1)}) custom-call(bf16[640,1024]{1,0:T(8,128)(2,1)S(1)} %get-tuple-element.41.lt_high, bf16[640,1024]{1,0:T(8,128)(2,1)S(1)} %get-tuple-element.42.lt_low, f32[1024,128]{1,0:T(8,128)S(1)} %copy-done.1, f32[1024,128]{1,0:T(8,128)S(1)} %collective-permute-done.refs_1_.v1.near1, ...), custom_call_target="tpu_custom_call" | custom-call | bytes 4096 | tf_op jit(solution)/shard_map/pallas_call | solution.py:204
  8.0 1.6 %collective-permute-start.4 = (f32[256,512]{1,0:T(8,128)S(1)}, f32[256,512]{1,0:T(8,128)S(1)}, u32[]{:S(2)}, u32[]{:S(2)}) collective-permute-start(f32[256,512]{1,0:T(8,128)S(1)} %get-tuple-element.44), channel_id=1, source_target_pairs={{0,4},{1,9},{2,6},{3,11},{4,0},{5,13},{6,2},{7,15},{8,12},{9,1},{1... | collective-permute-start | bytes 1572872 | tf_op jit(solution)/shard_map/ppermute | solution.py:246
  9.6 6.3 %collective-permute-done.1.v2.far0 = f32[1024,128]{1,0:T(8,128)S(1)} collective-permute-done((f32[1024,128]{1,0:T(8,128)}, f32[1024,128]{1,0:T(8,128)S(1)}, u32[]{:S(2)}, u32[]{:S(2)}) %collective-permute-start.1) | collective-permute-done | bytes 524320 | tf_op jit(solution)/shard_map/ppermute | solution.py:246
  15.9 1.4 %collective-permute-done.4.got = f32[256,512]{1,0:T(8,128)S(1)} collective-permute-done((f32[256,512]{1,0:T(8,128)S(1)}, f32[256,512]{1,0:T(8,128)S(1)}, u32[]{:S(2)}, u32[]{:S(2)}) %collective-permute-start.4) | collective-permute-done | bytes 524320 | tf_op jit(solution)/shard_map/ppermute | solution.py:246
  17.3 1.6 %collective-permute-start.5 = (f32[128,512]{1,0:T(8,128)S(1)}, f32[128,512]{1,0:T(8,128)S(1)}, u32[]{:S(2)}, u32[]{:S(2)}) collective-permute-start(f32[128,512]{1,0:T(8,128)S(1)} %get-tuple-element.49), channel_id=1, source_target_pairs={{0,8},{1,5},{2,10},{3,7},{4,12},{5,1},{6,14},{7,3},{8,0},{9,13},{1... | collective-permute-start | bytes 786440 | tf_op jit(solution)/shard_map/ppermute | solution.py:246
  19.5 1.4 %shard_map.64 = (f32[384,256]{1,0:T(8,128)S(1)}, f32[384,256]{1,0:T(8,128)S(1)}) custom-call(bf16[640,1024]{1,0:T(8,128)(2,1)S(1)} %get-tuple-element.41.lt_high, bf16[640,1024]{1,0:T(8,128)(2,1)S(1)} %get-tuple-element.42.lt_low, f32[1024,128]{1,0:T(8,128)S(1)} %copy-done.1, f32[1024,128]{1,0:T(8,128)S(1)} %collective-permute-done.refs_1_.v1.near1, ...), custom_call_target="tpu_custom_call" | custom-call | bytes 4096 | tf_op jit(solution)/shard_map/pallas_call | solution.py:204
  20.9 1.6 %collective-permute-start.10 = (f32[384,256]{1,0:T(8,128)S(1)}, f32[384,256]{1,0:T(8,128)S(1)}, u32[]{:S(2)}, u32[]{:S(2)}) collective-permute-start(f32[384,256]{1,0:T(8,128)S(1)} %get-tuple-element.55), channel_id=1, source_target_pairs={{0,4},{1,9},{2,6},{3,11},{4,0},{5,13},{6,2},{7,15},{8,12},{9,1},{1... | collective-permute-start | bytes 1179656 | tf_op jit(solution)/shard_map/ppermute | solution.py:246
  22.5 1.8 %collective-permute-done.5 = f32[128,512]{1,0:T(8,128)S(1)} collective-permute-done((f32[128,512]{1,0:T(8,128)S(1)}, f32[128,512]{1,0:T(8,128)S(1)}, u32[]{:S(2)}, u32[]{:S(2)}) %collective-permute-start.5) | collective-permute-done | bytes 262176 | tf_op jit(solution)/shard_map/ppermute | solution.py:246
  24.3 2.7 %collective-permute-start.6 = (f32[128,512]{1,0:T(8,128)S(1)}, f32[128,512]{1,0:T(8,128)S(1)}, u32[]{:S(2)}, u32[]{:S(2)}) collective-permute-start(f32[128,512]{1,0:T(8,128)S(1)} %add.19.left), channel_id=1, source_target_pairs={{0,16},{1,17},{2,18},{3,19},{4,20},{5,21},{6,22},{7,23},{8,24},{9,... | collective-permute-start | bytes 786440 | tf_op jit(solution)/shard_map/ppermute | solution.py:246
  27.0 1.7 %collective-permute-done.10.got = f32[384,256]{1,0:T(8,128)S(1)} collective-permute-done((f32[384,256]{1,0:T(8,128)S(1)}, f32[384,256]{1,0:T(8,128)S(1)}, u32[]{:S(2)}, u32[]{:S(2)}) %collective-permute-start.10) | collective-permute-done | bytes 393248 | tf_op jit(solution)/shard_map/ppermute | solution.py:246
  28.8 3.0 %collective-permute-done.9.v2.refs_0_ = f32[1024,128]{1,0:T(8,128)S(1)} collective-permute-done((f32[1024,128]{1,0:T(8,128)S(1)}, f32[1024,128]{1,0:T(8,128)S(1)}, u32[]{:S(2)}, u32[]{:S(2)}) %collective-permute-start.9) | collective-permute-done | bytes 524320 | tf_op jit(solution)/shard_map/ppermute | solution.py:246
  31.8 1.6 %collective-permute-start.13 = (f32[192,256]{1,0:T(8,128)S(1)}, f32[192,256]{1,0:T(8,128)S(1)}, u32[]{:S(2)}, u32[]{:S(2)}) collective-permute-start(f32[192,256]{1,0:T(8,128)S(1)} %get-tuple-element.56), channel_id=1, source_target_pairs={{0,8},{1,5},{2,10},{3,7},{4,12},{5,1},{6,14},{7,3},{8,0},{9,13},{1... | collective-permute-start | bytes 589832 | tf_op jit(solution)/shard_map/ppermute | solution.py:246
  33.3 6.3 %collective-permute-done.6.right = f32[128,512]{1,0:T(8,128)S(1)} collective-permute-done((f32[128,512]{1,0:T(8,128)S(1)}, f32[128,512]{1,0:T(8,128)S(1)}, u32[]{:S(2)}, u32[]{:S(2)}) %collective-permute-start.6) | collective-permute-done | bytes 262176 | tf_op jit(solution)/shard_map/ppermute | solution.py:246
  39.7 1.6 %collective-permute-done.13 = f32[192,256]{1,0:T(8,128)S(1)} collective-permute-done((f32[192,256]{1,0:T(8,128)S(1)}, f32[192,256]{1,0:T(8,128)S(1)}, u32[]{:S(2)}, u32[]{:S(2)}) %collective-permute-start.13) | collective-permute-done | bytes 196640 | tf_op jit(solution)/shard_map/ppermute | solution.py:246
  41.3 2.0 %collective-permute-start.14 = (f32[192,256]{1,0:T(8,128)S(1)}, f32[192,256]{1,0:T(8,128)S(1)}, u32[]{:S(2)}, u32[]{:S(2)}) collective-permute-start(f32[192,256]{1,0:T(8,128)S(1)} %add.20.left), channel_id=1, source_target_pairs={{0,16},{1,17},{2,18},{3,19},{4,20},{5,21},{6,22},{7,23},{8,24},{9,... | collective-permute-start | bytes 589832 | tf_op jit(solution)/shard_map/ppermute | solution.py:246
  43.3 2.5 %collective-permute-start.7 = (f32[128,512]{1,0:T(8,128)S(1)}, f32[128,512]{1,0:T(8,128)S(1)}, u32[]{:S(2)}, u32[]{:S(2)}) collective-permute-start(f32[128,512]{1,0:T(8,128)S(1)} %shard_map.60.refs_0_), channel_id=1, source_target_pairs={{0,8},{1,5},{2,10},{3,7},{4,12},{5,1},{6,14},{7,3},{8,0},{9,13},{1... | collective-permute-start | bytes 786440 | tf_op jit(solution)/shard_map/ppermute | solution.py:246
  45.8 5.6 %collective-permute-done.14.right = f32[192,256]{1,0:T(8,128)S(1)} collective-permute-done((f32[192,256]{1,0:T(8,128)S(1)}, f32[192,256]{1,0:T(8,128)S(1)}, u32[]{:S(2)}, u32[]{:S(2)}) %collective-permute-start.14) | collective-permute-done | bytes 196640 | tf_op jit(solution)/shard_map/ppermute | solution.py:246
  54.7 1.9 %collective-permute-start.17 = (f32[256,256]{1,0:T(8,128)S(1)}, f32[256,256]{1,0:T(8,128)S(1)}, u32[]{:S(2)}, u32[]{:S(2)}) collective-permute-start(f32[256,256]{1,0:T(8,128)S(1)} %get-tuple-element.64), channel_id=1, source_target_pairs={{0,4},{1,9},{2,6},{3,11},{4,0},{5,13},{6,2},{7,15},{8,12},{9,1},{1... | collective-permute-start | bytes 786440 | tf_op jit(solution)/shard_map/ppermute | solution.py:246
  56.7 1.8 %shard_map.58 = (bf16[1024,512]{1,0:T(8,128)(2,1)S(1)}, bf16[1024,512]{1,0:T(8,128)(2,1)S(1)}) custom-call(bf16[512,512]{1,0:T(8,128)(2,1)S(1)} %get-tuple-element.39.t_high, bf16[512,512]{1,0:T(8,128)(2,1)S(1)} %get-tuple-element.40.t_low, f32[1024,128]{1,0:T(8,128)S(1)} %copy-done.1, f32[1024,128]{1,0:T(8,128)S(1)} %collective-permute-done.refs_1_.v1.near1, ...), custom_call_target="tpu_custom_call" | custom-call | flops 1610612736 | bytes 4096 | tf_op jit(solution)/shard_map/pallas_call | solution.py:204
  58.6 1.8 %collective-permute-start.8 = (f32[256,512]{1,0:T(8,128)S(1)}, f32[256,512]{1,0:T(8,128)S(1)}, u32[]{:S(2)}, u32[]{:S(2)}) collective-permute-start(f32[256,512]{1,0:T(8,128)S(1)} %shard_map.61.low.n_low), channel_id=1, source_target_pairs={{0,4},{1,9},{2,6},{3,11},{4,0},{5,13},{6,2},{7,15},{8,12},{9,1},{1... | collective-permute-start | bytes 1572872 | tf_op jit(solution)/shard_map/ppermute | solution.py:246
  60.3 1.8 %shard_map.66 = (bf16[1024,512]{1,0:T(8,128)(2,1)S(1)}, bf16[1024,512]{1,0:T(8,128)(2,1)S(1)}) custom-call(bf16[512,512]{1,0:T(8,128)(2,1)S(1)} %get-tuple-element.51.t_high, bf16[512,512]{1,0:T(8,128)(2,1)S(1)} %get-tuple-element.52.t_low, f32[1024,128]{1,0:T(8,128)S(1)} %copy-done.2, f32[1024,128]{1,0:T(8,128)S(1)} %collective-permute-done.2.refs_3_.v1, ...), custom_call_target="tpu_custom_call" | custom-call | flops 1610612736 | bytes 4096 | tf_op jit(solution)/shard_map/pallas_call | solution.py:204
  62.4 3.5 %collective-permute-done.16.refs_1_ = f32[256,256]{1,0:T(8,128)S(1)} collective-permute-done((f32[256,256]{1,0:T(8,128)S(1)}, f32[256,256]{1,0:T(8,128)S(1)}, u32[]{:S(2)}, u32[]{:S(2)}) %collective-permute-start.16) | collective-permute-done | bytes 262176 | tf_op jit(solution)/shard_map/ppermute | solution.py:246
  65.9 1.8 %collective-permute-start.18 = (f32[512,256]{1,0:T(8,128)S(1)}, f32[512,256]{1,0:T(8,128)S(1)}, u32[]{:S(2)}, u32[]{:S(2)}) collective-permute-start(f32[512,256]{1,0:T(8,128)S(1)} %shard_map.71.low), channel_id=1, source_target_pairs={{0,4},{1,9},{2,6},{3,11},{4,0},{5,13},{6,2},{7,15},{8,12},{9,1},{1... | collective-permute-start | bytes 1572872 | tf_op jit(solution)/shard_map/ppermute | solution.py:246
  67.7 7.8 %collective-permute-done.19 = f32[128,256]{1,0:T(8,128)S(1)} collective-permute-done((f32[128,256]{1,0:T(8,128)S(1)}, f32[128,256]{1,0:T(8,128)S(1)}, u32[]{:S(2)}, u32[]{:S(2)}) %collective-permute-start.19) | collective-permute-done | bytes 131104 | tf_op jit(solution)/shard_map/ppermute | solution.py:246
  75.7 2.0 %shard_map.62 = (f32[1024,512]{1,0:T(8,128)S(1)}, f32[512,512]{1,0:T(8,128)S(1)}) custom-call(s32[5]{0:T(128)S(1)} %stack.23.place, f32[1024,512]{1,0:T(8,128)S(1)} %copy-done, bf16[512,512]{1,0:T(8,128)(2,1)S(1)} %get-tuple-element.39.t_high, bf16[512,512]{1,0:T(8,128)(2,1)S(1)} %get-tuple-element.40.t_low, ...), custom_call_target="tpu_custom_call" | custom-call | flops 1207959552 | bytes 4096 | tf_op jit(solution)/shard_map/pallas_call | solution.py:204
  77.7 4.2 %collective-permute-done.20.right = f32[128,256]{1,0:T(8,128)S(1)} collective-permute-done((f32[128,256]{1,0:T(8,128)S(1)}, f32[128,256]{1,0:T(8,128)S(1)}, u32[]{:S(2)}, u32[]{:S(2)}) %collective-permute-start.20) | collective-permute-done | bytes 131104 | tf_op jit(solution)/shard_map/ppermute | solution.py:246
  82.7 5.0 %collective-permute-done.22.refs_1_ = f32[128,256]{1,0:T(8,128)S(1)} collective-permute-done((f32[128,256]{1,0:T(8,128)S(1)}, f32[128,256]{1,0:T(8,128)S(1)}, u32[]{:S(2)}, u32[]{:S(2)}) %collective-permute-start.22) | collective-permute-done | bytes 131104 | tf_op jit(solution)/shard_map/ppermute | solution.py:246
  87.9 3.0 %shard_map.74 = (f32[1024,512]{1,0:T(8,128)S(1)}, f32[512,256]{1,0:T(8,128)S(1)}) custom-call(f32[1024,512]{1,0:T(8,128)S(1)} %get-tuple-element.50.x, bf16[512,512]{1,0:T(8,128)(2,1)S(1)} %get-tuple-element.39.t_high, bf16[512,512]{1,0:T(8,128)(2,1)S(1)} %get-tuple-element.40.t_low, bf16[1024,512]{1,0:T(8,128)(2,1)S(1)} %get-tuple-element.46.w_high.w2_high, ...), custom_call_target="tpu_custom_call" | custom-call | flops 2415919104 | bytes 4096 | tf_op jit(solution)/shard_map/pallas_call | solution.py:204
  90.9 3.2 %collective-permute-done.23.high = f32[256,256]{1,0:T(8,128)S(1)} collective-permute-done((f32[256,256]{1,0:T(8,128)S(1)}, f32[256,256]{1,0:T(8,128)S(1)}, u32[]{:S(2)}, u32[]{:S(2)}) %collective-permute-start.23) | collective-permute-done | bytes 262176 | tf_op jit(solution)/shard_map/ppermute | solution.py:246
  94.1 2.6 %shard_map.76 = f32[1024,512]{1,0:T(8,128)} custom-call(s32[5]{0:T(128)S(1)} %stack.23.place, f32[1024,512]{1,0:T(8,128)S(1)} %get-tuple-element.71.x, bf16[1024,512]{1,0:T(8,128)(2,1)S(1)} %get-tuple-element.58.w1_high.w_high, bf16[1024,512]{1,0:T(8,128)(2,1)S(1)} %get-tuple-element.59.w1_low.w_low, f32[512,256]{1,0:T(8,128)S(1)} %get-tuple-element.72.rest, ...), custom_call_target="tpu_custom_call" | custom-call | flops 805306368 | bytes 4096 | tf_op jit(solution)/shard_map/pallas_call | solution.py:204
  (53 shorter events, 6.0 us)
Async XLA Ops:
  0.0 6.2 %copy-start.2 = (f32[1024,128]{1,0:T(8,128)S(1)}, f32[1024,128]{1,0:T(8,128)}, u32[]{:S(2)}) copy-start(f32[1024,128]{1,0:T(8,128)} %v0.3) | copy-start | bytes 1572868
  0.0 6.2 %copy-start.1 = (f32[1024,128]{1,0:T(8,128)S(1)}, f32[1024,128]{1,0:T(8,128)}, u32[]{:S(2)}) copy-start(f32[1024,128]{1,0:T(8,128)} %near0.1) | copy-start | bytes 1572868
  0.0 6.2 %collective-permute-start.2 = (f32[1024,128]{1,0:T(8,128)}, f32[1024,128]{1,0:T(8,128)S(1)}, u32[]{:S(2)}, u32[]{:S(2)}) collective-permute-start(f32[1024,128]{1,0:T(8,128)} %v0.3), channel_id=1, source_target_pairs={{0,1},{1,0},{2,3},{3,2},{4,5},{5,4},{6,7},{7,6},{8,9},{9,8},{10,11... | collective-permute-start | bytes 1572872 | tf_op jit(solution)/shard_map/ppermute | solution.py:246
  0.5 5.7 %collective-permute-start = (f32[1024,128]{1,0:T(8,128)}, f32[1024,128]{1,0:T(8,128)S(1)}, u32[]{:S(2)}, u32[]{:S(2)}) collective-permute-start(f32[1024,128]{1,0:T(8,128)} %near0.1), channel_id=1, source_target_pairs={{0,1},{1,0},{2,3},{3,2},{4,5},{5,4},{6,7},{7,6},{8,9},{9,8},{10,11... | collective-permute-start | bytes 1572872 | tf_op jit(solution)/shard_map/ppermute | solution.py:246
  0.5 15.3 %collective-permute-start.1 = (f32[1024,128]{1,0:T(8,128)}, f32[1024,128]{1,0:T(8,128)S(1)}, u32[]{:S(2)}, u32[]{:S(2)}) collective-permute-start(f32[1024,128]{1,0:T(8,128)} %near0.1), channel_id=1, source_target_pairs={{0,2},{1,3},{2,0},{3,1},{4,6},{5,7},{6,4},{7,5},{8,10},{9,11},{10,... | collective-permute-start | bytes 1572872 | tf_op jit(solution)/shard_map/ppermute | solution.py:246
  8.0 9.2 %collective-permute-start.4 = (f32[256,512]{1,0:T(8,128)S(1)}, f32[256,512]{1,0:T(8,128)S(1)}, u32[]{:S(2)}, u32[]{:S(2)}) collective-permute-start(f32[256,512]{1,0:T(8,128)S(1)} %get-tuple-element.44), channel_id=1, source_target_pairs={{0,4},{1,9},{2,6},{3,11},{4,0},{5,13},{6,2},{7,15},{8,12},{9,1},{1... | collective-permute-start | bytes 1572872 | tf_op jit(solution)/shard_map/ppermute | solution.py:246
  15.9 3.6 %collective-permute-start.3 = (f32[1024,128]{1,0:T(8,128)S(1)}, f32[1024,128]{1,0:T(8,128)S(1)}, u32[]{:S(2)}, u32[]{:S(2)}) collective-permute-start(f32[1024,128]{1,0:T(8,128)S(1)} %collective-permute-done.1.v2.far0), channel_id=1, source_target_pairs={{0,1},{1,0},{2,3},{3,2},{4,5},{5,4},{6,7},{7,6},{8,9},{9,8},{10,11... | collective-permute-start | bytes 1572872 | tf_op jit(solution)/shard_map/ppermute | solution.py:246
  17.3 6.9 %collective-permute-start.5 = (f32[128,512]{1,0:T(8,128)S(1)}, f32[128,512]{1,0:T(8,128)S(1)}, u32[]{:S(2)}, u32[]{:S(2)}) collective-permute-start(f32[128,512]{1,0:T(8,128)S(1)} %get-tuple-element.49), channel_id=1, source_target_pairs={{0,8},{1,5},{2,10},{3,7},{4,12},{5,1},{6,14},{7,3},{8,0},{9,13},{1... | collective-permute-start | bytes 786440 | tf_op jit(solution)/shard_map/ppermute | solution.py:246
  19.0 12.8 %collective-permute-start.9 = (f32[1024,128]{1,0:T(8,128)S(1)}, f32[1024,128]{1,0:T(8,128)S(1)}, u32[]{:S(2)}, u32[]{:S(2)}) collective-permute-start(f32[1024,128]{1,0:T(8,128)S(1)} %copy-done.2), channel_id=1, source_target_pairs={{0,2},{1,3},{2,0},{3,1},{4,6},{5,7},{6,4},{7,5},{8,10},{9,11},{10,... | collective-permute-start | bytes 1572872 | tf_op jit(solution)/shard_map/ppermute | solution.py:246
  20.9 31.3 %copy-start.3 = (f32[512,512]{1,0:T(8,128)S(1)}, f32[512,512]{1,0:T(8,128)}, u32[]{:S(2)}) copy-start(f32[512,512]{1,0:T(8,128)} %t.3) | copy-start | bytes 3145732
  20.9 7.8 %collective-permute-start.10 = (f32[384,256]{1,0:T(8,128)S(1)}, f32[384,256]{1,0:T(8,128)S(1)}, u32[]{:S(2)}, u32[]{:S(2)}) collective-permute-start(f32[384,256]{1,0:T(8,128)S(1)} %get-tuple-element.55), channel_id=1, source_target_pairs={{0,4},{1,9},{2,6},{3,11},{4,0},{5,13},{6,2},{7,15},{8,12},{9,1},{1... | collective-permute-start | bytes 1179656 | tf_op jit(solution)/shard_map/ppermute | solution.py:246
  24.3 4.5 %collective-permute-start.11 = (f32[128,512]{1,0:T(8,128)S(1)}, f32[128,512]{1,0:T(8,128)S(1)}, u32[]{:S(2)}, u32[]{:S(2)}) collective-permute-start(f32[128,512]{1,0:T(8,128)S(1)} %add.19.left), channel_id=1, source_target_pairs={{0,1},{1,0},{2,3},{3,2},{4,5},{5,4},{6,7},{7,6},{8,9},{9,8},{10,11... | collective-permute-start | bytes 786440 | tf_op jit(solution)/shard_map/ppermute | solution.py:246
  24.3 15.3 %collective-permute-start.6 = (f32[128,512]{1,0:T(8,128)S(1)}, f32[128,512]{1,0:T(8,128)S(1)}, u32[]{:S(2)}, u32[]{:S(2)}) collective-permute-start(f32[128,512]{1,0:T(8,128)S(1)} %add.19.left), channel_id=1, source_target_pairs={{0,16},{1,17},{2,18},{3,19},{4,20},{5,21},{6,22},{7,23},{8,24},{9,... | collective-permute-start | bytes 786440 | tf_op jit(solution)/shard_map/ppermute | solution.py:246
  28.7 24.2 %copy-start.4 = (f32[512,512]{1,0:T(8,128)S(1)}, f32[512,512]{1,0:T(8,128)}, u32[]{:S(2)}) copy-start(f32[512,512]{1,0:T(8,128)} %t.2) | copy-start | bytes 3145732
  31.8 21.9 %collective-permute-start.12 = (f32[1024,128]{1,0:T(8,128)S(1)}, f32[1024,128]{1,0:T(8,128)S(1)}, u32[]{:S(2)}, u32[]{:S(2)}) collective-permute-start(f32[1024,128]{1,0:T(8,128)S(1)} %collective-permute-done.9.v2.refs_0_), channel_id=1, source_target_pairs={{0,1},{1,0},{2,3},{3,2},{4,5},{5,4},{6,7},{7,6},{8,9},{9,8},{10,11... | collective-permute-start | bytes 1572872 | tf_op jit(solution)/shard_map/ppermute | solution.py:246
  31.8 9.5 %collective-permute-start.13 = (f32[192,256]{1,0:T(8,128)S(1)}, f32[192,256]{1,0:T(8,128)S(1)}, u32[]{:S(2)}, u32[]{:S(2)}) collective-permute-start(f32[192,256]{1,0:T(8,128)S(1)} %get-tuple-element.56), channel_id=1, source_target_pairs={{0,8},{1,5},{2,10},{3,7},{4,12},{5,1},{6,14},{7,3},{8,0},{9,13},{1... | collective-permute-start | bytes 589832 | tf_op jit(solution)/shard_map/ppermute | solution.py:246
  41.3 10.1 %collective-permute-start.14 = (f32[192,256]{1,0:T(8,128)S(1)}, f32[192,256]{1,0:T(8,128)S(1)}, u32[]{:S(2)}, u32[]{:S(2)}) collective-permute-start(f32[192,256]{1,0:T(8,128)S(1)} %add.20.left), channel_id=1, source_target_pairs={{0,16},{1,17},{2,18},{3,19},{4,20},{5,21},{6,22},{7,23},{8,24},{9,... | collective-permute-start | bytes 589832 | tf_op jit(solution)/shard_map/ppermute | solution.py:246
  43.3 15.2 %collective-permute-start.7 = (f32[128,512]{1,0:T(8,128)S(1)}, f32[128,512]{1,0:T(8,128)S(1)}, u32[]{:S(2)}, u32[]{:S(2)}) collective-permute-start(f32[128,512]{1,0:T(8,128)S(1)} %shard_map.60.refs_0_), channel_id=1, source_target_pairs={{0,8},{1,5},{2,10},{3,7},{4,12},{5,1},{6,14},{7,3},{8,0},{9,13},{1... | collective-permute-start | bytes 786440 | tf_op jit(solution)/shard_map/ppermute | solution.py:246
  51.5 5.1 %collective-permute-start.15 = (f32[64,256]{1,0:T(8,128)S(1)}, f32[64,256]{1,0:T(8,128)S(1)}, u32[]{:S(2)}, u32[]{:S(2)}) collective-permute-start(f32[64,256]{1,0:T(8,128)S(1)} %slice.4), channel_id=1, source_target_pairs={{0,2},{1,3},{2,0},{3,1},{4,6},{5,7},{6,4},{7,5},{8,10},{9,11},{10,... | collective-permute-start | bytes 196616 | tf_op jit(solution)/shard_map/ppermute | solution.py:246
  54.7 7.7 %collective-permute-start.17 = (f32[256,256]{1,0:T(8,128)S(1)}, f32[256,256]{1,0:T(8,128)S(1)}, u32[]{:S(2)}, u32[]{:S(2)}) collective-permute-start(f32[256,256]{1,0:T(8,128)S(1)} %get-tuple-element.64), channel_id=1, source_target_pairs={{0,4},{1,9},{2,6},{3,11},{4,0},{5,13},{6,2},{7,15},{8,12},{9,1},{1... | collective-permute-start | bytes 786440 | tf_op jit(solution)/shard_map/ppermute | solution.py:246
  56.6 9.2 %collective-permute-start.16 = (f32[256,256]{1,0:T(8,128)S(1)}, f32[256,256]{1,0:T(8,128)S(1)}, u32[]{:S(2)}, u32[]{:S(2)}) collective-permute-start(f32[256,256]{1,0:T(8,128)S(1)} %shard_map.69.refs_0_), channel_id=1, source_target_pairs={{0,8},{1,5},{2,10},{3,7},{4,12},{5,1},{6,14},{7,3},{8,0},{9,13},{1... | collective-permute-start | bytes 786440 | tf_op jit(solution)/shard_map/ppermute | solution.py:246
  58.6 17.1 %collective-permute-start.8 = (f32[256,512]{1,0:T(8,128)S(1)}, f32[256,512]{1,0:T(8,128)S(1)}, u32[]{:S(2)}, u32[]{:S(2)}) collective-permute-start(f32[256,512]{1,0:T(8,128)S(1)} %shard_map.61.low.n_low), channel_id=1, source_target_pairs={{0,4},{1,9},{2,6},{3,11},{4,0},{5,13},{6,2},{7,15},{8,12},{9,1},{1... | collective-permute-start | bytes 1572872 | tf_op jit(solution)/shard_map/ppermute | solution.py:246
  60.3 15.3 %copy-start = (f32[1024,512]{1,0:T(8,128)S(1)}, f32[1024,512]{1,0:T(8,128)}, u32[]{:S(2)}) copy-start(f32[1024,512]{1,0:T(8,128)} %x.3) | copy-start | bytes 6291460
  65.9 16.0 %collective-permute-start.18 = (f32[512,256]{1,0:T(8,128)S(1)}, f32[512,256]{1,0:T(8,128)S(1)}, u32[]{:S(2)}, u32[]{:S(2)}) collective-permute-start(f32[512,256]{1,0:T(8,128)S(1)} %shard_map.71.low), channel_id=1, source_target_pairs={{0,4},{1,9},{2,6},{3,11},{4,0},{5,13},{6,2},{7,15},{8,12},{9,1},{1... | collective-permute-start | bytes 1572872 | tf_op jit(solution)/shard_map/ppermute | solution.py:246
  67.7 7.8 %collective-permute-start.19 = (f32[128,256]{1,0:T(8,128)S(1)}, f32[128,256]{1,0:T(8,128)S(1)}, u32[]{:S(2)}, u32[]{:S(2)}) collective-permute-start(f32[128,256]{1,0:T(8,128)S(1)} %get-tuple-element.66), channel_id=1, source_target_pairs={{0,8},{1,5},{2,10},{3,7},{4,12},{5,1},{6,14},{7,3},{8,0},{9,13},{1... | collective-permute-start | bytes 393224 | tf_op jit(solution)/shard_map/ppermute | solution.py:246
  75.6 6.3 %collective-permute-start.20 = (f32[128,256]{1,0:T(8,128)S(1)}, f32[128,256]{1,0:T(8,128)S(1)}, u32[]{:S(2)}, u32[]{:S(2)}) collective-permute-start(f32[128,256]{1,0:T(8,128)S(1)} %add.21.left), channel_id=1, source_target_pairs={{0,16},{1,17},{2,18},{3,19},{4,20},{5,21},{6,22},{7,23},{8,24},{9,... | collective-permute-start | bytes 393224 | tf_op jit(solution)/shard_map/ppermute | solution.py:246
  82.5 5.3 %collective-permute-start.21 = (f32[256,512]{1,0:T(8,128)S(1)}, f32[256,512]{1,0:T(8,128)S(1)}, u32[]{:S(2)}, u32[]{:S(2)}) collective-permute-start(f32[256,512]{1,0:T(8,128)S(1)} %shard_map.73.g), channel_id=1, source_target_pairs={{0,1},{1,0},{2,3},{3,2},{4,5},{5,4},{6,7},{7,6},{8,9},{9,8},{10,11... | collective-permute-start | bytes 1572872 | tf_op jit(solution)/shard_map/ppermute | solution.py:246
  82.6 5.0 %collective-permute-start.22 = (f32[128,256]{1,0:T(8,128)S(1)}, f32[128,256]{1,0:T(8,128)S(1)}, u32[]{:S(2)}, u32[]{:S(2)}) collective-permute-start(f32[128,256]{1,0:T(8,128)S(1)} %shard_map.72.refs_0_), channel_id=1, source_target_pairs={{0,8},{1,5},{2,10},{3,7},{4,12},{5,1},{6,14},{7,3},{8,0},{9,13},{1... | collective-permute-start | bytes 393224 | tf_op jit(solution)/shard_map/ppermute | solution.py:246
  87.7 6.4 %collective-permute-start.23 = (f32[256,256]{1,0:T(8,128)S(1)}, f32[256,256]{1,0:T(8,128)S(1)}, u32[]{:S(2)}, u32[]{:S(2)}) collective-permute-start(f32[256,256]{1,0:T(8,128)S(1)} %shard_map.75.low), channel_id=1, source_target_pairs={{0,4},{1,9},{2,6},{3,11},{4,0},{5,13},{6,2},{7,15},{8,12},{9,1},{1... | collective-permute-start | bytes 786440 | tf_op jit(solution)/shard_map/ppermute | solution.py:246

commit v2 on v1

--- a/solution.py
+++ b/solution.py
@@ -29,8 +29,8 @@
     return jnp.concatenate([ref[...] for ref in refs], axis=1)
 
 
-def stacked(refs, cols=slice(None)):
-    return jnp.concatenate([ref[:, cols] for ref in refs], axis=0)
+def stacked(refs, part=...):
+    return jnp.concatenate([ref[part] for ref in refs], axis=0)
 
 
 def block(index, size):
@@ -68,39 +68,47 @@
             t_low[at] = rest
 
 
-def project_kernel(pairs, lt_high, lt_low, *refs):
-    vectors, outs = refs[: 2 * pairs], refs[-2:]
+def put(total, at, *outs):
     rows = outs[0].shape[0]
-    left = (lt_high[: 2 * rows, :], lt_low[: 2 * rows, :])
-    for k in range(pairs):
-        total = dot3(left, split(joined(vectors[2 * k : 2 * k + 2])), NN)
-        size = total.shape[1]
-        for i in range(2):
-            outs[i][:, k * size : (k + 1) * size] = total[i * rows : (i + 1) * rows, :]
-
-
-def project_cross_kernel(lt_high, lt_low, near0, near1, far0, far1, *outs):
+    for p in range(GROUP):
+        outs[p][:, at : at + total.shape[1]] = total[p * rows : (p + 1) * rows, :]
+
+
+def project_kernel(lt_high, lt_low, *refs):
+    vectors, outs = refs[:-GROUP], refs[-GROUP:]
+    rows = GROUP * outs[0].shape[0]
+    left = (lt_high[:rows, :], lt_low[:rows, :])
+    for k in range(0, len(vectors), 2):
+        total = dot3(left, split(joined(vectors[k : k + 2])), NN)
+        put(total, k // 2 * total.shape[1], *outs)
+
+
+def project_last_kernel(lt_high, lt_low, v0, *refs):
+    pieces, outs = refs[:-GROUP], refs[-GROUP:]
+    rows = GROUP * outs[0].shape[0]
+    right = jnp.concatenate([v0[...], stacked(pieces)], axis=1)
+    put(dot3((lt_high[:rows, :], lt_low[:rows, :]), split(right), NN), 0, *outs)
+
+
+def project_cross_kernel(lt_high, lt_low, near0, near1, far0, *refs):
     thin = near0.shape[1] // GROUP
     cols = lt_high.shape[0] - GROUP * thin
     wide = cols // GROUP
-    total = dot3((lt_high[...], lt_low[...]), split(joined((far0, far1))), NN)
+    pieces, outs = refs[:-GROUP], refs[-GROUP:]
+    far = jnp.concatenate([far0[...], stacked(pieces)], axis=1)
+    total = dot3((lt_high[...], lt_low[...]), split(far), NN)
     cross = dot3((lt_high[cols:, :], lt_low[cols:, :]), split(joined((near0, near1))), NN)
     for p in range(GROUP):
-        out, at = outs[p // 2], (p % 2) * (wide + 2 * thin)
-        out[at : at + wide, :] = total[p * wide : (p + 1) * wide, :]
-        out[at + wide : at + wide + thin, :] = cross[p * thin : (p + 1) * thin, :]
-        out[at + wide + thin : at + wide + 2 * thin, :] = total[cols + p * thin : cols + (p + 1) * thin, :]
-
-
-def fold_kernel(keep, got, *refs):
-    mine, other = refs[-2:]
-    rows = mine.shape[0]
-    mine[...] = keep[:rows, :] + got[:rows, :]
-    other[...] = keep[rows:, :] + got[rows:, :]
-
-
-def add_kernel(left, right, *refs):
-    refs[-1][...] = left[...] + right[...]
+        outs[p][:wide, :] = total[p * wide : (p + 1) * wide, :]
+        outs[p][wide : wide + thin, :] = cross[p * thin : (p + 1) * thin, :]
+        outs[p][wide + thin :, :] = total[cols + p * thin : cols + (p + 1) * thin, :]
+
+
+def add_kernel(count, *refs):
+    total = refs[0][...]
+    for ref in refs[1:count]:
+        total = total + ref[...]
+    refs[-1][...] = total
 
 
 def pile_kernel(count, *refs):
@@ -111,32 +119,39 @@
         at += part.shape[0]
 
 
-def cross_kernel(wide, place, low, high, out):
+def cross_kernel(wide, place, *refs):
+    blocks, out = refs[:GROUP], refs[GROUP]
     width = out.shape[0] // 2
     half = out.shape[1] // 2
     thin = width // GROUP
-    size = low.shape[0] // 2
     for i in range(2):
         for j in range(2):
+            at = wide + (2 * i + j) * thin
             for p in range(GROUP):
-                at = (p % 2) * size + wide + (2 * i + j) * thin
                 to = pl.ds(pl.multiple_of(i * width + place[p] * thin, thin), thin)
-                out[to, j * half : (j + 1) * half] = (low, high)[p // 2][at : at + thin, :]
-
-
-def factor_kernel(t_high, t_low, v0, v1, v2, v3, w_high, w_low):
-    tile = v0.shape[0] // 2
+                out[to, j * half : (j + 1) * half] = blocks[p][at : at + thin, :]
+
+
+def factor_kernel(t_high, t_low, v0, v1, v2, *refs):
+    pieces, (w_high, w_low) = refs[:-2], refs[-2:]
+    count = 2
+    tile = v0.shape[0] // count
     right = (t_high[...], t_low[...])
-    for i in range(2):
+    for i in range(count):
         at = slice(i * tile, (i + 1) * tile)
-        left = split(jnp.concatenate([v[at, :] for v in (v0, v1, v2, v3)], axis=1))
+        if len(pieces) == 1:
+            last = pieces[0][at, :]
+        else:
+            each = len(pieces) // count
+            last = jnp.concatenate([piece[...] for piece in pieces[i * each : (i + 1) * each]], axis=0)
+        left = split(jnp.concatenate([v0[at, :], v1[at, :], v2[at, :], last], axis=1))
         w_high[at, :], w_low[at, :] = split(dot3(left, right, NN))
 
 
-def near_kernel(place, x, t_high, t_low, w_high, w_low, low, high, out, c):
-    half = low.shape[1] // 2
-    wide = low.shape[0] // 2
-    p2 = split(stacked((low, high), slice(0, half)))
+def near_kernel(place, x, t_high, t_low, w_high, w_low, *refs):
+    blocks, (out, c) = refs[:GROUP], refs[GROUP:]
+    wide, half = blocks[0].shape[0], blocks[0].shape[1] // 2
+    p2 = split(stacked(blocks, (slice(None), slice(0, half))))
     c[...] = dot3(p2, (t_high[:, :half], t_low[:, :half]), NT)
     tile = x.shape[0] // 2
     for i in range(2):
@@ -147,14 +162,11 @@
             out[at, cols] = x[at, block(place[p], wide)] - change[:, cols]
 
 
-def middle_kernel(x, t_high, t_low, w2_high, w2_low, w1_high, w1_low, c, g, g_core, n_low, n_high, low, high, out, rest):
-    half = rest.shape[1]
-    wide = n_low.shape[0] // 2
+def middle_kernel(x, t_high, t_low, w2_high, w2_low, w1_high, w1_low, c, g, g_core, *refs):
+    near, far, (out, rest) = refs[:GROUP], refs[GROUP : 2 * GROUP], refs[2 * GROUP :]
+    wide, half = near[0].shape[0], rest.shape[1]
     width = g.shape[0] // 2
-    size = low.shape[0] // 2
-    p2 = split(
-        jnp.concatenate([(low, high)[p // 2][(p % 2) * size : (p % 2) * size + wide, :] for p in range(GROUP)], axis=0)
-    )
+    p2 = split(stacked(far, (slice(0, wide), slice(None))))
     c2 = split(c[...] + dot3(p2, (t_high[:, half:], t_low[:, half:]), NT))
     parts = []
     for i in range(4):
@@ -162,7 +174,7 @@
         parts.append(jnp.concatenate([rows[:, (j ^ i) * width : ((j ^ i) + 1) * width] for j in range(4)], axis=1))
     cross = dot3(c2, split(jnp.concatenate(parts, axis=0)), NT)
     rest[...] = cross[:, half:]
-    p1 = split(stacked((n_low, n_high), slice(half, 2 * half)) - cross[:, :half])
+    p1 = split(stacked(near, (slice(None), slice(half, 2 * half))) - cross[:, :half])
     tile = x.shape[0] // 2
     for i in range(2):
         at = slice(i * tile, (i + 1) * tile)
@@ -170,9 +182,9 @@
         out[at, :] = x[at, :] - (change + dot3((w1_high[at, :half], w1_low[at, :half]), p1, NT))
 
 
-def last_kernel(place, x, w_high, w_low, rest, low, high, out, tiles, sems):
-    wide, half = low.shape[0] // 2, low.shape[1]
-    right = split(stacked((low, high)) - rest[...])
+def last_kernel(place, x, w_high, w_low, rest, b0, b1, b2, b3, out, tiles, sems):
+    wide, half = b0.shape
+    right = split(stacked((b0, b1, b2, b3)) - rest[...])
     count = tiles.shape[0]
     tile = tiles.shape[1]
     copies = []
@@ -254,31 +266,33 @@
     def to_two(value):
         return permute(value, lambda r, c: (r ^ (2 - c % 2), c))
 
-    def add(left, right, *pads):
-        return call(add_kernel, [(left.shape, f32)], (left, right, *map(InAny, pads)))[0]
+    def add(*parts, pads=()):
+        return call(functools.partial(add_kernel, len(parts)), [(parts[0].shape, f32)], (*parts, *map(InAny, pads)))[0]
 
     def across(value, *earlier, pads=()):
         bit = GROUP
         while bit < row_size:
             got = after(permute(value, lambda r, c, bit=bit: (r ^ bit, c)), *earlier)
-            value = add(value, got, *pads)
+            value = add(value, got, pads=pads)
             bit *= 2
         return value
 
-    def pad(value):
-        return to_col(value[:wide], 1)
-
-    def fold(keep, sent, *pads):
-        shape = (keep.shape[0] // 2, keep.shape[1])
-        return call(fold_kernel, [(shape, f32)] * 2, (keep, to_one(sent), *map(InAny, pads)))
+    def pad(value, rows=wide):
+        return to_col(value[:rows], 1)
+
+    def relayed(far):
+        return far, *(to_col(piece, 1) for piece in jnp.split(far, 4))
+
+    def projections(height, size):
+        return [((height, size), f32)] * GROUP
 
     def pile(*parts, pads=()):
         shape = (sum(p.shape[0] for p in parts), parts[0].shape[1])
         return call(functools.partial(pile_kernel, len(parts)), [(shape, f32)], (*parts, *map(InAny, pads)))[0]
 
     def spread(mine, *earlier):
-        pair = pile(mine, after(to_two(mine), *earlier))
-        return pair, to_one(pair)
+        got = to_two(mine)
+        return mine, got, to_one(mine), to_one(after(got, *earlier))
 
     second_far = to_col(panel_second, 2)
     first_far = to_col(panel_first, 2)
@@ -299,43 +313,37 @@
         ],
     )
     near_parts = call(
-        functools.partial(project_kernel, 2),
-        [((2 * wide, total), f32)] * 2,
-        (lt_high, lt_low, *second_near, *first_near),
-    )
-    second_far = after(second_far, near_parts)
-    second_far = (second_far, to_col(second_far, 1))
+        project_kernel, projections(wide, total), (lt_high, lt_low, *second_near, *first_near)
+    )
+    near_got = to_one(near_parts[2])
+    near_other = add(near_parts[1], to_one(near_parts[3]), pads=(near_got,))
+
+    second_far = relayed(after(second_far, near_other))
     second = second_near + second_far
-    near_mine, near_other = fold(*near_parts)
-    near_sum = near_mine + to_two(near_other)
     second_parts = call(
         project_cross_kernel,
-        [((2 * (wide + 2 * thin), half), f32)] * 2,
-        (lt_high, lt_low, *second_near, after(second_far[0], near_other), second_far[1]),
-    )
-    second_mine, second_other = fold(second_parts[0], second_parts[1], pad(near_sum))
-    second_sum = second_mine + to_two(second_other)
-
-    near_sum = across(near_sum)
-    first_far = after(first_far, second_other)
-    first_far = (first_far, to_col(first_far, 1))
+        projections(wide + 2 * thin, half),
+        (lt_high, lt_low, *second),
+    )
+    near_sum = add(near_parts[0], near_got, after(to_two(near_other), second_parts, first_far))
+    second_got = to_one(second_parts[2])
+    second_other = add(second_parts[1], to_one(second_parts[3]), pads=(second_got,))
+    second_sum = add(second_parts[0], second_got, to_two(second_other))
+    first_far = relayed(after(first_far, near_sum))
     first = first_near + first_far
-    first_parts = call(
-        functools.partial(project_kernel, 1),
-        [((2 * wide, half), f32)] * 2,
-        (lt_high, lt_low, *first_far),
-    )
-    second_sum = across(after(second_sum, near_sum))
-    near = spread(near_sum)
-    first_mine, first_other = fold(*first_parts)
-    first_sum = first_mine + to_two(first_other)
-
+    first_parts = call(project_last_kernel, projections(wide, half), (lt_high, lt_low, *first_far))
     arrange = functools.partial(call, functools.partial(arrange_kernel, width), [((total, total), bf16)] * 2, scalars=1)
     factor = functools.partial(call, factor_kernel, [((rows, total), bf16)] * 2)
     t1 = arrange((place, factor_first), rows * total // 2)
     t2 = arrange((place, factor_second), rows * total // 2)
     w2 = factor((*t2, *second), rows * total * total)
     w1 = factor((*t1, *first), rows * total * total)
+    near_sum = across(near_sum, first_parts, w2)
+    first_other = add(first_parts[1], to_one(first_parts[3]))
+    first_sum = add(first_parts[0], to_one(first_parts[2]), to_two(first_other))
+    second_sum = across(second_sum, first_other, pads=(pad(pad(near_sum), wide // 2),))
+    near = spread(near_sum, first_other)
+
     left, coefficients = call(
         near_kernel,
         [((rows, cols), f32), ((cols, total), f32)],
@@ -344,14 +352,17 @@
         scalars=1,
     )
 
-    second_sum = pile(second_sum, after(to_col(second_sum[wide:], 2), first_parts))
-    second_blocks = spread(second_sum, w1, w2, first_other)
+    second_sum = pile(second_sum, after(to_col(second_sum[wide:], 2), first_sum, w1))
     first_sum = across(first_sum)
+    second_blocks = spread(second_sum, near)
+    first_blocks = spread(first_sum)
     (cross,) = call(
-        functools.partial(cross_kernel, wide), [((2 * width, total), f32)], (place, *after(second_blocks, left, first_sum)), scalars=1
+        functools.partial(cross_kernel, wide),
+        [((2 * width, total), f32)],
+        (place, *after(second_blocks, left, first_blocks[1])),
+        scalars=1,
     )
     cross_core = to_col(cross, 1)
-    first_blocks = spread(first_sum)
 
     left, rest = call(
         middle_kernel,

time: 96.9 us -> 87.8 us (0.906)
  waiting for transfers between devices: 51.6 us -> 31.8 us
  starting transfers between devices: 24.3 us -> 34.9 us
    ppermute x24 -> x37, waiting for transfers between devices: 51.6 us -> 31.8 us  [permute(): return lax.ppermute(value, ('row', 'col'), pairs)]
    ppermute x24 -> x37, starting transfers between devices: 24.3 us -> 34.9 us  [permute(): return lax.ppermute(value, ('row', 'col'), pairs)]
  transfers between devices with their start and end apart: 24 -> 37, of which waited for: 14 -> 15; matrix products, arithmetic and copies ran while one was open for 0% -> 0% of each run, Pallas kernels for 18% -> 20%
where the time goes in v2:
time: 87.8 us; the launch traced here: 87.6 us
  starting transfers between devices  34.9 us (40%)
  waiting for transfers between devices  31.8 us (36%)
  Pallas kernels  20.4 us (23%)
    ppermute x37, starting transfers between devices, permute(): return lax.ppermute(value, ('row', 'col'), pairs)  34.9 us
    ppermute x37, waiting for transfers between devices, permute(): return lax.ppermute(value, ('row', 'col'), pairs)  31.8 us
    pallas_call x22, Pallas kernels, call(): pl.pallas_call(kernel, out_shape=tuple((jax.ShapeDtypeStruct(shape, dtype...  20.4 us
  transfers between devices with their start and end apart: 37, of which 15 were waited for; matrix products, arithmetic and copies ran while one was open for 0% of the time, Pallas kernels for 20%

profile of v2, /device:TPU:0, one launch (start us, length us, event | category | flops | bytes accessed | tf_op | source)
XLA Modules:
  0.0 87.6 jit_solution(8298509281250289076)
XLA Ops:
  0.5 3.0 %collective-permute-start.1 = (f32[1024,128]{1,0:T(8,128)}, f32[1024,128]{1,0:T(8,128)S(1)}, u32[]{:S(2)}, u32[]{:S(2)}) collective-permute-start(f32[1024,128]{1,0:T(8,128)} %near0.1), channel_id=1, source_target_pairs={{0,2},{1,3},{2,0},{3,1},{4,6},{5,7},{6,4},{7,5},{8,10},{9,11},{10,... | collective-permute-start | bytes 1572872 | tf_op jit(solution)/shard_map/ppermute | solution.py:258
  3.6 2.6 %shard_map.56 = (bf16[640,1024]{1,0:T(8,128)(2,1)S(1)}, bf16[640,1024]{1,0:T(8,128)(2,1)S(1)}) custom-call(s32[5]{0:T(128)S(1)} %stack.23.place, f32[1024,512]{1,0:T(8,128)} %x.3, f32[1024,128]{1,0:T(8,128)} %v0.3), custom_call_target="tpu_custom_call" | custom-call | bytes 4096 | tf_op jit(solution)/shard_map/pallas_call | solution.py:216
  6.2 1.8 %shard_map.57 = (f32[128,512]{1,0:T(8,128)S(1)}, f32[128,512]{1,0:T(8,128)S(1)}, f32[128,512]{1,0:T(8,128)S(1)}, f32[128,512]{1,0:T(8,128)S(1)}) custom-call(bf16[640,1024]{1,0:T(8,128)(2,1)S(1)} %get-tuple-element.45.lt_high, bf16[640,1024]{1,0:T(8,128)(2,1)S(1)} %get-tuple-element.46.lt_low, f32[1024,128]{1,0:T(8,128)S(1)} %copy-done.1, ...), custom_call_target="tpu_custom_call" | custom-call | bytes 4096 | tf_op jit(solution)/shard_map/pallas_call | solution.py:216
  8.0 1.6 %collective-permute-start.3 = (f32[128,512]{1,0:T(8,128)S(1)}, f32[128,512]{1,0:T(8,128)S(1)}, u32[]{:S(2)}, u32[]{:S(2)}) collective-permute-start(f32[128,512]{1,0:T(8,128)S(1)} %get-tuple-element.48), channel_id=1, source_target_pairs={{0,4},{1,9},{2,6},{3,11},{4,0},{5,13},{6,2},{7,15},{8,12},{9,1},{1... | collective-permute-start | bytes 786440 | tf_op jit(solution)/shard_map/ppermute | solution.py:258
  10.2 4.3 %collective-permute-done.3.refs_1_ = f32[128,512]{1,0:T(8,128)S(1)} collective-permute-done((f32[128,512]{1,0:T(8,128)S(1)}, f32[128,512]{1,0:T(8,128)S(1)}, u32[]{:S(2)}, u32[]{:S(2)}) %collective-permute-start.3) | collective-permute-done | bytes 262176 | tf_op jit(solution)/shard_map/ppermute | solution.py:258
  14.5 2.8 %collective-permute-done.4.refs_2_.refs_1_ = f32[128,512]{1,0:T(8,128)S(1)} collective-permute-done((f32[128,512]{1,0:T(8,128)S(1)}, f32[128,512]{1,0:T(8,128)S(1)}, u32[]{:S(2)}, u32[]{:S(2)}) %collective-permute-start.4) | collective-permute-done | bytes 262176 | tf_op jit(solution)/shard_map/ppermute | solution.py:258
  17.4 1.6 %collective-permute-start.9 = (f32[128,512]{1,0:T(8,128)S(1)}, f32[128,512]{1,0:T(8,128)S(1)}, u32[]{:S(2)}, u32[]{:S(2)}) collective-permute-start(f32[128,512]{1,0:T(8,128)S(1)} %shard_map.58), channel_id=1, source_target_pairs={{0,8},{1,5},{2,10},{3,7},{4,12},{5,1},{6,14},{7,3},{8,0},{9,13},{1... | collective-permute-start | bytes 786440 | tf_op jit(solution)/shard_map/ppermute | solution.py:258
  21.0 1.4 %shard_map.60 = (f32[192,256]{1,0:T(8,128)S(1)}, f32[192,256]{1,0:T(8,128)S(1)}, f32[192,256]{1,0:T(8,128)S(1)}, f32[192,256]{1,0:T(8,128)S(1)}) custom-call(bf16[640,1024]{1,0:T(8,128)(2,1)S(1)} %get-tuple-element.45.lt_high, bf16[640,1024]{1,0:T(8,128)(2,1)S(1)} %get-tuple-element.46.lt_low, f32[1024,128]{1,0:T(8,128)S(1)} %copy-done.1, ...), custom_call_target="tpu_custom_call" | custom-call | bytes 4096 | tf_op jit(solution)/shard_map/pallas_call | solution.py:216
  22.4 1.6 %collective-permute-start.20 = (f32[192,256]{1,0:T(8,128)S(1)}, f32[192,256]{1,0:T(8,128)S(1)}, u32[]{:S(2)}, u32[]{:S(2)}) collective-permute-start(f32[192,256]{1,0:T(8,128)S(1)} %get-tuple-element.56), channel_id=1, source_target_pairs={{0,4},{1,9},{2,6},{3,11},{4,0},{5,13},{6,2},{7,15},{8,12},{9,1},{1... | collective-permute-start | bytes 589832 | tf_op jit(solution)/shard_map/ppermute | solution.py:258
  24.4 2.6 %collective-permute-done.10.v0.v2 = f32[1024,128]{1,0:T(8,128)S(1)} collective-permute-done((f32[1024,128]{1,0:T(8,128)S(1)}, f32[1024,128]{1,0:T(8,128)S(1)}, u32[]{:S(2)}, u32[]{:S(2)}) %collective-permute-start.10) | collective-permute-done | bytes 524320 | tf_op jit(solution)/shard_map/ppermute | solution.py:258
  27.1 2.9 %collective-permute-start.11 = (f32[128,512]{1,0:T(8,128)S(1)}, f32[128,512]{1,0:T(8,128)S(1)}, u32[]{:S(2)}, u32[]{:S(2)}) collective-permute-start(f32[128,512]{1,0:T(8,128)S(1)} %shard_map.61.refs_0_), channel_id=1, source_target_pairs={{0,16},{1,17},{2,18},{3,19},{4,20},{5,21},{6,22},{7,23},{8,24},{9,... | collective-permute-start | bytes 786440 | tf_op jit(solution)/shard_map/ppermute | solution.py:258
  31.2 1.8 %shard_map.59 = (bf16[1024,512]{1,0:T(8,128)(2,1)S(1)}, bf16[1024,512]{1,0:T(8,128)(2,1)S(1)}) custom-call(bf16[512,512]{1,0:T(8,128)(2,1)S(1)} %get-tuple-element.43.t_high, bf16[512,512]{1,0:T(8,128)(2,1)S(1)} %get-tuple-element.44.t_low, f32[1024,128]{1,0:T(8,128)S(1)} %copy-done.1, f32[1024,128]{1,0:T(8,128)S(1)} %collective-permute-done.refs_1_.v1.near1, ...), custom_call_target="tpu_custom_call" | custom-call | flops 1610612736 | bytes 4096 | tf_op jit(solution)/shard_map/pallas_call | solution.py:216
  33.0 1.6 %collective-permute-start.22 = (f32[192,256]{1,0:T(8,128)S(1)}, f32[192,256]{1,0:T(8,128)S(1)}, u32[]{:S(2)}, u32[]{:S(2)}) collective-permute-start(f32[192,256]{1,0:T(8,128)S(1)} %shard_map.68), channel_id=1, source_target_pairs={{0,8},{1,5},{2,10},{3,7},{4,12},{5,1},{6,14},{7,3},{8,0},{9,13},{1... | collective-permute-start | bytes 589832 | tf_op jit(solution)/shard_map/ppermute | solution.py:258
  35.7 5.9 %collective-permute-done.11.refs_1_ = f32[128,512]{1,0:T(8,128)S(1)} collective-permute-done((f32[128,512]{1,0:T(8,128)S(1)}, f32[128,512]{1,0:T(8,128)S(1)}, u32[]{:S(2)}, u32[]{:S(2)}) %collective-permute-start.11) | collective-permute-done | bytes 262176 | tf_op jit(solution)/shard_map/ppermute | solution.py:258
  41.7 1.4 %collective-permute-done.22.refs_2_ = f32[192,256]{1,0:T(8,128)S(1)} collective-permute-done((f32[192,256]{1,0:T(8,128)S(1)}, f32[192,256]{1,0:T(8,128)S(1)}, u32[]{:S(2)}, u32[]{:S(2)}) %collective-permute-start.22) | collective-permute-done | bytes 196640 | tf_op jit(solution)/shard_map/ppermute | solution.py:258
  43.1 1.7 %collective-permute-start.23 = (f32[192,256]{1,0:T(8,128)S(1)}, f32[192,256]{1,0:T(8,128)S(1)}, u32[]{:S(2)}, u32[]{:S(2)}) collective-permute-start(f32[192,256]{1,0:T(8,128)S(1)} %shard_map.69.refs_0_), channel_id=1, source_target_pairs={{0,16},{1,17},{2,18},{3,19},{4,20},{5,21},{6,22},{7,23},{8,24},{9,... | collective-permute-start | bytes 589832 | tf_op jit(solution)/shard_map/ppermute | solution.py:258
  45.9 2.5 %collective-permute-start.16 = (f32[128,512]{1,0:T(8,128)S(1)}, f32[128,512]{1,0:T(8,128)S(1)}, u32[]{:S(2)}, u32[]{:S(2)}) collective-permute-start(f32[128,512]{1,0:T(8,128)S(1)} %shard_map.63.refs_0_), channel_id=1, source_target_pairs={{0,8},{1,5},{2,10},{3,7},{4,12},{5,1},{6,14},{7,3},{8,0},{9,13},{1... | collective-permute-start | bytes 786440 | tf_op jit(solution)/shard_map/ppermute | solution.py:258
  49.2 1.2 %collective-permute-start.27 = (f32[128,256]{1,0:T(8,128)S(1)}, f32[128,256]{1,0:T(8,128)S(1)}, u32[]{:S(2)}, u32[]{:S(2)}) collective-permute-start(f32[128,256]{1,0:T(8,128)S(1)} %get-tuple-element.62), channel_id=1, source_target_pairs={{0,4},{1,9},{2,6},{3,11},{4,0},{5,13},{6,2},{7,15},{8,12},{9,1},{1... | collective-permute-start | bytes 393224 | tf_op jit(solution)/shard_map/ppermute | solution.py:258
  50.8 2.5 %collective-permute-start.28 = (f32[128,256]{1,0:T(8,128)S(1)}, f32[128,256]{1,0:T(8,128)S(1)}, u32[]{:S(2)}, u32[]{:S(2)}) collective-permute-start(f32[128,256]{1,0:T(8,128)S(1)} %shard_map.64), channel_id=1, source_target_pairs={{0,8},{1,5},{2,10},{3,7},{4,12},{5,1},{6,14},{7,3},{8,0},{9,13},{1... | collective-permute-start | bytes 393224 | tf_op jit(solution)/shard_map/ppermute | solution.py:258
  54.4 1.5 %collective-permute-start.26 = (f32[64,256]{1,0:T(8,128)S(1)}, f32[64,256]{1,0:T(8,128)S(1)}, u32[]{:S(2)}, u32[]{:S(2)}) collective-permute-start(f32[64,256]{1,0:T(8,128)S(1)} %slice.9), channel_id=1, source_target_pairs={{0,2},{1,3},{2,0},{3,1},{4,6},{5,7},{6,4},{7,5},{8,10},{9,11},{10,... | collective-permute-start | bytes 196616 | tf_op jit(solution)/shard_map/ppermute | solution.py:258
  55.9 1.8 %shard_map.67 = (bf16[1024,512]{1,0:T(8,128)(2,1)S(1)}, bf16[1024,512]{1,0:T(8,128)(2,1)S(1)}) custom-call(bf16[512,512]{1,0:T(8,128)(2,1)S(1)} %get-tuple-element.67.t_high, bf16[512,512]{1,0:T(8,128)(2,1)S(1)} %get-tuple-element.68.t_low, f32[1024,128]{1,0:T(8,128)S(1)} %copy-done.2, f32[1024,128]{1,0:T(8,128)S(1)} %collective-permute-done.2.refs_3_.v1, ...), custom_call_target="tpu_custom_call" | custom-call | flops 1610612736 | bytes 4096 | tf_op jit(solution)/shard_map/pallas_call | solution.py:216
  57.7 1.6 %collective-permute-start.17 = (f32[128,512]{1,0:T(8,128)S(1)}, f32[128,512]{1,0:T(8,128)S(1)}, u32[]{:S(2)}, u32[]{:S(2)}) collective-permute-start(f32[128,512]{1,0:T(8,128)S(1)} %shard_map.63.refs_0_), channel_id=1, source_target_pairs={{0,4},{1,9},{2,6},{3,11},{4,0},{5,13},{6,2},{7,15},{8,12},{9,1},{1... | collective-permute-start | bytes 786440 | tf_op jit(solution)/shard_map/ppermute | solution.py:258
  60.2 2.2 %collective-permute-start.32 = (f32[128,256]{1,0:T(8,128)S(1)}, f32[128,256]{1,0:T(8,128)S(1)}, u32[]{:S(2)}, u32[]{:S(2)}) collective-permute-start(f32[128,256]{1,0:T(8,128)S(1)} %shard_map.71.refs_0_), channel_id=1, source_target_pairs={{0,16},{1,17},{2,18},{3,19},{4,20},{5,21},{6,22},{7,23},{8,24},{9,... | collective-permute-start | bytes 393224 | tf_op jit(solution)/shard_map/ppermute | solution.py:258
  62.3 1.1 %collective-permute-start.30 = (f32[256,256]{1,0:T(8,128)S(1)}, f32[256,256]{1,0:T(8,128)S(1)}, u32[]{:S(2)}, u32[]{:S(2)}) collective-permute-start(f32[256,256]{1,0:T(8,128)S(1)} %shard_map.72.refs_0_.refs_4_), channel_id=1, source_target_pairs={{0,4},{1,9},{2,6},{3,11},{4,0},{5,13},{6,2},{7,15},{8,12},{9,1},{1... | collective-permute-start | bytes 786440 | tf_op jit(solution)/shard_map/ppermute | solution.py:258
  63.4 2.9 %collective-permute-done.17.refs_2_ = f32[128,512]{1,0:T(8,128)S(1)} collective-permute-done((f32[128,512]{1,0:T(8,128)S(1)}, f32[128,512]{1,0:T(8,128)S(1)}, u32[]{:S(2)}, u32[]{:S(2)}) %collective-permute-start.17) | collective-permute-done | bytes 262176 | tf_op jit(solution)/shard_map/ppermute | solution.py:258
  66.4 2.8 %collective-permute-done.19.refs_3_ = f32[128,512]{1,0:T(8,128)S(1)} collective-permute-done((f32[128,512]{1,0:T(8,128)S(1)}, f32[128,512]{1,0:T(8,128)S(1)}, u32[]{:S(2)}, u32[]{:S(2)}) %collective-permute-start.19) | collective-permute-done | bytes 262176 | tf_op jit(solution)/shard_map/ppermute | solution.py:258
  69.2 2.3 %collective-permute-done.29.refs_1_.refs_5_ = f32[256,256]{1,0:T(8,128)S(1)} collective-permute-done((f32[256,256]{1,0:T(8,128)S(1)}, f32[256,256]{1,0:T(8,128)S(1)}, u32[]{:S(2)}, u32[]{:S(2)}) %collective-permute-start.29) | collective-permute-done | bytes 262176 | tf_op jit(solution)/shard_map/ppermute | solution.py:258
  72.4 2.0 %shard_map.65 = (f32[1024,512]{1,0:T(8,128)S(1)}, f32[512,512]{1,0:T(8,128)S(1)}) custom-call(s32[5]{0:T(128)S(1)} %stack.23.place, f32[1024,512]{1,0:T(8,128)S(1)} %copy-done, bf16[512,512]{1,0:T(8,128)(2,1)S(1)} %get-tuple-element.43.t_high, bf16[512,512]{1,0:T(8,128)(2,1)S(1)} %get-tuple-element.44.t_low, ...), custom_call_target="tpu_custom_call" | custom-call | flops 1207959552 | bytes 4096 | tf_op jit(solution)/shard_map/pallas_call | solution.py:216
  74.4 2.9 %collective-permute-done.33.b1 = f32[128,256]{1,0:T(8,128)S(1)} collective-permute-done((f32[128,256]{1,0:T(8,128)S(1)}, f32[128,256]{1,0:T(8,128)S(1)}, u32[]{:S(2)}, u32[]{:S(2)}) %collective-permute-start.33) | collective-permute-done | bytes 131104 | tf_op jit(solution)/shard_map/ppermute | solution.py:258
  80.6 3.1 %shard_map.75 = (f32[1024,512]{1,0:T(8,128)S(1)}, f32[512,256]{1,0:T(8,128)S(1)}) custom-call(f32[1024,512]{1,0:T(8,128)S(1)} %get-tuple-element.66.x, bf16[512,512]{1,0:T(8,128)(2,1)S(1)} %get-tuple-element.43.t_high, bf16[512,512]{1,0:T(8,128)(2,1)S(1)} %get-tuple-element.44.t_low, bf16[1024,512]{1,0:T(8,128)(2,1)S(1)} %get-tuple-element.51.w_high.w2_high, ...), custom_call_target="tpu_custom_call" | custom-call | flops 2415919104 | bytes 4096 | tf_op jit(solution)/shard_map/pallas_call | solution.py:216
  83.7 1.2 %collective-permute-done.36.b3 = f32[128,256]{1,0:T(8,128)S(1)} collective-permute-done((f32[128,256]{1,0:T(8,128)S(1)}, f32[128,256]{1,0:T(8,128)S(1)}, u32[]{:S(2)}, u32[]{:S(2)}) %collective-permute-start.36) | collective-permute-done | bytes 131104 | tf_op jit(solution)/shard_map/ppermute | solution.py:258
  85.0 2.7 %shard_map.76 = f32[1024,512]{1,0:T(8,128)} custom-call(s32[5]{0:T(128)S(1)} %stack.23.place, f32[1024,512]{1,0:T(8,128)S(1)} %get-tuple-element.79.x, bf16[1024,512]{1,0:T(8,128)(2,1)S(1)} %get-tuple-element.69.w1_high.w_high, bf16[1024,512]{1,0:T(8,128)(2,1)S(1)} %get-tuple-element.70.w1_low.w_low, f32[512,256]{1,0:T(8,128)S(1)} %get-tuple-element.80.rest, ...), custom_call_target="tpu_custom_call" | custom-call | flops 805306368 | bytes 4096 | tf_op jit(solution)/shard_map/pallas_call | solution.py:216
  (79 shorter events, 14.4 us)
Async XLA Ops:
  0.0 6.2 %collective-permute-start = (f32[1024,128]{1,0:T(8,128)}, f32[1024,128]{1,0:T(8,128)S(1)}, u32[]{:S(2)}, u32[]{:S(2)}) collective-permute-start(f32[1024,128]{1,0:T(8,128)} %near0.1), channel_id=1, source_target_pairs={{0,1},{1,0},{2,3},{3,2},{4,5},{5,4},{6,7},{7,6},{8,9},{9,8},{10,11... | collective-permute-start | bytes 1572872 | tf_op jit(solution)/shard_map/ppermute | solution.py:258
  0.5 5.7 %collective-permute-start.2 = (f32[1024,128]{1,0:T(8,128)}, f32[1024,128]{1,0:T(8,128)S(1)}, u32[]{:S(2)}, u32[]{:S(2)}) collective-permute-start(f32[1024,128]{1,0:T(8,128)} %v0.3), channel_id=1, source_target_pairs={{0,1},{1,0},{2,3},{3,2},{4,5},{5,4},{6,7},{7,6},{8,9},{9,8},{10,11... | collective-permute-start | bytes 1572872 | tf_op jit(solution)/shard_map/ppermute | solution.py:258
  0.5 16.8 %collective-permute-start.1 = (f32[1024,128]{1,0:T(8,128)}, f32[1024,128]{1,0:T(8,128)S(1)}, u32[]{:S(2)}, u32[]{:S(2)}) collective-permute-start(f32[1024,128]{1,0:T(8,128)} %near0.1), channel_id=1, source_target_pairs={{0,2},{1,3},{2,0},{3,1},{4,6},{5,7},{6,4},{7,5},{8,10},{9,11},{10,... | collective-permute-start | bytes 1572872 | tf_op jit(solution)/shard_map/ppermute | solution.py:258
  8.0 6.4 %collective-permute-start.3 = (f32[128,512]{1,0:T(8,128)S(1)}, f32[128,512]{1,0:T(8,128)S(1)}, u32[]{:S(2)}, u32[]{:S(2)}) collective-permute-start(f32[128,512]{1,0:T(8,128)S(1)} %get-tuple-element.48), channel_id=1, source_target_pairs={{0,4},{1,9},{2,6},{3,11},{4,0},{5,13},{6,2},{7,15},{8,12},{9,1},{1... | collective-permute-start | bytes 786440 | tf_op jit(solution)/shard_map/ppermute | solution.py:258
  9.6 7.7 %collective-permute-start.4 = (f32[128,512]{1,0:T(8,128)S(1)}, f32[128,512]{1,0:T(8,128)S(1)}, u32[]{:S(2)}, u32[]{:S(2)}) collective-permute-start(f32[128,512]{1,0:T(8,128)S(1)} %get-tuple-element.49), channel_id=1, source_target_pairs={{0,4},{1,9},{2,6},{3,11},{4,0},{5,13},{6,2},{7,15},{8,12},{9,1},{1... | collective-permute-start | bytes 786440 | tf_op jit(solution)/shard_map/ppermute | solution.py:258
  10.1 17.0 %collective-permute-start.10 = (f32[1024,128]{1,0:T(8,128)S(1)}, f32[1024,128]{1,0:T(8,128)S(1)}, u32[]{:S(2)}, u32[]{:S(2)}) collective-permute-start(f32[1024,128]{1,0:T(8,128)S(1)} %copy-done.2), channel_id=1, source_target_pairs={{0,2},{1,3},{2,0},{3,1},{4,6},{5,7},{6,4},{7,5},{8,10},{9,11},{10,... | collective-permute-start | bytes 1572872 | tf_op jit(solution)/shard_map/ppermute | solution.py:258
  17.4 9.6 %collective-permute-start.9 = (f32[128,512]{1,0:T(8,128)S(1)}, f32[128,512]{1,0:T(8,128)S(1)}, u32[]{:S(2)}, u32[]{:S(2)}) collective-permute-start(f32[128,512]{1,0:T(8,128)S(1)} %shard_map.58), channel_id=1, source_target_pairs={{0,8},{1,5},{2,10},{3,7},{4,12},{5,1},{6,14},{7,3},{8,0},{9,13},{1... | collective-permute-start | bytes 786440 | tf_op jit(solution)/shard_map/ppermute | solution.py:258
  22.4 8.3 %collective-permute-start.20 = (f32[192,256]{1,0:T(8,128)S(1)}, f32[192,256]{1,0:T(8,128)S(1)}, u32[]{:S(2)}, u32[]{:S(2)}) collective-permute-start(f32[192,256]{1,0:T(8,128)S(1)} %get-tuple-element.56), channel_id=1, source_target_pairs={{0,4},{1,9},{2,6},{3,11},{4,0},{5,13},{6,2},{7,15},{8,12},{9,1},{1... | collective-permute-start | bytes 589832 | tf_op jit(solution)/shard_map/ppermute | solution.py:258
  23.9 6.8 %collective-permute-start.21 = (f32[192,256]{1,0:T(8,128)S(1)}, f32[192,256]{1,0:T(8,128)S(1)}, u32[]{:S(2)}, u32[]{:S(2)}) collective-permute-start(f32[192,256]{1,0:T(8,128)S(1)} %get-tuple-element.57), channel_id=1, source_target_pairs={{0,4},{1,9},{2,6},{3,11},{4,0},{5,13},{6,2},{7,15},{8,12},{9,1},{1... | collective-permute-start | bytes 589832 | tf_op jit(solution)/shard_map/ppermute | solution.py:258
  27.1 14.5 %collective-permute-start.11 = (f32[128,512]{1,0:T(8,128)S(1)}, f32[128,512]{1,0:T(8,128)S(1)}, u32[]{:S(2)}, u32[]{:S(2)}) collective-permute-start(f32[128,512]{1,0:T(8,128)S(1)} %shard_map.61.refs_0_), channel_id=1, source_target_pairs={{0,16},{1,17},{2,18},{3,19},{4,20},{5,21},{6,22},{7,23},{8,24},{9,... | collective-permute-start | bytes 786440 | tf_op jit(solution)/shard_map/ppermute | solution.py:258
  30.1 3.0 %collective-permute-start.12 = (f32[256,128]{1,0:T(8,128)S(1)}, f32[256,128]{1,0:T(8,128)S(1)}, u32[]{:S(2)}, u32[]{:S(2)}) collective-permute-start(f32[256,128]{1,0:T(8,128)S(1)} %get-tuple-element.84), channel_id=1, source_target_pairs={{0,1},{1,0},{2,3},{3,2},{4,5},{5,4},{6,7},{7,6},{8,9},{9,8},{10,11... | collective-permute-start | bytes 393224 | tf_op jit(solution)/shard_map/ppermute | solution.py:258
  30.1 4.6 %collective-permute-start.13 = (f32[256,128]{1,0:T(8,128)S(1)}, f32[256,128]{1,0:T(8,128)S(1)}, u32[]{:S(2)}, u32[]{:S(2)}) collective-permute-start(f32[256,128]{1,0:T(8,128)S(1)} %get-tuple-element.83), channel_id=1, source_target_pairs={{0,1},{1,0},{2,3},{3,2},{4,5},{5,4},{6,7},{7,6},{8,9},{9,8},{10,11... | collective-permute-start | bytes 393224 | tf_op jit(solution)/shard_map/ppermute | solution.py:258
  30.6 4.1 %collective-permute-start.14 = (f32[256,128]{1,0:T(8,128)S(1)}, f32[256,128]{1,0:T(8,128)S(1)}, u32[]{:S(2)}, u32[]{:S(2)}) collective-permute-start(f32[256,128]{1,0:T(8,128)S(1)} %get-tuple-element.82), channel_id=1, source_target_pairs={{0,1},{1,0},{2,3},{3,2},{4,5},{5,4},{6,7},{7,6},{8,9},{9,8},{10,11... | collective-permute-start | bytes 393224 | tf_op jit(solution)/shard_map/ppermute | solution.py:258
  30.7 4.0 %collective-permute-start.15 = (f32[256,128]{1,0:T(8,128)S(1)}, f32[256,128]{1,0:T(8,128)S(1)}, u32[]{:S(2)}, u32[]{:S(2)}) collective-permute-start(f32[256,128]{1,0:T(8,128)S(1)} %get-tuple-element.81), channel_id=1, source_target_pairs={{0,1},{1,0},{2,3},{3,2},{4,5},{5,4},{6,7},{7,6},{8,9},{9,8},{10,11... | collective-permute-start | bytes 393224 | tf_op jit(solution)/shard_map/ppermute | solution.py:258
  33.0 10.1 %collective-permute-start.22 = (f32[192,256]{1,0:T(8,128)S(1)}, f32[192,256]{1,0:T(8,128)S(1)}, u32[]{:S(2)}, u32[]{:S(2)}) collective-permute-start(f32[192,256]{1,0:T(8,128)S(1)} %shard_map.68), channel_id=1, source_target_pairs={{0,8},{1,5},{2,10},{3,7},{4,12},{5,1},{6,14},{7,3},{8,0},{9,13},{1... | collective-permute-start | bytes 589832 | tf_op jit(solution)/shard_map/ppermute | solution.py:258
  41.6 4.2 %collective-permute-start.24 = (f32[128,512]{1,0:T(8,128)S(1)}, f32[128,512]{1,0:T(8,128)S(1)}, u32[]{:S(2)}, u32[]{:S(2)}) collective-permute-start(f32[128,512]{1,0:T(8,128)S(1)} %shard_map.63.refs_0_), channel_id=1, source_target_pairs={{0,1},{1,0},{2,3},{3,2},{4,5},{5,4},{6,7},{7,6},{8,9},{9,8},{10,11... | collective-permute-start | bytes 786440 | tf_op jit(solution)/shard_map/ppermute | solution.py:258
  43.1 11.2 %collective-permute-start.23 = (f32[192,256]{1,0:T(8,128)S(1)}, f32[192,256]{1,0:T(8,128)S(1)}, u32[]{:S(2)}, u32[]{:S(2)}) collective-permute-start(f32[192,256]{1,0:T(8,128)S(1)} %shard_map.69.refs_0_), channel_id=1, source_target_pairs={{0,16},{1,17},{2,18},{3,19},{4,20},{5,21},{6,22},{7,23},{8,24},{9,... | collective-permute-start | bytes 589832 | tf_op jit(solution)/shard_map/ppermute | solution.py:258
  44.9 5.9 %collective-permute-start.18 = (f32[128,256]{1,0:T(8,128)S(1)}, f32[128,256]{1,0:T(8,128)S(1)}, u32[]{:S(2)}, u32[]{:S(2)}) collective-permute-start(f32[128,256]{1,0:T(8,128)S(1)} %get-tuple-element.63), channel_id=1, source_target_pairs={{0,4},{1,9},{2,6},{3,11},{4,0},{5,13},{6,2},{7,15},{8,12},{9,1},{1... | collective-permute-start | bytes 393224 | tf_op jit(solution)/shard_map/ppermute | solution.py:258
  45.8 8.5 %collective-permute-start.25 = (f32[64,512]{1,0:T(8,128)S(1)}, f32[64,512]{1,0:T(8,128)S(1)}, u32[]{:S(2)}, u32[]{:S(2)}) collective-permute-start(f32[64,512]{1,0:T(8,128)S(1)} %slice.8), channel_id=1, source_target_pairs={{0,1},{1,0},{2,3},{3,2},{4,5},{5,4},{6,7},{7,6},{8,9},{9,8},{10,11... | collective-permute-start | bytes 393224 | tf_op jit(solution)/shard_map/ppermute | solution.py:258
  45.9 13.4 %collective-permute-start.16 = (f32[128,512]{1,0:T(8,128)S(1)}, f32[128,512]{1,0:T(8,128)S(1)}, u32[]{:S(2)}, u32[]{:S(2)}) collective-permute-start(f32[128,512]{1,0:T(8,128)S(1)} %shard_map.63.refs_0_), channel_id=1, source_target_pairs={{0,8},{1,5},{2,10},{3,7},{4,12},{5,1},{6,14},{7,3},{8,0},{9,13},{1... | collective-permute-start | bytes 786440 | tf_op jit(solution)/shard_map/ppermute | solution.py:258
  49.2 10.1 %collective-permute-start.27 = (f32[128,256]{1,0:T(8,128)S(1)}, f32[128,256]{1,0:T(8,128)S(1)}, u32[]{:S(2)}, u32[]{:S(2)}) collective-permute-start(f32[128,256]{1,0:T(8,128)S(1)} %get-tuple-element.62), channel_id=1, source_target_pairs={{0,4},{1,9},{2,6},{3,11},{4,0},{5,13},{6,2},{7,15},{8,12},{9,1},{1... | collective-permute-start | bytes 393224 | tf_op jit(solution)/shard_map/ppermute | solution.py:258
  50.8 8.5 %collective-permute-start.28 = (f32[128,256]{1,0:T(8,128)S(1)}, f32[128,256]{1,0:T(8,128)S(1)}, u32[]{:S(2)}, u32[]{:S(2)}) collective-permute-start(f32[128,256]{1,0:T(8,128)S(1)} %shard_map.64), channel_id=1, source_target_pairs={{0,8},{1,5},{2,10},{3,7},{4,12},{5,1},{6,14},{7,3},{8,0},{9,13},{1... | collective-permute-start | bytes 393224 | tf_op jit(solution)/shard_map/ppermute | solution.py:258
  54.4 5.7 %collective-permute-start.26 = (f32[64,256]{1,0:T(8,128)S(1)}, f32[64,256]{1,0:T(8,128)S(1)}, u32[]{:S(2)}, u32[]{:S(2)}) collective-permute-start(f32[64,256]{1,0:T(8,128)S(1)} %slice.9), channel_id=1, source_target_pairs={{0,2},{1,3},{2,0},{3,1},{4,6},{5,7},{6,4},{7,5},{8,10},{9,11},{10,... | collective-permute-start | bytes 196616 | tf_op jit(solution)/shard_map/ppermute | solution.py:258
  57.7 8.7 %collective-permute-start.17 = (f32[128,512]{1,0:T(8,128)S(1)}, f32[128,512]{1,0:T(8,128)S(1)}, u32[]{:S(2)}, u32[]{:S(2)}) collective-permute-start(f32[128,512]{1,0:T(8,128)S(1)} %shard_map.63.refs_0_), channel_id=1, source_target_pairs={{0,4},{1,9},{2,6},{3,11},{4,0},{5,13},{6,2},{7,15},{8,12},{9,1},{1... | collective-permute-start | bytes 786440 | tf_op jit(solution)/shard_map/ppermute | solution.py:258
  59.3 9.9 %collective-permute-start.19 = (f32[128,512]{1,0:T(8,128)S(1)}, f32[128,512]{1,0:T(8,128)S(1)}, u32[]{:S(2)}, u32[]{:S(2)}) collective-permute-start(f32[128,512]{1,0:T(8,128)S(1)} %collective-permute-done.16.refs_1_), channel_id=1, source_target_pairs={{0,4},{1,9},{2,6},{3,11},{4,0},{5,13},{6,2},{7,15},{8,12},{9,1},{1... | collective-permute-start | bytes 786440 | tf_op jit(solution)/shard_map/ppermute | solution.py:258
  60.1 11.4 %collective-permute-start.29 = (f32[256,256]{1,0:T(8,128)S(1)}, f32[256,256]{1,0:T(8,128)S(1)}, u32[]{:S(2)}, u32[]{:S(2)}) collective-permute-start(f32[256,256]{1,0:T(8,128)S(1)} %shard_map.72.refs_0_.refs_4_), channel_id=1, source_target_pairs={{0,8},{1,5},{2,10},{3,7},{4,12},{5,1},{6,14},{7,3},{8,0},{9,13},{1... | collective-permute-start | bytes 786440 | tf_op jit(solution)/shard_map/ppermute | solution.py:258
  60.2 12.0 %collective-permute-start.32 = (f32[128,256]{1,0:T(8,128)S(1)}, f32[128,256]{1,0:T(8,128)S(1)}, u32[]{:S(2)}, u32[]{:S(2)}) collective-permute-start(f32[128,256]{1,0:T(8,128)S(1)} %shard_map.71.refs_0_), channel_id=1, source_target_pairs={{0,16},{1,17},{2,18},{3,19},{4,20},{5,21},{6,22},{7,23},{8,24},{9,... | collective-permute-start | bytes 393224 | tf_op jit(solution)/shard_map/ppermute | solution.py:258
  62.3 15.0 %collective-permute-start.30 = (f32[256,256]{1,0:T(8,128)S(1)}, f32[256,256]{1,0:T(8,128)S(1)}, u32[]{:S(2)}, u32[]{:S(2)}) collective-permute-start(f32[256,256]{1,0:T(8,128)S(1)} %shard_map.72.refs_0_.refs_4_), channel_id=1, source_target_pairs={{0,4},{1,9},{2,6},{3,11},{4,0},{5,13},{6,2},{7,15},{8,12},{9,1},{1... | collective-permute-start | bytes 786440 | tf_op jit(solution)/shard_map/ppermute | solution.py:258
  71.5 6.4 %collective-permute-start.31 = (f32[256,256]{1,0:T(8,128)S(1)}, f32[256,256]{1,0:T(8,128)S(1)}, u32[]{:S(2)}, u32[]{:S(2)}) collective-permute-start(f32[256,256]{1,0:T(8,128)S(1)} %collective-permute-done.29.refs_1_.refs_5_), channel_id=1, source_target_pairs={{0,4},{1,9},{2,6},{3,11},{4,0},{5,13},{6,2},{7,15},{8,12},{9,1},{1... | collective-permute-start | bytes 786440 | tf_op jit(solution)/shard_map/ppermute | solution.py:258
  72.2 5.2 %collective-permute-start.33 = (f32[128,256]{1,0:T(8,128)S(1)}, f32[128,256]{1,0:T(8,128)S(1)}, u32[]{:S(2)}, u32[]{:S(2)}) collective-permute-start(f32[128,256]{1,0:T(8,128)S(1)} %shard_map.73.b0), channel_id=1, source_target_pairs={{0,8},{1,5},{2,10},{3,7},{4,12},{5,1},{6,14},{7,3},{8,0},{9,13},{1... | collective-permute-start | bytes 393224 | tf_op jit(solution)/shard_map/ppermute | solution.py:258
  78.5 5.2 %collective-permute-start.35 = (f32[128,256]{1,0:T(8,128)S(1)}, f32[128,256]{1,0:T(8,128)S(1)}, u32[]{:S(2)}, u32[]{:S(2)}) collective-permute-start(f32[128,256]{1,0:T(8,128)S(1)} %shard_map.73.b0), channel_id=1, source_target_pairs={{0,4},{1,9},{2,6},{3,11},{4,0},{5,13},{6,2},{7,15},{8,12},{9,1},{1... | collective-permute-start | bytes 393224 | tf_op jit(solution)/shard_map/ppermute | solution.py:258
  79.6 5.4 %collective-permute-start.36 = (f32[128,256]{1,0:T(8,128)S(1)}, f32[128,256]{1,0:T(8,128)S(1)}, u32[]{:S(2)}, u32[]{:S(2)}) collective-permute-start(f32[128,256]{1,0:T(8,128)S(1)} %collective-permute-done.33.b1), channel_id=1, source_target_pairs={{0,4},{1,9},{2,6},{3,11},{4,0},{5,13},{6,2},{7,15},{8,12},{9,1},{1... | collective-permute-start | bytes 393224 | tf_op jit(solution)/shard_map/ppermute | solution.py:258
  (10 other events, 64.6 us)

commit v3 on v2

--- a/solution.py
+++ b/solution.py
@@ -120,7 +120,7 @@
 
 
 def cross_kernel(wide, place, *refs):
-    blocks, out = refs[:GROUP], refs[GROUP]
+    blocks, out = refs[:GROUP], refs[-1]
     width = out.shape[0] // 2
     half = out.shape[1] // 2
     thin = width // GROUP
@@ -280,8 +280,8 @@
     def pad(value, rows=wide):
         return to_col(value[:rows], 1)
 
-    def relayed(far):
-        return far, *(to_col(piece, 1) for piece in jnp.split(far, 4))
+    def relayed(far, pieces):
+        return far, *(to_col(piece, 1) for piece in jnp.split(far, pieces))
 
     def projections(height, size):
         return [((height, size), f32)] * GROUP
@@ -294,8 +294,8 @@
         got = to_two(mine)
         return mine, got, to_one(mine), to_one(after(got, *earlier))
 
-    second_far = to_col(panel_second, 2)
-    first_far = to_col(panel_first, 2)
+    second_across = to_col(panel_second, 2)
+    first_across = to_col(panel_first, 2)
     second_near = (panel_second, to_col(panel_second, 1))
     first_near = (panel_first, to_col(panel_first, 1))
 
@@ -317,19 +317,18 @@
     )
     near_got = to_one(near_parts[2])
     near_other = add(near_parts[1], to_one(near_parts[3]), pads=(near_got,))
-
-    second_far = relayed(after(second_far, near_other))
+    second_far = relayed(after(second_across, near_other), 4)
     second = second_near + second_far
     second_parts = call(
         project_cross_kernel,
         projections(wide + 2 * thin, half),
         (lt_high, lt_low, *second),
     )
-    near_sum = add(near_parts[0], near_got, after(to_two(near_other), second_parts, first_far))
+    near_sum = add(near_parts[0], near_got, after(to_two(near_other), second_parts))
     second_got = to_one(second_parts[2])
     second_other = add(second_parts[1], to_one(second_parts[3]), pads=(second_got,))
     second_sum = add(second_parts[0], second_got, to_two(second_other))
-    first_far = relayed(after(first_far, near_sum))
+    first_far = relayed(after(first_across, near_sum), 4)
     first = first_near + first_far
     first_parts = call(project_last_kernel, projections(wide, half), (lt_high, lt_low, *first_far))
     arrange = functools.partial(call, functools.partial(arrange_kernel, width), [((total, total), bf16)] * 2, scalars=1)
@@ -338,12 +337,13 @@
     t2 = arrange((place, factor_second), rows * total // 2)
     w2 = factor((*t2, *second), rows * total * total)
     w1 = factor((*t1, *first), rows * total * total)
-    near_sum = across(near_sum, first_parts, w2)
-    first_other = add(first_parts[1], to_one(first_parts[3]))
-    first_sum = add(first_parts[0], to_one(first_parts[2]), to_two(first_other))
-    second_sum = across(second_sum, first_other, pads=(pad(pad(near_sum), wide // 2),))
-    near = spread(near_sum, first_other)
-
+    first_got = to_one(first_parts[2])
+    first_other = add(first_parts[1], to_one(first_parts[3]), pads=(first_got,))
+    first_sum = add(first_parts[0], first_got, after(to_two(first_other), second_sum))
+    near_total = across(near_sum, first_parts, w2)
+    second_total = across(after(second_sum, near_total), first_other, pads=(pad(pad(near_total), wide // 2),))
+    near_two = to_two(near_total)
+    near = (near_total, near_two, to_one(near_total), to_one(after(near_two, first_other)))
     left, coefficients = call(
         near_kernel,
         [((rows, cols), f32), ((cols, total), f32)],
@@ -351,15 +351,19 @@
         (rows + total) * cols * half,
         scalars=1,
     )
-
-    second_sum = pile(second_sum, after(to_col(second_sum[wide:], 2), first_sum, w1))
-    first_sum = across(first_sum)
-    second_blocks = spread(second_sum, near)
-    first_blocks = spread(first_sum)
+    second_packed = pile(second_total, after(to_col(second_total[wide:], 2), first_sum, w1))
+    second_two = to_two(second_packed)
+    first_total = across(after(first_sum, second_total))
+    second_one = to_one(second_packed)
+    second_last = to_one(after(second_two, near))
+    second_blocks = (second_packed, second_two, second_one, second_last)
+    first_two = to_two(first_total)
+    first_one = to_one(first_total)
+    first_blocks = (first_total, first_two, first_one, to_one(first_two))
     (cross,) = call(
         functools.partial(cross_kernel, wide),
         [((2 * width, total), f32)],
-        (place, *after(second_blocks, left, first_blocks[1])),
+        (place, *after(second_blocks, left, first_two)),
         scalars=1,
     )
     cross_core = to_col(cross, 1)

time: 87.8 us -> 85.6 us (0.975)
  waiting for transfers between devices: 31.8 us -> 29.6 us
    ppermute x37, waiting for transfers between devices: 31.8 us -> 29.6 us  [permute(): return lax.ppermute(value, ('row', 'col'), pairs)]
where the time goes in v3:
time: 85.6 us; the launch traced here: 85.5 us
  starting transfers between devices  35 us (41%)
  waiting for transfers between devices  29.6 us (35%)
  Pallas kernels  20.4 us (24%)
    ppermute x37, starting transfers between devices, permute(): return lax.ppermute(value, ('row', 'col'), pairs)  35 us
    ppermute x37, waiting for transfers between devices, permute(): return lax.ppermute(value, ('row', 'col'), pairs)  29.6 us
    pallas_call x22, Pallas kernels, call(): pl.pallas_call(kernel, out_shape=tuple((jax.ShapeDtypeStruct(shape, dtype...  20.4 us
  transfers between devices with their start and end apart: 37, of which 15 were waited for; matrix products, arithmetic and copies ran while one was open for 0% of the time, Pallas kernels for 20%

profile of v3, /device:TPU:0, one launch (start us, length us, event | category | flops | bytes accessed | tf_op | source)
XLA Modules:
  0.0 85.5 jit_solution(9199739827404674336)
XLA Ops:
  0.5 3.0 %collective-permute-start.1 = (f32[1024,128]{1,0:T(8,128)}, f32[1024,128]{1,0:T(8,128)S(1)}, u32[]{:S(2)}, u32[]{:S(2)}) collective-permute-start(f32[1024,128]{1,0:T(8,128)} %near0.1), channel_id=1, source_target_pairs={{0,2},{1,3},{2,0},{3,1},{4,6},{5,7},{6,4},{7,5},{8,10},{9,11},{10,... | collective-permute-start | bytes 1572872 | tf_op jit(solution)/shard_map/ppermute | solution.py:258
  3.6 2.6 %shard_map.56 = (bf16[640,1024]{1,0:T(8,128)(2,1)S(1)}, bf16[640,1024]{1,0:T(8,128)(2,1)S(1)}) custom-call(s32[5]{0:T(128)S(1)} %stack.23.place, f32[1024,512]{1,0:T(8,128)} %x.3, f32[1024,128]{1,0:T(8,128)} %v0.3), custom_call_target="tpu_custom_call" | custom-call | bytes 4096 | tf_op jit(solution)/shard_map/pallas_call | solution.py:216
  6.2 1.8 %shard_map.57 = (f32[128,512]{1,0:T(8,128)S(1)}, f32[128,512]{1,0:T(8,128)S(1)}, f32[128,512]{1,0:T(8,128)S(1)}, f32[128,512]{1,0:T(8,128)S(1)}) custom-call(bf16[640,1024]{1,0:T(8,128)(2,1)S(1)} %get-tuple-element.48.lt_high, bf16[640,1024]{1,0:T(8,128)(2,1)S(1)} %get-tuple-element.49.lt_low, f32[1024,128]{1,0:T(8,128)S(1)} %copy-done.1, ...), custom_call_target="tpu_custom_call" | custom-call | bytes 4096 | tf_op jit(solution)/shard_map/pallas_call | solution.py:216
  8.0 1.6 %collective-permute-start.3 = (f32[128,512]{1,0:T(8,128)S(1)}, f32[128,512]{1,0:T(8,128)S(1)}, u32[]{:S(2)}, u32[]{:S(2)}) collective-permute-start(f32[128,512]{1,0:T(8,128)S(1)} %get-tuple-element.51), channel_id=1, source_target_pairs={{0,4},{1,9},{2,6},{3,11},{4,0},{5,13},{6,2},{7,15},{8,12},{9,1},{1... | collective-permute-start | bytes 786440 | tf_op jit(solution)/shard_map/ppermute | solution.py:258
  10.2 4.3 %collective-permute-done.3.refs_1_ = f32[128,512]{1,0:T(8,128)S(1)} collective-permute-done((f32[128,512]{1,0:T(8,128)S(1)}, f32[128,512]{1,0:T(8,128)S(1)}, u32[]{:S(2)}, u32[]{:S(2)}) %collective-permute-start.3) | collective-permute-done | bytes 262176 | tf_op jit(solution)/shard_map/ppermute | solution.py:258
  14.5 2.8 %collective-permute-done.4.refs_2_.refs_1_ = f32[128,512]{1,0:T(8,128)S(1)} collective-permute-done((f32[128,512]{1,0:T(8,128)S(1)}, f32[128,512]{1,0:T(8,128)S(1)}, u32[]{:S(2)}, u32[]{:S(2)}) %collective-permute-start.4) | collective-permute-done | bytes 262176 | tf_op jit(solution)/shard_map/ppermute | solution.py:258
  17.4 1.6 %collective-permute-start.9 = (f32[128,512]{1,0:T(8,128)S(1)}, f32[128,512]{1,0:T(8,128)S(1)}, u32[]{:S(2)}, u32[]{:S(2)}) collective-permute-start(f32[128,512]{1,0:T(8,128)S(1)} %shard_map.58), channel_id=1, source_target_pairs={{0,8},{1,5},{2,10},{3,7},{4,12},{5,1},{6,14},{7,3},{8,0},{9,13},{1... | collective-permute-start | bytes 786440 | tf_op jit(solution)/shard_map/ppermute | solution.py:258
  21.0 1.4 %shard_map.60 = (f32[192,256]{1,0:T(8,128)S(1)}, f32[192,256]{1,0:T(8,128)S(1)}, f32[192,256]{1,0:T(8,128)S(1)}, f32[192,256]{1,0:T(8,128)S(1)}) custom-call(bf16[640,1024]{1,0:T(8,128)(2,1)S(1)} %get-tuple-element.48.lt_high, bf16[640,1024]{1,0:T(8,128)(2,1)S(1)} %get-tuple-element.49.lt_low, f32[1024,128]{1,0:T(8,128)S(1)} %copy-done.1, ...), custom_call_target="tpu_custom_call" | custom-call | bytes 4096 | tf_op jit(solution)/shard_map/pallas_call | solution.py:216
  22.3 1.6 %collective-permute-start.21 = (f32[192,256]{1,0:T(8,128)S(1)}, f32[192,256]{1,0:T(8,128)S(1)}, u32[]{:S(2)}, u32[]{:S(2)}) collective-permute-start(f32[192,256]{1,0:T(8,128)S(1)} %get-tuple-element.59), channel_id=1, source_target_pairs={{0,4},{1,9},{2,6},{3,11},{4,0},{5,13},{6,2},{7,15},{8,12},{9,1},{1... | collective-permute-start | bytes 589832 | tf_op jit(solution)/shard_map/ppermute | solution.py:258
  24.5 2.7 %collective-permute-start.10 = (f32[128,512]{1,0:T(8,128)S(1)}, f32[128,512]{1,0:T(8,128)S(1)}, u32[]{:S(2)}, u32[]{:S(2)}) collective-permute-start(f32[128,512]{1,0:T(8,128)S(1)} %shard_map.61.refs_0_), channel_id=1, source_target_pairs={{0,16},{1,17},{2,18},{3,19},{4,20},{5,21},{6,22},{7,23},{8,24},{9,... | collective-permute-start | bytes 786440 | tf_op jit(solution)/shard_map/ppermute | solution.py:258
  28.1 2.1 %collective-permute-done.22.refs_1_ = f32[192,256]{1,0:T(8,128)S(1)} collective-permute-done((f32[192,256]{1,0:T(8,128)S(1)}, f32[192,256]{1,0:T(8,128)S(1)}, u32[]{:S(2)}, u32[]{:S(2)}) %collective-permute-start.22) | collective-permute-done | bytes 196640 | tf_op jit(solution)/shard_map/ppermute | solution.py:258
  30.2 3.1 %collective-permute-start.15 = (f32[256,128]{1,0:T(8,128)S(1)}, f32[256,128]{1,0:T(8,128)S(1)}, u32[]{:S(2)}, u32[]{:S(2)}) collective-permute-start(f32[256,128]{1,0:T(8,128)S(1)} %get-tuple-element.87), channel_id=1, source_target_pairs={{0,1},{1,0},{2,3},{3,2},{4,5},{5,4},{6,7},{7,6},{8,9},{9,8},{10,11... | collective-permute-start | bytes 393224 | tf_op jit(solution)/shard_map/ppermute | solution.py:258
  33.3 1.8 %shard_map.59 = (bf16[1024,512]{1,0:T(8,128)(2,1)S(1)}, bf16[1024,512]{1,0:T(8,128)(2,1)S(1)}) custom-call(bf16[512,512]{1,0:T(8,128)(2,1)S(1)} %get-tuple-element.46.t_high, bf16[512,512]{1,0:T(8,128)(2,1)S(1)} %get-tuple-element.47.t_low, f32[1024,128]{1,0:T(8,128)S(1)} %copy-done.1, f32[1024,128]{1,0:T(8,128)S(1)} %collective-permute-done.refs_1_.v1.near1, ...), custom_call_target="tpu_custom_call" | custom-call | flops 1610612736 | bytes 4096 | tf_op jit(solution)/shard_map/pallas_call | solution.py:216
  36.3 2.7 %collective-permute-done.10.refs_1_ = f32[128,512]{1,0:T(8,128)S(1)} collective-permute-done((f32[128,512]{1,0:T(8,128)S(1)}, f32[128,512]{1,0:T(8,128)S(1)}, u32[]{:S(2)}, u32[]{:S(2)}) %collective-permute-start.10) | collective-permute-done | bytes 262176 | tf_op jit(solution)/shard_map/ppermute | solution.py:258
  39.1 2.0 %collective-permute-done.23.refs_2_ = f32[192,256]{1,0:T(8,128)S(1)} collective-permute-done((f32[192,256]{1,0:T(8,128)S(1)}, f32[192,256]{1,0:T(8,128)S(1)}, u32[]{:S(2)}, u32[]{:S(2)}) %collective-permute-start.23) | collective-permute-done | bytes 196640 | tf_op jit(solution)/shard_map/ppermute | solution.py:258
  41.1 1.6 %collective-permute-start.24 = (f32[192,256]{1,0:T(8,128)S(1)}, f32[192,256]{1,0:T(8,128)S(1)}, u32[]{:S(2)}, u32[]{:S(2)}) collective-permute-start(f32[192,256]{1,0:T(8,128)S(1)} %shard_map.69.refs_0_), channel_id=1, source_target_pairs={{0,16},{1,17},{2,18},{3,19},{4,20},{5,21},{6,22},{7,23},{8,24},{9,... | collective-permute-start | bytes 589832 | tf_op jit(solution)/shard_map/ppermute | solution.py:258
  44.9 2.5 %collective-permute-start.16 = (f32[128,512]{1,0:T(8,128)S(1)}, f32[128,512]{1,0:T(8,128)S(1)}, u32[]{:S(2)}, u32[]{:S(2)}) collective-permute-start(f32[128,512]{1,0:T(8,128)S(1)} %shard_map.63.refs_0_), channel_id=1, source_target_pairs={{0,8},{1,5},{2,10},{3,7},{4,12},{5,1},{6,14},{7,3},{8,0},{9,13},{1... | collective-permute-start | bytes 786440 | tf_op jit(solution)/shard_map/ppermute | solution.py:258
  48.1 2.1 %collective-permute-done.19.refs_2_.refs_1_ = f32[128,256]{1,0:T(8,128)S(1)} collective-permute-done((f32[128,256]{1,0:T(8,128)S(1)}, f32[128,256]{1,0:T(8,128)S(1)}, u32[]{:S(2)}, u32[]{:S(2)}) %collective-permute-start.19) | collective-permute-done | bytes 131104 | tf_op jit(solution)/shard_map/ppermute | solution.py:258
  50.2 2.5 %collective-permute-start.28 = (f32[128,256]{1,0:T(8,128)S(1)}, f32[128,256]{1,0:T(8,128)S(1)}, u32[]{:S(2)}, u32[]{:S(2)}) collective-permute-start(f32[128,256]{1,0:T(8,128)S(1)} %shard_map.64), channel_id=1, source_target_pairs={{0,8},{1,5},{2,10},{3,7},{4,12},{5,1},{6,14},{7,3},{8,0},{9,13},{1... | collective-permute-start | bytes 393224 | tf_op jit(solution)/shard_map/ppermute | solution.py:258
  52.8 1.2 %collective-permute-start.27 = (f32[64,256]{1,0:T(8,128)S(1)}, f32[64,256]{1,0:T(8,128)S(1)}, u32[]{:S(2)}, u32[]{:S(2)}) collective-permute-start(f32[64,256]{1,0:T(8,128)S(1)} %slice.9), channel_id=1, source_target_pairs={{0,2},{1,3},{2,0},{3,1},{4,6},{5,7},{6,4},{7,5},{8,10},{9,11},{10,... | collective-permute-start | bytes 196616 | tf_op jit(solution)/shard_map/ppermute | solution.py:258
  54.0 1.8 %shard_map.67 = (bf16[1024,512]{1,0:T(8,128)(2,1)S(1)}, bf16[1024,512]{1,0:T(8,128)(2,1)S(1)}) custom-call(bf16[512,512]{1,0:T(8,128)(2,1)S(1)} %get-tuple-element.70.t_high, bf16[512,512]{1,0:T(8,128)(2,1)S(1)} %get-tuple-element.71.t_low, f32[1024,128]{1,0:T(8,128)S(1)} %copy-done.2, f32[1024,128]{1,0:T(8,128)S(1)} %collective-permute-done.2.refs_3_.v1, ...), custom_call_target="tpu_custom_call" | custom-call | flops 1610612736 | bytes 4096 | tf_op jit(solution)/shard_map/pallas_call | solution.py:216
  57.0 1.1 %collective-permute-start.20 = (f32[128,512]{1,0:T(8,128)S(1)}, f32[128,512]{1,0:T(8,128)S(1)}, u32[]{:S(2)}, u32[]{:S(2)}) collective-permute-start(f32[128,512]{1,0:T(8,128)S(1)} %collective-permute-done.16.refs_1_), channel_id=1, source_target_pairs={{0,4},{1,9},{2,6},{3,11},{4,0},{5,13},{6,2},{7,15},{8,12},{9,1},{1... | collective-permute-start | bytes 786440 | tf_op jit(solution)/shard_map/ppermute | solution.py:258
  59.4 1.7 %collective-permute-start.30 = (f32[256,256]{1,0:T(8,128)S(1)}, f32[256,256]{1,0:T(8,128)S(1)}, u32[]{:S(2)}, u32[]{:S(2)}) collective-permute-start(f32[256,256]{1,0:T(8,128)S(1)} %shard_map.72.refs_0_.refs_4_), channel_id=1, source_target_pairs={{0,4},{1,9},{2,6},{3,11},{4,0},{5,13},{6,2},{7,15},{8,12},{9,1},{1... | collective-permute-start | bytes 786440 | tf_op jit(solution)/shard_map/ppermute | solution.py:258
  61.2 3.2 %collective-permute-done.17.refs_2_ = f32[128,512]{1,0:T(8,128)S(1)} collective-permute-done((f32[128,512]{1,0:T(8,128)S(1)}, f32[128,512]{1,0:T(8,128)S(1)}, u32[]{:S(2)}, u32[]{:S(2)}) %collective-permute-start.17) | collective-permute-done | bytes 262176 | tf_op jit(solution)/shard_map/ppermute | solution.py:258
  64.4 2.8 %collective-permute-done.20.refs_3_ = f32[128,512]{1,0:T(8,128)S(1)} collective-permute-done((f32[128,512]{1,0:T(8,128)S(1)}, f32[128,512]{1,0:T(8,128)S(1)}, u32[]{:S(2)}, u32[]{:S(2)}) %collective-permute-start.20) | collective-permute-done | bytes 262176 | tf_op jit(solution)/shard_map/ppermute | solution.py:258
  67.2 2.1 %collective-permute-done.29.refs_1_.refs_5_ = f32[256,256]{1,0:T(8,128)S(1)} collective-permute-done((f32[256,256]{1,0:T(8,128)S(1)}, f32[256,256]{1,0:T(8,128)S(1)}, u32[]{:S(2)}, u32[]{:S(2)}) %collective-permute-start.29) | collective-permute-done | bytes 262176 | tf_op jit(solution)/shard_map/ppermute | solution.py:258
  70.4 2.0 %shard_map.65 = (f32[1024,512]{1,0:T(8,128)S(1)}, f32[512,512]{1,0:T(8,128)S(1)}) custom-call(s32[5]{0:T(128)S(1)} %stack.23.place, f32[1024,512]{1,0:T(8,128)S(1)} %copy-done, bf16[512,512]{1,0:T(8,128)(2,1)S(1)} %get-tuple-element.46.t_high, bf16[512,512]{1,0:T(8,128)(2,1)S(1)} %get-tuple-element.47.t_low, ...), custom_call_target="tpu_custom_call" | custom-call | flops 1207959552 | bytes 4096 | tf_op jit(solution)/shard_map/pallas_call | solution.py:216
  72.4 3.0 %collective-permute-done.33.b1 = f32[128,256]{1,0:T(8,128)S(1)} collective-permute-done((f32[128,256]{1,0:T(8,128)S(1)}, f32[128,256]{1,0:T(8,128)S(1)}, u32[]{:S(2)}, u32[]{:S(2)}) %collective-permute-start.33) | collective-permute-done | bytes 131104 | tf_op jit(solution)/shard_map/ppermute | solution.py:258
  76.4 1.1 %collective-permute-start.35 = (f32[128,256]{1,0:T(8,128)S(1)}, f32[128,256]{1,0:T(8,128)S(1)}, u32[]{:S(2)}, u32[]{:S(2)}) collective-permute-start(f32[128,256]{1,0:T(8,128)S(1)} %shard_map.73.b0), channel_id=1, source_target_pairs={{0,4},{1,9},{2,6},{3,11},{4,0},{5,13},{6,2},{7,15},{8,12},{9,1},{1... | collective-permute-start | bytes 393224 | tf_op jit(solution)/shard_map/ppermute | solution.py:258
  78.5 3.1 %shard_map.75 = (f32[1024,512]{1,0:T(8,128)S(1)}, f32[512,256]{1,0:T(8,128)S(1)}) custom-call(f32[1024,512]{1,0:T(8,128)S(1)} %get-tuple-element.69.x, bf16[512,512]{1,0:T(8,128)(2,1)S(1)} %get-tuple-element.46.t_high, bf16[512,512]{1,0:T(8,128)(2,1)S(1)} %get-tuple-element.47.t_low, bf16[1024,512]{1,0:T(8,128)(2,1)S(1)} %get-tuple-element.54.w_high.w2_high, ...), custom_call_target="tpu_custom_call" | custom-call | flops 2415919104 | bytes 4096 | tf_op jit(solution)/shard_map/pallas_call | solution.py:216
  81.6 1.2 %collective-permute-done.36.b3 = f32[128,256]{1,0:T(8,128)S(1)} collective-permute-done((f32[128,256]{1,0:T(8,128)S(1)}, f32[128,256]{1,0:T(8,128)S(1)}, u32[]{:S(2)}, u32[]{:S(2)}) %collective-permute-start.36) | collective-permute-done | bytes 131104 | tf_op jit(solution)/shard_map/ppermute | solution.py:258
  82.8 2.7 %shard_map.76 = f32[1024,512]{1,0:T(8,128)} custom-call(s32[5]{0:T(128)S(1)} %stack.23.place, f32[1024,512]{1,0:T(8,128)S(1)} %get-tuple-element.85.x, bf16[1024,512]{1,0:T(8,128)(2,1)S(1)} %get-tuple-element.72.w1_high.w_high, bf16[1024,512]{1,0:T(8,128)(2,1)S(1)} %get-tuple-element.73.w1_low.w_low, f32[512,256]{1,0:T(8,128)S(1)} %get-tuple-element.86.rest, ...), custom_call_target="tpu_custom_call" | custom-call | flops 805306368 | bytes 4096 | tf_op jit(solution)/shard_map/pallas_call | solution.py:216
  (79 shorter events, 14.3 us)
Async XLA Ops:
  0.0 6.2 %collective-permute-start = (f32[1024,128]{1,0:T(8,128)}, f32[1024,128]{1,0:T(8,128)S(1)}, u32[]{:S(2)}, u32[]{:S(2)}) collective-permute-start(f32[1024,128]{1,0:T(8,128)} %near0.1), channel_id=1, source_target_pairs={{0,1},{1,0},{2,3},{3,2},{4,5},{5,4},{6,7},{7,6},{8,9},{9,8},{10,11... | collective-permute-start | bytes 1572872 | tf_op jit(solution)/shard_map/ppermute | solution.py:258
  0.5 5.7 %collective-permute-start.2 = (f32[1024,128]{1,0:T(8,128)}, f32[1024,128]{1,0:T(8,128)S(1)}, u32[]{:S(2)}, u32[]{:S(2)}) collective-permute-start(f32[1024,128]{1,0:T(8,128)} %v0.3), channel_id=1, source_target_pairs={{0,1},{1,0},{2,3},{3,2},{4,5},{5,4},{6,7},{7,6},{8,9},{9,8},{10,11... | collective-permute-start | bytes 1572872 | tf_op jit(solution)/shard_map/ppermute | solution.py:258
  0.5 16.8 %collective-permute-start.1 = (f32[1024,128]{1,0:T(8,128)}, f32[1024,128]{1,0:T(8,128)S(1)}, u32[]{:S(2)}, u32[]{:S(2)}) collective-permute-start(f32[1024,128]{1,0:T(8,128)} %near0.1), channel_id=1, source_target_pairs={{0,2},{1,3},{2,0},{3,1},{4,6},{5,7},{6,4},{7,5},{8,10},{9,11},{10,... | collective-permute-start | bytes 1572872 | tf_op jit(solution)/shard_map/ppermute | solution.py:258
  8.0 6.4 %collective-permute-start.3 = (f32[128,512]{1,0:T(8,128)S(1)}, f32[128,512]{1,0:T(8,128)S(1)}, u32[]{:S(2)}, u32[]{:S(2)}) collective-permute-start(f32[128,512]{1,0:T(8,128)S(1)} %get-tuple-element.51), channel_id=1, source_target_pairs={{0,4},{1,9},{2,6},{3,11},{4,0},{5,13},{6,2},{7,15},{8,12},{9,1},{1... | collective-permute-start | bytes 786440 | tf_op jit(solution)/shard_map/ppermute | solution.py:258
  9.6 7.7 %collective-permute-start.4 = (f32[128,512]{1,0:T(8,128)S(1)}, f32[128,512]{1,0:T(8,128)S(1)}, u32[]{:S(2)}, u32[]{:S(2)}) collective-permute-start(f32[128,512]{1,0:T(8,128)S(1)} %get-tuple-element.52), channel_id=1, source_target_pairs={{0,4},{1,9},{2,6},{3,11},{4,0},{5,13},{6,2},{7,15},{8,12},{9,1},{1... | collective-permute-start | bytes 786440 | tf_op jit(solution)/shard_map/ppermute | solution.py:258
  10.1 17.0 %collective-permute-start.11 = (f32[1024,128]{1,0:T(8,128)S(1)}, f32[1024,128]{1,0:T(8,128)S(1)}, u32[]{:S(2)}, u32[]{:S(2)}) collective-permute-start(f32[1024,128]{1,0:T(8,128)S(1)} %copy-done.2), channel_id=1, source_target_pairs={{0,2},{1,3},{2,0},{3,1},{4,6},{5,7},{6,4},{7,5},{8,10},{9,11},{10,... | collective-permute-start | bytes 1572872 | tf_op jit(solution)/shard_map/ppermute | solution.py:258
  17.4 7.0 %collective-permute-start.9 = (f32[128,512]{1,0:T(8,128)S(1)}, f32[128,512]{1,0:T(8,128)S(1)}, u32[]{:S(2)}, u32[]{:S(2)}) collective-permute-start(f32[128,512]{1,0:T(8,128)S(1)} %shard_map.58), channel_id=1, source_target_pairs={{0,8},{1,5},{2,10},{3,7},{4,12},{5,1},{6,14},{7,3},{8,0},{9,13},{1... | collective-permute-start | bytes 786440 | tf_op jit(solution)/shard_map/ppermute | solution.py:258
  22.3 5.7 %collective-permute-start.21 = (f32[192,256]{1,0:T(8,128)S(1)}, f32[192,256]{1,0:T(8,128)S(1)}, u32[]{:S(2)}, u32[]{:S(2)}) collective-permute-start(f32[192,256]{1,0:T(8,128)S(1)} %get-tuple-element.59), channel_id=1, source_target_pairs={{0,4},{1,9},{2,6},{3,11},{4,0},{5,13},{6,2},{7,15},{8,12},{9,1},{1... | collective-permute-start | bytes 589832 | tf_op jit(solution)/shard_map/ppermute | solution.py:258
  23.9 6.3 %collective-permute-start.22 = (f32[192,256]{1,0:T(8,128)S(1)}, f32[192,256]{1,0:T(8,128)S(1)}, u32[]{:S(2)}, u32[]{:S(2)}) collective-permute-start(f32[192,256]{1,0:T(8,128)S(1)} %get-tuple-element.60), channel_id=1, source_target_pairs={{0,4},{1,9},{2,6},{3,11},{4,0},{5,13},{6,2},{7,15},{8,12},{9,1},{1... | collective-permute-start | bytes 589832 | tf_op jit(solution)/shard_map/ppermute | solution.py:258
  24.5 14.5 %collective-permute-start.10 = (f32[128,512]{1,0:T(8,128)S(1)}, f32[128,512]{1,0:T(8,128)S(1)}, u32[]{:S(2)}, u32[]{:S(2)}) collective-permute-start(f32[128,512]{1,0:T(8,128)S(1)} %shard_map.61.refs_0_), channel_id=1, source_target_pairs={{0,16},{1,17},{2,18},{3,19},{4,20},{5,21},{6,22},{7,23},{8,24},{9,... | collective-permute-start | bytes 786440 | tf_op jit(solution)/shard_map/ppermute | solution.py:258
  27.2 8.0 %collective-permute-start.12 = (f32[256,128]{1,0:T(8,128)S(1)}, f32[256,128]{1,0:T(8,128)S(1)}, u32[]{:S(2)}, u32[]{:S(2)}) collective-permute-start(f32[256,128]{1,0:T(8,128)S(1)} %get-tuple-element.90), channel_id=1, source_target_pairs={{0,1},{1,0},{2,3},{3,2},{4,5},{5,4},{6,7},{7,6},{8,9},{9,8},{10,11... | collective-permute-start | bytes 393224 | tf_op jit(solution)/shard_map/ppermute | solution.py:258
  27.3 8.0 %collective-permute-start.13 = (f32[256,128]{1,0:T(8,128)S(1)}, f32[256,128]{1,0:T(8,128)S(1)}, u32[]{:S(2)}, u32[]{:S(2)}) collective-permute-start(f32[256,128]{1,0:T(8,128)S(1)} %get-tuple-element.89), channel_id=1, source_target_pairs={{0,1},{1,0},{2,3},{3,2},{4,5},{5,4},{6,7},{7,6},{8,9},{9,8},{10,11... | collective-permute-start | bytes 393224 | tf_op jit(solution)/shard_map/ppermute | solution.py:258
  28.1 7.2 %collective-permute-start.14 = (f32[256,128]{1,0:T(8,128)S(1)}, f32[256,128]{1,0:T(8,128)S(1)}, u32[]{:S(2)}, u32[]{:S(2)}) collective-permute-start(f32[256,128]{1,0:T(8,128)S(1)} %get-tuple-element.88), channel_id=1, source_target_pairs={{0,1},{1,0},{2,3},{3,2},{4,5},{5,4},{6,7},{7,6},{8,9},{9,8},{10,11... | collective-permute-start | bytes 393224 | tf_op jit(solution)/shard_map/ppermute | solution.py:258
  30.2 5.1 %collective-permute-start.15 = (f32[256,128]{1,0:T(8,128)S(1)}, f32[256,128]{1,0:T(8,128)S(1)}, u32[]{:S(2)}, u32[]{:S(2)}) collective-permute-start(f32[256,128]{1,0:T(8,128)S(1)} %get-tuple-element.87), channel_id=1, source_target_pairs={{0,1},{1,0},{2,3},{3,2},{4,5},{5,4},{6,7},{7,6},{8,9},{9,8},{10,11... | collective-permute-start | bytes 393224 | tf_op jit(solution)/shard_map/ppermute | solution.py:258
  35.2 5.9 %collective-permute-start.23 = (f32[192,256]{1,0:T(8,128)S(1)}, f32[192,256]{1,0:T(8,128)S(1)}, u32[]{:S(2)}, u32[]{:S(2)}) collective-permute-start(f32[192,256]{1,0:T(8,128)S(1)} %shard_map.68), channel_id=1, source_target_pairs={{0,8},{1,5},{2,10},{3,7},{4,12},{5,1},{6,14},{7,3},{8,0},{9,13},{1... | collective-permute-start | bytes 589832 | tf_op jit(solution)/shard_map/ppermute | solution.py:258
  39.0 5.8 %collective-permute-start.25 = (f32[128,512]{1,0:T(8,128)S(1)}, f32[128,512]{1,0:T(8,128)S(1)}, u32[]{:S(2)}, u32[]{:S(2)}) collective-permute-start(f32[128,512]{1,0:T(8,128)S(1)} %shard_map.63.refs_0_), channel_id=1, source_target_pairs={{0,1},{1,0},{2,3},{3,2},{4,5},{5,4},{6,7},{7,6},{8,9},{9,8},{10,11... | collective-permute-start | bytes 786440 | tf_op jit(solution)/shard_map/ppermute | solution.py:258
  41.1 11.7 %collective-permute-start.24 = (f32[192,256]{1,0:T(8,128)S(1)}, f32[192,256]{1,0:T(8,128)S(1)}, u32[]{:S(2)}, u32[]{:S(2)}) collective-permute-start(f32[192,256]{1,0:T(8,128)S(1)} %shard_map.69.refs_0_), channel_id=1, source_target_pairs={{0,16},{1,17},{2,18},{3,19},{4,20},{5,21},{6,22},{7,23},{8,24},{9,... | collective-permute-start | bytes 589832 | tf_op jit(solution)/shard_map/ppermute | solution.py:258
  42.7 5.4 %collective-permute-start.18 = (f32[128,256]{1,0:T(8,128)S(1)}, f32[128,256]{1,0:T(8,128)S(1)}, u32[]{:S(2)}, u32[]{:S(2)}) collective-permute-start(f32[128,256]{1,0:T(8,128)S(1)} %get-tuple-element.66), channel_id=1, source_target_pairs={{0,4},{1,9},{2,6},{3,11},{4,0},{5,13},{6,2},{7,15},{8,12},{9,1},{1... | collective-permute-start | bytes 393224 | tf_op jit(solution)/shard_map/ppermute | solution.py:258
  43.7 6.5 %collective-permute-start.19 = (f32[128,256]{1,0:T(8,128)S(1)}, f32[128,256]{1,0:T(8,128)S(1)}, u32[]{:S(2)}, u32[]{:S(2)}) collective-permute-start(f32[128,256]{1,0:T(8,128)S(1)} %get-tuple-element.65), channel_id=1, source_target_pairs={{0,4},{1,9},{2,6},{3,11},{4,0},{5,13},{6,2},{7,15},{8,12},{9,1},{1... | collective-permute-start | bytes 393224 | tf_op jit(solution)/shard_map/ppermute | solution.py:258
  44.8 8.0 %collective-permute-start.26 = (f32[64,512]{1,0:T(8,128)S(1)}, f32[64,512]{1,0:T(8,128)S(1)}, u32[]{:S(2)}, u32[]{:S(2)}) collective-permute-start(f32[64,512]{1,0:T(8,128)S(1)} %slice.8), channel_id=1, source_target_pairs={{0,1},{1,0},{2,3},{3,2},{4,5},{5,4},{6,7},{7,6},{8,9},{9,8},{10,11... | collective-permute-start | bytes 393224 | tf_op jit(solution)/shard_map/ppermute | solution.py:258
  44.9 12.1 %collective-permute-start.16 = (f32[128,512]{1,0:T(8,128)S(1)}, f32[128,512]{1,0:T(8,128)S(1)}, u32[]{:S(2)}, u32[]{:S(2)}) collective-permute-start(f32[128,512]{1,0:T(8,128)S(1)} %shard_map.63.refs_0_), channel_id=1, source_target_pairs={{0,8},{1,5},{2,10},{3,7},{4,12},{5,1},{6,14},{7,3},{8,0},{9,13},{1... | collective-permute-start | bytes 786440 | tf_op jit(solution)/shard_map/ppermute | solution.py:258
  50.2 6.7 %collective-permute-start.28 = (f32[128,256]{1,0:T(8,128)S(1)}, f32[128,256]{1,0:T(8,128)S(1)}, u32[]{:S(2)}, u32[]{:S(2)}) collective-permute-start(f32[128,256]{1,0:T(8,128)S(1)} %shard_map.64), channel_id=1, source_target_pairs={{0,8},{1,5},{2,10},{3,7},{4,12},{5,1},{6,14},{7,3},{8,0},{9,13},{1... | collective-permute-start | bytes 393224 | tf_op jit(solution)/shard_map/ppermute | solution.py:258
  52.8 5.2 %collective-permute-start.27 = (f32[64,256]{1,0:T(8,128)S(1)}, f32[64,256]{1,0:T(8,128)S(1)}, u32[]{:S(2)}, u32[]{:S(2)}) collective-permute-start(f32[64,256]{1,0:T(8,128)S(1)} %slice.9), channel_id=1, source_target_pairs={{0,2},{1,3},{2,0},{3,1},{4,6},{5,7},{6,4},{7,5},{8,10},{9,11},{10,... | collective-permute-start | bytes 196616 | tf_op jit(solution)/shard_map/ppermute | solution.py:258
  55.9 8.6 %collective-permute-start.17 = (f32[128,512]{1,0:T(8,128)S(1)}, f32[128,512]{1,0:T(8,128)S(1)}, u32[]{:S(2)}, u32[]{:S(2)}) collective-permute-start(f32[128,512]{1,0:T(8,128)S(1)} %shard_map.63.refs_0_), channel_id=1, source_target_pairs={{0,4},{1,9},{2,6},{3,11},{4,0},{5,13},{6,2},{7,15},{8,12},{9,1},{1... | collective-permute-start | bytes 786440 | tf_op jit(solution)/shard_map/ppermute | solution.py:258
  57.0 10.3 %collective-permute-start.20 = (f32[128,512]{1,0:T(8,128)S(1)}, f32[128,512]{1,0:T(8,128)S(1)}, u32[]{:S(2)}, u32[]{:S(2)}) collective-permute-start(f32[128,512]{1,0:T(8,128)S(1)} %collective-permute-done.16.refs_1_), channel_id=1, source_target_pairs={{0,4},{1,9},{2,6},{3,11},{4,0},{5,13},{6,2},{7,15},{8,12},{9,1},{1... | collective-permute-start | bytes 786440 | tf_op jit(solution)/shard_map/ppermute | solution.py:258
  58.1 11.3 %collective-permute-start.29 = (f32[256,256]{1,0:T(8,128)S(1)}, f32[256,256]{1,0:T(8,128)S(1)}, u32[]{:S(2)}, u32[]{:S(2)}) collective-permute-start(f32[256,256]{1,0:T(8,128)S(1)} %shard_map.72.refs_0_.refs_4_), channel_id=1, source_target_pairs={{0,8},{1,5},{2,10},{3,7},{4,12},{5,1},{6,14},{7,3},{8,0},{9,13},{1... | collective-permute-start | bytes 786440 | tf_op jit(solution)/shard_map/ppermute | solution.py:258
  58.9 11.1 %collective-permute-start.32 = (f32[128,256]{1,0:T(8,128)S(1)}, f32[128,256]{1,0:T(8,128)S(1)}, u32[]{:S(2)}, u32[]{:S(2)}) collective-permute-start(f32[128,256]{1,0:T(8,128)S(1)} %shard_map.71.refs_0_), channel_id=1, source_target_pairs={{0,16},{1,17},{2,18},{3,19},{4,20},{5,21},{6,22},{7,23},{8,24},{9,... | collective-permute-start | bytes 393224 | tf_op jit(solution)/shard_map/ppermute | solution.py:258
  59.4 16.0 %collective-permute-start.30 = (f32[256,256]{1,0:T(8,128)S(1)}, f32[256,256]{1,0:T(8,128)S(1)}, u32[]{:S(2)}, u32[]{:S(2)}) collective-permute-start(f32[256,256]{1,0:T(8,128)S(1)} %shard_map.72.refs_0_.refs_4_), channel_id=1, source_target_pairs={{0,4},{1,9},{2,6},{3,11},{4,0},{5,13},{6,2},{7,15},{8,12},{9,1},{1... | collective-permute-start | bytes 786440 | tf_op jit(solution)/shard_map/ppermute | solution.py:258
  69.4 6.4 %collective-permute-start.31 = (f32[256,256]{1,0:T(8,128)S(1)}, f32[256,256]{1,0:T(8,128)S(1)}, u32[]{:S(2)}, u32[]{:S(2)}) collective-permute-start(f32[256,256]{1,0:T(8,128)S(1)} %collective-permute-done.29.refs_1_.refs_5_), channel_id=1, source_target_pairs={{0,4},{1,9},{2,6},{3,11},{4,0},{5,13},{6,2},{7,15},{8,12},{9,1},{1... | collective-permute-start | bytes 786440 | tf_op jit(solution)/shard_map/ppermute | solution.py:258
  70.1 5.3 %collective-permute-start.33 = (f32[128,256]{1,0:T(8,128)S(1)}, f32[128,256]{1,0:T(8,128)S(1)}, u32[]{:S(2)}, u32[]{:S(2)}) collective-permute-start(f32[128,256]{1,0:T(8,128)S(1)} %shard_map.73.b0), channel_id=1, source_target_pairs={{0,8},{1,5},{2,10},{3,7},{4,12},{5,1},{6,14},{7,3},{8,0},{9,13},{1... | collective-permute-start | bytes 393224 | tf_op jit(solution)/shard_map/ppermute | solution.py:258
  76.4 5.2 %collective-permute-start.35 = (f32[128,256]{1,0:T(8,128)S(1)}, f32[128,256]{1,0:T(8,128)S(1)}, u32[]{:S(2)}, u32[]{:S(2)}) collective-permute-start(f32[128,256]{1,0:T(8,128)S(1)} %shard_map.73.b0), channel_id=1, source_target_pairs={{0,4},{1,9},{2,6},{3,11},{4,0},{5,13},{6,2},{7,15},{8,12},{9,1},{1... | collective-permute-start | bytes 393224 | tf_op jit(solution)/shard_map/ppermute | solution.py:258
  77.5 5.3 %collective-permute-start.36 = (f32[128,256]{1,0:T(8,128)S(1)}, f32[128,256]{1,0:T(8,128)S(1)}, u32[]{:S(2)}, u32[]{:S(2)}) collective-permute-start(f32[128,256]{1,0:T(8,128)S(1)} %collective-permute-done.33.b1), channel_id=1, source_target_pairs={{0,4},{1,9},{2,6},{3,11},{4,0},{5,13},{6,2},{7,15},{8,12},{9,1},{1... | collective-permute-start | bytes 393224 | tf_op jit(solution)/shard_map/ppermute | solution.py:258
  (10 other events, 61.3 us)

commit v4 on v3

--- a/solution.py
+++ b/solution.py
@@ -335,7 +335,7 @@
     factor = functools.partial(call, factor_kernel, [((rows, total), bf16)] * 2)
     t1 = arrange((place, factor_first), rows * total // 2)
     t2 = arrange((place, factor_second), rows * total // 2)
-    w2 = factor((*t2, *second), rows * total * total)
+    w2 = factor((*after(t2, second_other), *second), rows * total * total)
     w1 = factor((*t1, *first), rows * total * total)
     first_got = to_one(first_parts[2])
     first_other = add(first_parts[1], to_one(first_parts[3]), pads=(first_got,))

time: 85.6 us -> 85.6 us (level)
  no operation moved by 1% of the time
where the time goes in v4:
time: 85.6 us; the launch traced here: 85.5 us
  starting transfers between devices  35 us (41%)
  waiting for transfers between devices  29.6 us (35%)
  Pallas kernels  20.4 us (24%)
    ppermute x37, starting transfers between devices, permute(): return lax.ppermute(value, ('row', 'col'), pairs)  35 us
    ppermute x37, waiting for transfers between devices, permute(): return lax.ppermute(value, ('row', 'col'), pairs)  29.6 us
    pallas_call x22, Pallas kernels, call(): pl.pallas_call(kernel, out_shape=tuple((jax.ShapeDtypeStruct(shape, dtype...  20.4 us
  transfers between devices with their start and end apart: 37, of which 15 were waited for; matrix products, arithmetic and copies ran while one was open for 0% of the time, Pallas kernels for 20%

profile of v4, /device:TPU:0, one launch (start us, length us, event | category | flops | bytes accessed | tf_op | source)
XLA Modules:
  0.0 85.5 jit_solution(15198174562528591908)
XLA Ops:
  0.5 3.0 %collective-permute-start.1 = (f32[1024,128]{1,0:T(8,128)}, f32[1024,128]{1,0:T(8,128)S(1)}, u32[]{:S(2)}, u32[]{:S(2)}) collective-permute-start(f32[1024,128]{1,0:T(8,128)} %v0.2), channel_id=1, source_target_pairs={{0,2},{1,3},{2,0},{3,1},{4,6},{5,7},{6,4},{7,5},{8,10},{9,11},{10,... | collective-permute-start | bytes 1572872 | tf_op jit(solution)/shard_map/ppermute | solution.py:258
  3.6 2.6 %shard_map.56 = (bf16[640,1024]{1,0:T(8,128)(2,1)S(1)}, bf16[640,1024]{1,0:T(8,128)(2,1)S(1)}) custom-call(s32[5]{0:T(128)S(1)} %stack.23.place, f32[1024,512]{1,0:T(8,128)} %x.3, f32[1024,128]{1,0:T(8,128)} %v0.3), custom_call_target="tpu_custom_call" | custom-call | bytes 4096 | tf_op jit(solution)/shard_map/pallas_call | solution.py:216
  6.2 1.8 %shard_map.57 = (f32[128,512]{1,0:T(8,128)S(1)}, f32[128,512]{1,0:T(8,128)S(1)}, f32[128,512]{1,0:T(8,128)S(1)}, f32[128,512]{1,0:T(8,128)S(1)}) custom-call(bf16[640,1024]{1,0:T(8,128)(2,1)S(1)} %get-tuple-element.50.lt_high, bf16[640,1024]{1,0:T(8,128)(2,1)S(1)} %get-tuple-element.51.lt_low, f32[1024,128]{1,0:T(8,128)S(1)} %copy-done.1, ...), custom_call_target="tpu_custom_call" | custom-call | bytes 4096 | tf_op jit(solution)/shard_map/pallas_call | solution.py:216
  8.0 1.6 %collective-permute-start.3 = (f32[128,512]{1,0:T(8,128)S(1)}, f32[128,512]{1,0:T(8,128)S(1)}, u32[]{:S(2)}, u32[]{:S(2)}) collective-permute-start(f32[128,512]{1,0:T(8,128)S(1)} %get-tuple-element.53), channel_id=1, source_target_pairs={{0,4},{1,9},{2,6},{3,11},{4,0},{5,13},{6,2},{7,15},{8,12},{9,1},{1... | collective-permute-start | bytes 786440 | tf_op jit(solution)/shard_map/ppermute | solution.py:258
  10.2 4.3 %collective-permute-done.3.refs_1_ = f32[128,512]{1,0:T(8,128)S(1)} collective-permute-done((f32[128,512]{1,0:T(8,128)S(1)}, f32[128,512]{1,0:T(8,128)S(1)}, u32[]{:S(2)}, u32[]{:S(2)}) %collective-permute-start.3) | collective-permute-done | bytes 262176 | tf_op jit(solution)/shard_map/ppermute | solution.py:258
  14.5 2.8 %collective-permute-done.4.refs_2_.refs_1_ = f32[128,512]{1,0:T(8,128)S(1)} collective-permute-done((f32[128,512]{1,0:T(8,128)S(1)}, f32[128,512]{1,0:T(8,128)S(1)}, u32[]{:S(2)}, u32[]{:S(2)}) %collective-permute-start.4) | collective-permute-done | bytes 262176 | tf_op jit(solution)/shard_map/ppermute | solution.py:258
  17.4 1.6 %collective-permute-start.11 = (f32[128,512]{1,0:T(8,128)S(1)}, f32[128,512]{1,0:T(8,128)S(1)}, u32[]{:S(2)}, u32[]{:S(2)}) collective-permute-start(f32[128,512]{1,0:T(8,128)S(1)} %shard_map.58), channel_id=1, source_target_pairs={{0,8},{1,5},{2,10},{3,7},{4,12},{5,1},{6,14},{7,3},{8,0},{9,13},{1... | collective-permute-start | bytes 786440 | tf_op jit(solution)/shard_map/ppermute | solution.py:258
  21.0 1.4 %shard_map.59 = (f32[192,256]{1,0:T(8,128)S(1)}, f32[192,256]{1,0:T(8,128)S(1)}, f32[192,256]{1,0:T(8,128)S(1)}, f32[192,256]{1,0:T(8,128)S(1)}) custom-call(bf16[640,1024]{1,0:T(8,128)(2,1)S(1)} %get-tuple-element.50.lt_high, bf16[640,1024]{1,0:T(8,128)(2,1)S(1)} %get-tuple-element.51.lt_low, f32[1024,128]{1,0:T(8,128)S(1)} %copy-done.1, ...), custom_call_target="tpu_custom_call" | custom-call | bytes 4096 | tf_op jit(solution)/shard_map/pallas_call | solution.py:216
  22.4 1.6 %collective-permute-start.10 = (f32[192,256]{1,0:T(8,128)S(1)}, f32[192,256]{1,0:T(8,128)S(1)}, u32[]{:S(2)}, u32[]{:S(2)}) collective-permute-start(f32[192,256]{1,0:T(8,128)S(1)} %get-tuple-element.58), channel_id=1, source_target_pairs={{0,4},{1,9},{2,6},{3,11},{4,0},{5,13},{6,2},{7,15},{8,12},{9,1},{1... | collective-permute-start | bytes 589832 | tf_op jit(solution)/shard_map/ppermute | solution.py:258
  24.5 2.7 %collective-permute-start.12 = (f32[128,512]{1,0:T(8,128)S(1)}, f32[128,512]{1,0:T(8,128)S(1)}, u32[]{:S(2)}, u32[]{:S(2)}) collective-permute-start(f32[128,512]{1,0:T(8,128)S(1)} %shard_map.62.refs_0_), channel_id=1, source_target_pairs={{0,16},{1,17},{2,18},{3,19},{4,20},{5,21},{6,22},{7,23},{8,24},{9,... | collective-permute-start | bytes 786440 | tf_op jit(solution)/shard_map/ppermute | solution.py:258
  28.1 2.1 %collective-permute-done.9.refs_1_ = f32[192,256]{1,0:T(8,128)S(1)} collective-permute-done((f32[192,256]{1,0:T(8,128)S(1)}, f32[192,256]{1,0:T(8,128)S(1)}, u32[]{:S(2)}, u32[]{:S(2)}) %collective-permute-start.9) | collective-permute-done | bytes 196640 | tf_op jit(solution)/shard_map/ppermute | solution.py:258
  30.2 3.1 %collective-permute-start.17 = (f32[256,128]{1,0:T(8,128)S(1)}, f32[256,128]{1,0:T(8,128)S(1)}, u32[]{:S(2)}, u32[]{:S(2)}) collective-permute-start(f32[256,128]{1,0:T(8,128)S(1)} %get-tuple-element.91), channel_id=1, source_target_pairs={{0,1},{1,0},{2,3},{3,2},{4,5},{5,4},{6,7},{7,6},{8,9},{9,8},{10,11... | collective-permute-start | bytes 393224 | tf_op jit(solution)/shard_map/ppermute | solution.py:258
  33.4 1.8 %shard_map.61 = (bf16[1024,512]{1,0:T(8,128)(2,1)S(1)}, bf16[1024,512]{1,0:T(8,128)(2,1)S(1)}) custom-call(bf16[512,512]{1,0:T(8,128)(2,1)S(1)} %get-tuple-element.59.t_high, bf16[512,512]{1,0:T(8,128)(2,1)S(1)} %get-tuple-element.60.t_low, f32[1024,128]{1,0:T(8,128)S(1)} %copy-done.1, f32[1024,128]{1,0:T(8,128)S(1)} %collective-permute-done.refs_1_.near1.v1, ...), custom_call_target="tpu_custom_call" | custom-call | flops 1610612736 | bytes 4096 | tf_op jit(solution)/shard_map/pallas_call | solution.py:216
  36.3 2.6 %collective-permute-done.12.refs_1_ = f32[128,512]{1,0:T(8,128)S(1)} collective-permute-done((f32[128,512]{1,0:T(8,128)S(1)}, f32[128,512]{1,0:T(8,128)S(1)}, u32[]{:S(2)}, u32[]{:S(2)}) %collective-permute-start.12) | collective-permute-done | bytes 262176 | tf_op jit(solution)/shard_map/ppermute | solution.py:258
  39.1 2.0 %collective-permute-done.23.refs_2_ = f32[192,256]{1,0:T(8,128)S(1)} collective-permute-done((f32[192,256]{1,0:T(8,128)S(1)}, f32[192,256]{1,0:T(8,128)S(1)}, u32[]{:S(2)}, u32[]{:S(2)}) %collective-permute-start.23) | collective-permute-done | bytes 196640 | tf_op jit(solution)/shard_map/ppermute | solution.py:258
  41.1 1.6 %collective-permute-start.24 = (f32[192,256]{1,0:T(8,128)S(1)}, f32[192,256]{1,0:T(8,128)S(1)}, u32[]{:S(2)}, u32[]{:S(2)}) collective-permute-start(f32[192,256]{1,0:T(8,128)S(1)} %shard_map.69.refs_0_), channel_id=1, source_target_pairs={{0,16},{1,17},{2,18},{3,19},{4,20},{5,21},{6,22},{7,23},{8,24},{9,... | collective-permute-start | bytes 589832 | tf_op jit(solution)/shard_map/ppermute | solution.py:258
  44.9 2.5 %collective-permute-start.18 = (f32[128,512]{1,0:T(8,128)S(1)}, f32[128,512]{1,0:T(8,128)S(1)}, u32[]{:S(2)}, u32[]{:S(2)}) collective-permute-start(f32[128,512]{1,0:T(8,128)S(1)} %shard_map.64.refs_0_), channel_id=1, source_target_pairs={{0,8},{1,5},{2,10},{3,7},{4,12},{5,1},{6,14},{7,3},{8,0},{9,13},{1... | collective-permute-start | bytes 786440 | tf_op jit(solution)/shard_map/ppermute | solution.py:258
  48.1 2.1 %collective-permute-done.21.refs_2_.refs_1_ = f32[128,256]{1,0:T(8,128)S(1)} collective-permute-done((f32[128,256]{1,0:T(8,128)S(1)}, f32[128,256]{1,0:T(8,128)S(1)}, u32[]{:S(2)}, u32[]{:S(2)}) %collective-permute-start.21) | collective-permute-done | bytes 131104 | tf_op jit(solution)/shard_map/ppermute | solution.py:258
  50.2 2.5 %collective-permute-start.28 = (f32[128,256]{1,0:T(8,128)S(1)}, f32[128,256]{1,0:T(8,128)S(1)}, u32[]{:S(2)}, u32[]{:S(2)}) collective-permute-start(f32[128,256]{1,0:T(8,128)S(1)} %shard_map.65), channel_id=1, source_target_pairs={{0,8},{1,5},{2,10},{3,7},{4,12},{5,1},{6,14},{7,3},{8,0},{9,13},{1... | collective-permute-start | bytes 393224 | tf_op jit(solution)/shard_map/ppermute | solution.py:258
  52.8 1.2 %collective-permute-start.27 = (f32[64,256]{1,0:T(8,128)S(1)}, f32[64,256]{1,0:T(8,128)S(1)}, u32[]{:S(2)}, u32[]{:S(2)}) collective-permute-start(f32[64,256]{1,0:T(8,128)S(1)} %slice.9), channel_id=1, source_target_pairs={{0,2},{1,3},{2,0},{3,1},{4,6},{5,7},{6,4},{7,5},{8,10},{9,11},{10,... | collective-permute-start | bytes 196616 | tf_op jit(solution)/shard_map/ppermute | solution.py:258
  54.0 1.8 %shard_map.68 = (bf16[1024,512]{1,0:T(8,128)(2,1)S(1)}, bf16[1024,512]{1,0:T(8,128)(2,1)S(1)}) custom-call(bf16[512,512]{1,0:T(8,128)(2,1)S(1)} %get-tuple-element.74.t_high, bf16[512,512]{1,0:T(8,128)(2,1)S(1)} %get-tuple-element.75.t_low, f32[1024,128]{1,0:T(8,128)S(1)} %copy-done.2, f32[1024,128]{1,0:T(8,128)S(1)} %collective-permute-done.2.refs_3_.v1, ...), custom_call_target="tpu_custom_call" | custom-call | flops 1610612736 | bytes 4096 | tf_op jit(solution)/shard_map/pallas_call | solution.py:216
  57.0 1.1 %collective-permute-start.22 = (f32[128,512]{1,0:T(8,128)S(1)}, f32[128,512]{1,0:T(8,128)S(1)}, u32[]{:S(2)}, u32[]{:S(2)}) collective-permute-start(f32[128,512]{1,0:T(8,128)S(1)} %collective-permute-done.18.refs_1_), channel_id=1, source_target_pairs={{0,4},{1,9},{2,6},{3,11},{4,0},{5,13},{6,2},{7,15},{8,12},{9,1},{1... | collective-permute-start | bytes 786440 | tf_op jit(solution)/shard_map/ppermute | solution.py:258
  59.5 1.7 %collective-permute-start.30 = (f32[256,256]{1,0:T(8,128)S(1)}, f32[256,256]{1,0:T(8,128)S(1)}, u32[]{:S(2)}, u32[]{:S(2)}) collective-permute-start(f32[256,256]{1,0:T(8,128)S(1)} %shard_map.72.refs_0_.refs_4_), channel_id=1, source_target_pairs={{0,4},{1,9},{2,6},{3,11},{4,0},{5,13},{6,2},{7,15},{8,12},{9,1},{1... | collective-permute-start | bytes 786440 | tf_op jit(solution)/shard_map/ppermute | solution.py:258
  61.2 3.3 %collective-permute-done.19.refs_2_ = f32[128,512]{1,0:T(8,128)S(1)} collective-permute-done((f32[128,512]{1,0:T(8,128)S(1)}, f32[128,512]{1,0:T(8,128)S(1)}, u32[]{:S(2)}, u32[]{:S(2)}) %collective-permute-start.19) | collective-permute-done | bytes 262176 | tf_op jit(solution)/shard_map/ppermute | solution.py:258
  64.4 2.8 %collective-permute-done.22.refs_3_ = f32[128,512]{1,0:T(8,128)S(1)} collective-permute-done((f32[128,512]{1,0:T(8,128)S(1)}, f32[128,512]{1,0:T(8,128)S(1)}, u32[]{:S(2)}, u32[]{:S(2)}) %collective-permute-start.22) | collective-permute-done | bytes 262176 | tf_op jit(solution)/shard_map/ppermute | solution.py:258
  67.3 2.1 %collective-permute-done.29.refs_1_.refs_5_ = f32[256,256]{1,0:T(8,128)S(1)} collective-permute-done((f32[256,256]{1,0:T(8,128)S(1)}, f32[256,256]{1,0:T(8,128)S(1)}, u32[]{:S(2)}, u32[]{:S(2)}) %collective-permute-start.29) | collective-permute-done | bytes 262176 | tf_op jit(solution)/shard_map/ppermute | solution.py:258
  70.4 2.0 %shard_map.66 = (f32[1024,512]{1,0:T(8,128)S(1)}, f32[512,512]{1,0:T(8,128)S(1)}) custom-call(s32[5]{0:T(128)S(1)} %stack.23.place, f32[1024,512]{1,0:T(8,128)S(1)} %copy-done, bf16[512,512]{1,0:T(8,128)(2,1)S(1)} %get-tuple-element.59.t_high, bf16[512,512]{1,0:T(8,128)(2,1)S(1)} %get-tuple-element.60.t_low, ...), custom_call_target="tpu_custom_call" | custom-call | flops 1207959552 | bytes 4096 | tf_op jit(solution)/shard_map/pallas_call | solution.py:216
  72.4 3.0 %collective-permute-done.33.b1 = f32[128,256]{1,0:T(8,128)S(1)} collective-permute-done((f32[128,256]{1,0:T(8,128)S(1)}, f32[128,256]{1,0:T(8,128)S(1)}, u32[]{:S(2)}, u32[]{:S(2)}) %collective-permute-start.33) | collective-permute-done | bytes 131104 | tf_op jit(solution)/shard_map/ppermute | solution.py:258
  76.4 1.1 %collective-permute-start.35 = (f32[128,256]{1,0:T(8,128)S(1)}, f32[128,256]{1,0:T(8,128)S(1)}, u32[]{:S(2)}, u32[]{:S(2)}) collective-permute-start(f32[128,256]{1,0:T(8,128)S(1)} %shard_map.73.b0), channel_id=1, source_target_pairs={{0,4},{1,9},{2,6},{3,11},{4,0},{5,13},{6,2},{7,15},{8,12},{9,1},{1... | collective-permute-start | bytes 393224 | tf_op jit(solution)/shard_map/ppermute | solution.py:258
  78.5 3.1 %shard_map.75 = (f32[1024,512]{1,0:T(8,128)S(1)}, f32[512,256]{1,0:T(8,128)S(1)}) custom-call(f32[1024,512]{1,0:T(8,128)S(1)} %get-tuple-element.73.x, bf16[512,512]{1,0:T(8,128)(2,1)S(1)} %get-tuple-element.59.t_high, bf16[512,512]{1,0:T(8,128)(2,1)S(1)} %get-tuple-element.60.t_low, bf16[1024,512]{1,0:T(8,128)(2,1)S(1)} %get-tuple-element.61.w_high.w2_high, ...), custom_call_target="tpu_custom_call" | custom-call | flops 2415919104 | bytes 4096 | tf_op jit(solution)/shard_map/pallas_call | solution.py:216
  81.6 1.3 %collective-permute-done.36.b3 = f32[128,256]{1,0:T(8,128)S(1)} collective-permute-done((f32[128,256]{1,0:T(8,128)S(1)}, f32[128,256]{1,0:T(8,128)S(1)}, u32[]{:S(2)}, u32[]{:S(2)}) %collective-permute-start.36) | collective-permute-done | bytes 131104 | tf_op jit(solution)/shard_map/ppermute | solution.py:258
  82.8 2.7 %shard_map.76 = f32[1024,512]{1,0:T(8,128)} custom-call(s32[5]{0:T(128)S(1)} %stack.23.place, f32[1024,512]{1,0:T(8,128)S(1)} %get-tuple-element.89.x, bf16[1024,512]{1,0:T(8,128)(2,1)S(1)} %get-tuple-element.76.w1_high.w_high, bf16[1024,512]{1,0:T(8,128)(2,1)S(1)} %get-tuple-element.77.w1_low.w_low, f32[512,256]{1,0:T(8,128)S(1)} %get-tuple-element.90.rest, ...), custom_call_target="tpu_custom_call" | custom-call | flops 805306368 | bytes 4096 | tf_op jit(solution)/shard_map/pallas_call | solution.py:216
  (79 shorter events, 14.3 us)
Async XLA Ops:
  0.0 6.2 %collective-permute-start = (f32[1024,128]{1,0:T(8,128)}, f32[1024,128]{1,0:T(8,128)S(1)}, u32[]{:S(2)}, u32[]{:S(2)}) collective-permute-start(f32[1024,128]{1,0:T(8,128)} %v0.2), channel_id=1, source_target_pairs={{0,1},{1,0},{2,3},{3,2},{4,5},{5,4},{6,7},{7,6},{8,9},{9,8},{10,11... | collective-permute-start | bytes 1572872 | tf_op jit(solution)/shard_map/ppermute | solution.py:258
  0.5 5.7 %collective-permute-start.2 = (f32[1024,128]{1,0:T(8,128)}, f32[1024,128]{1,0:T(8,128)S(1)}, u32[]{:S(2)}, u32[]{:S(2)}) collective-permute-start(f32[1024,128]{1,0:T(8,128)} %v0.3), channel_id=1, source_target_pairs={{0,1},{1,0},{2,3},{3,2},{4,5},{5,4},{6,7},{7,6},{8,9},{9,8},{10,11... | collective-permute-start | bytes 1572872 | tf_op jit(solution)/shard_map/ppermute | solution.py:258
  0.5 16.8 %collective-permute-start.1 = (f32[1024,128]{1,0:T(8,128)}, f32[1024,128]{1,0:T(8,128)S(1)}, u32[]{:S(2)}, u32[]{:S(2)}) collective-permute-start(f32[1024,128]{1,0:T(8,128)} %v0.2), channel_id=1, source_target_pairs={{0,2},{1,3},{2,0},{3,1},{4,6},{5,7},{6,4},{7,5},{8,10},{9,11},{10,... | collective-permute-start | bytes 1572872 | tf_op jit(solution)/shard_map/ppermute | solution.py:258
  8.0 6.4 %collective-permute-start.3 = (f32[128,512]{1,0:T(8,128)S(1)}, f32[128,512]{1,0:T(8,128)S(1)}, u32[]{:S(2)}, u32[]{:S(2)}) collective-permute-start(f32[128,512]{1,0:T(8,128)S(1)} %get-tuple-element.53), channel_id=1, source_target_pairs={{0,4},{1,9},{2,6},{3,11},{4,0},{5,13},{6,2},{7,15},{8,12},{9,1},{1... | collective-permute-start | bytes 786440 | tf_op jit(solution)/shard_map/ppermute | solution.py:258
  9.6 7.7 %collective-permute-start.4 = (f32[128,512]{1,0:T(8,128)S(1)}, f32[128,512]{1,0:T(8,128)S(1)}, u32[]{:S(2)}, u32[]{:S(2)}) collective-permute-start(f32[128,512]{1,0:T(8,128)S(1)} %get-tuple-element.54), channel_id=1, source_target_pairs={{0,4},{1,9},{2,6},{3,11},{4,0},{5,13},{6,2},{7,15},{8,12},{9,1},{1... | collective-permute-start | bytes 786440 | tf_op jit(solution)/shard_map/ppermute | solution.py:258
  10.1 17.0 %collective-permute-start.13 = (f32[1024,128]{1,0:T(8,128)S(1)}, f32[1024,128]{1,0:T(8,128)S(1)}, u32[]{:S(2)}, u32[]{:S(2)}) collective-permute-start(f32[1024,128]{1,0:T(8,128)S(1)} %copy-done.2), channel_id=1, source_target_pairs={{0,2},{1,3},{2,0},{3,1},{4,6},{5,7},{6,4},{7,5},{8,10},{9,11},{10,... | collective-permute-start | bytes 1572872 | tf_op jit(solution)/shard_map/ppermute | solution.py:258
  17.4 7.0 %collective-permute-start.11 = (f32[128,512]{1,0:T(8,128)S(1)}, f32[128,512]{1,0:T(8,128)S(1)}, u32[]{:S(2)}, u32[]{:S(2)}) collective-permute-start(f32[128,512]{1,0:T(8,128)S(1)} %shard_map.58), channel_id=1, source_target_pairs={{0,8},{1,5},{2,10},{3,7},{4,12},{5,1},{6,14},{7,3},{8,0},{9,13},{1... | collective-permute-start | bytes 786440 | tf_op jit(solution)/shard_map/ppermute | solution.py:258
  22.4 5.7 %collective-permute-start.10 = (f32[192,256]{1,0:T(8,128)S(1)}, f32[192,256]{1,0:T(8,128)S(1)}, u32[]{:S(2)}, u32[]{:S(2)}) collective-permute-start(f32[192,256]{1,0:T(8,128)S(1)} %get-tuple-element.58), channel_id=1, source_target_pairs={{0,4},{1,9},{2,6},{3,11},{4,0},{5,13},{6,2},{7,15},{8,12},{9,1},{1... | collective-permute-start | bytes 589832 | tf_op jit(solution)/shard_map/ppermute | solution.py:258
  23.9 6.3 %collective-permute-start.9 = (f32[192,256]{1,0:T(8,128)S(1)}, f32[192,256]{1,0:T(8,128)S(1)}, u32[]{:S(2)}, u32[]{:S(2)}) collective-permute-start(f32[192,256]{1,0:T(8,128)S(1)} %get-tuple-element.57), channel_id=1, source_target_pairs={{0,4},{1,9},{2,6},{3,11},{4,0},{5,13},{6,2},{7,15},{8,12},{9,1},{1... | collective-permute-start | bytes 589832 | tf_op jit(solution)/shard_map/ppermute | solution.py:258
  24.5 14.5 %collective-permute-start.12 = (f32[128,512]{1,0:T(8,128)S(1)}, f32[128,512]{1,0:T(8,128)S(1)}, u32[]{:S(2)}, u32[]{:S(2)}) collective-permute-start(f32[128,512]{1,0:T(8,128)S(1)} %shard_map.62.refs_0_), channel_id=1, source_target_pairs={{0,16},{1,17},{2,18},{3,19},{4,20},{5,21},{6,22},{7,23},{8,24},{9,... | collective-permute-start | bytes 786440 | tf_op jit(solution)/shard_map/ppermute | solution.py:258
  27.2 8.0 %collective-permute-start.14 = (f32[256,128]{1,0:T(8,128)S(1)}, f32[256,128]{1,0:T(8,128)S(1)}, u32[]{:S(2)}, u32[]{:S(2)}) collective-permute-start(f32[256,128]{1,0:T(8,128)S(1)} %get-tuple-element.94), channel_id=1, source_target_pairs={{0,1},{1,0},{2,3},{3,2},{4,5},{5,4},{6,7},{7,6},{8,9},{9,8},{10,11... | collective-permute-start | bytes 393224 | tf_op jit(solution)/shard_map/ppermute | solution.py:258
  27.3 8.0 %collective-permute-start.15 = (f32[256,128]{1,0:T(8,128)S(1)}, f32[256,128]{1,0:T(8,128)S(1)}, u32[]{:S(2)}, u32[]{:S(2)}) collective-permute-start(f32[256,128]{1,0:T(8,128)S(1)} %get-tuple-element.93), channel_id=1, source_target_pairs={{0,1},{1,0},{2,3},{3,2},{4,5},{5,4},{6,7},{7,6},{8,9},{9,8},{10,11... | collective-permute-start | bytes 393224 | tf_op jit(solution)/shard_map/ppermute | solution.py:258
  28.1 7.2 %collective-permute-start.16 = (f32[256,128]{1,0:T(8,128)S(1)}, f32[256,128]{1,0:T(8,128)S(1)}, u32[]{:S(2)}, u32[]{:S(2)}) collective-permute-start(f32[256,128]{1,0:T(8,128)S(1)} %get-tuple-element.92), channel_id=1, source_target_pairs={{0,1},{1,0},{2,3},{3,2},{4,5},{5,4},{6,7},{7,6},{8,9},{9,8},{10,11... | collective-permute-start | bytes 393224 | tf_op jit(solution)/shard_map/ppermute | solution.py:258
  30.2 5.1 %collective-permute-start.17 = (f32[256,128]{1,0:T(8,128)S(1)}, f32[256,128]{1,0:T(8,128)S(1)}, u32[]{:S(2)}, u32[]{:S(2)}) collective-permute-start(f32[256,128]{1,0:T(8,128)S(1)} %get-tuple-element.91), channel_id=1, source_target_pairs={{0,1},{1,0},{2,3},{3,2},{4,5},{5,4},{6,7},{7,6},{8,9},{9,8},{10,11... | collective-permute-start | bytes 393224 | tf_op jit(solution)/shard_map/ppermute | solution.py:258
  35.2 5.8 %collective-permute-start.23 = (f32[192,256]{1,0:T(8,128)S(1)}, f32[192,256]{1,0:T(8,128)S(1)}, u32[]{:S(2)}, u32[]{:S(2)}) collective-permute-start(f32[192,256]{1,0:T(8,128)S(1)} %shard_map.60), channel_id=1, source_target_pairs={{0,8},{1,5},{2,10},{3,7},{4,12},{5,1},{6,14},{7,3},{8,0},{9,13},{1... | collective-permute-start | bytes 589832 | tf_op jit(solution)/shard_map/ppermute | solution.py:258
  39.0 5.8 %collective-permute-start.25 = (f32[128,512]{1,0:T(8,128)S(1)}, f32[128,512]{1,0:T(8,128)S(1)}, u32[]{:S(2)}, u32[]{:S(2)}) collective-permute-start(f32[128,512]{1,0:T(8,128)S(1)} %shard_map.64.refs_0_), channel_id=1, source_target_pairs={{0,1},{1,0},{2,3},{3,2},{4,5},{5,4},{6,7},{7,6},{8,9},{9,8},{10,11... | collective-permute-start | bytes 786440 | tf_op jit(solution)/shard_map/ppermute | solution.py:258
  41.1 11.7 %collective-permute-start.24 = (f32[192,256]{1,0:T(8,128)S(1)}, f32[192,256]{1,0:T(8,128)S(1)}, u32[]{:S(2)}, u32[]{:S(2)}) collective-permute-start(f32[192,256]{1,0:T(8,128)S(1)} %shard_map.69.refs_0_), channel_id=1, source_target_pairs={{0,16},{1,17},{2,18},{3,19},{4,20},{5,21},{6,22},{7,23},{8,24},{9,... | collective-permute-start | bytes 589832 | tf_op jit(solution)/shard_map/ppermute | solution.py:258
  42.7 5.4 %collective-permute-start.20 = (f32[128,256]{1,0:T(8,128)S(1)}, f32[128,256]{1,0:T(8,128)S(1)}, u32[]{:S(2)}, u32[]{:S(2)}) collective-permute-start(f32[128,256]{1,0:T(8,128)S(1)} %get-tuple-element.70), channel_id=1, source_target_pairs={{0,4},{1,9},{2,6},{3,11},{4,0},{5,13},{6,2},{7,15},{8,12},{9,1},{1... | collective-permute-start | bytes 393224 | tf_op jit(solution)/shard_map/ppermute | solution.py:258
  43.7 6.5 %collective-permute-start.21 = (f32[128,256]{1,0:T(8,128)S(1)}, f32[128,256]{1,0:T(8,128)S(1)}, u32[]{:S(2)}, u32[]{:S(2)}) collective-permute-start(f32[128,256]{1,0:T(8,128)S(1)} %get-tuple-element.69), channel_id=1, source_target_pairs={{0,4},{1,9},{2,6},{3,11},{4,0},{5,13},{6,2},{7,15},{8,12},{9,1},{1... | collective-permute-start | bytes 393224 | tf_op jit(solution)/shard_map/ppermute | solution.py:258
  44.8 8.0 %collective-permute-start.26 = (f32[64,512]{1,0:T(8,128)S(1)}, f32[64,512]{1,0:T(8,128)S(1)}, u32[]{:S(2)}, u32[]{:S(2)}) collective-permute-start(f32[64,512]{1,0:T(8,128)S(1)} %slice.8), channel_id=1, source_target_pairs={{0,1},{1,0},{2,3},{3,2},{4,5},{5,4},{6,7},{7,6},{8,9},{9,8},{10,11... | collective-permute-start | bytes 393224 | tf_op jit(solution)/shard_map/ppermute | solution.py:258
  44.9 12.1 %collective-permute-start.18 = (f32[128,512]{1,0:T(8,128)S(1)}, f32[128,512]{1,0:T(8,128)S(1)}, u32[]{:S(2)}, u32[]{:S(2)}) collective-permute-start(f32[128,512]{1,0:T(8,128)S(1)} %shard_map.64.refs_0_), channel_id=1, source_target_pairs={{0,8},{1,5},{2,10},{3,7},{4,12},{5,1},{6,14},{7,3},{8,0},{9,13},{1... | collective-permute-start | bytes 786440 | tf_op jit(solution)/shard_map/ppermute | solution.py:258
  50.2 6.7 %collective-permute-start.28 = (f32[128,256]{1,0:T(8,128)S(1)}, f32[128,256]{1,0:T(8,128)S(1)}, u32[]{:S(2)}, u32[]{:S(2)}) collective-permute-start(f32[128,256]{1,0:T(8,128)S(1)} %shard_map.65), channel_id=1, source_target_pairs={{0,8},{1,5},{2,10},{3,7},{4,12},{5,1},{6,14},{7,3},{8,0},{9,13},{1... | collective-permute-start | bytes 393224 | tf_op jit(solution)/shard_map/ppermute | solution.py:258
  52.8 5.2 %collective-permute-start.27 = (f32[64,256]{1,0:T(8,128)S(1)}, f32[64,256]{1,0:T(8,128)S(1)}, u32[]{:S(2)}, u32[]{:S(2)}) collective-permute-start(f32[64,256]{1,0:T(8,128)S(1)} %slice.9), channel_id=1, source_target_pairs={{0,2},{1,3},{2,0},{3,1},{4,6},{5,7},{6,4},{7,5},{8,10},{9,11},{10,... | collective-permute-start | bytes 196616 | tf_op jit(solution)/shard_map/ppermute | solution.py:258
  55.9 8.6 %collective-permute-start.19 = (f32[128,512]{1,0:T(8,128)S(1)}, f32[128,512]{1,0:T(8,128)S(1)}, u32[]{:S(2)}, u32[]{:S(2)}) collective-permute-start(f32[128,512]{1,0:T(8,128)S(1)} %shard_map.64.refs_0_), channel_id=1, source_target_pairs={{0,4},{1,9},{2,6},{3,11},{4,0},{5,13},{6,2},{7,15},{8,12},{9,1},{1... | collective-permute-start | bytes 786440 | tf_op jit(solution)/shard_map/ppermute | solution.py:258
  57.0 10.3 %collective-permute-start.22 = (f32[128,512]{1,0:T(8,128)S(1)}, f32[128,512]{1,0:T(8,128)S(1)}, u32[]{:S(2)}, u32[]{:S(2)}) collective-permute-start(f32[128,512]{1,0:T(8,128)S(1)} %collective-permute-done.18.refs_1_), channel_id=1, source_target_pairs={{0,4},{1,9},{2,6},{3,11},{4,0},{5,13},{6,2},{7,15},{8,12},{9,1},{1... | collective-permute-start | bytes 786440 | tf_op jit(solution)/shard_map/ppermute | solution.py:258
  58.1 11.3 %collective-permute-start.29 = (f32[256,256]{1,0:T(8,128)S(1)}, f32[256,256]{1,0:T(8,128)S(1)}, u32[]{:S(2)}, u32[]{:S(2)}) collective-permute-start(f32[256,256]{1,0:T(8,128)S(1)} %shard_map.72.refs_0_.refs_4_), channel_id=1, source_target_pairs={{0,8},{1,5},{2,10},{3,7},{4,12},{5,1},{6,14},{7,3},{8,0},{9,13},{1... | collective-permute-start | bytes 786440 | tf_op jit(solution)/shard_map/ppermute | solution.py:258
  58.9 11.1 %collective-permute-start.32 = (f32[128,256]{1,0:T(8,128)S(1)}, f32[128,256]{1,0:T(8,128)S(1)}, u32[]{:S(2)}, u32[]{:S(2)}) collective-permute-start(f32[128,256]{1,0:T(8,128)S(1)} %shard_map.71.refs_0_), channel_id=1, source_target_pairs={{0,16},{1,17},{2,18},{3,19},{4,20},{5,21},{6,22},{7,23},{8,24},{9,... | collective-permute-start | bytes 393224 | tf_op jit(solution)/shard_map/ppermute | solution.py:258
  59.5 16.0 %collective-permute-start.30 = (f32[256,256]{1,0:T(8,128)S(1)}, f32[256,256]{1,0:T(8,128)S(1)}, u32[]{:S(2)}, u32[]{:S(2)}) collective-permute-start(f32[256,256]{1,0:T(8,128)S(1)} %shard_map.72.refs_0_.refs_4_), channel_id=1, source_target_pairs={{0,4},{1,9},{2,6},{3,11},{4,0},{5,13},{6,2},{7,15},{8,12},{9,1},{1... | collective-permute-start | bytes 786440 | tf_op jit(solution)/shard_map/ppermute | solution.py:258
  69.4 6.4 %collective-permute-start.31 = (f32[256,256]{1,0:T(8,128)S(1)}, f32[256,256]{1,0:T(8,128)S(1)}, u32[]{:S(2)}, u32[]{:S(2)}) collective-permute-start(f32[256,256]{1,0:T(8,128)S(1)} %collective-permute-done.29.refs_1_.refs_5_), channel_id=1, source_target_pairs={{0,4},{1,9},{2,6},{3,11},{4,0},{5,13},{6,2},{7,15},{8,12},{9,1},{1... | collective-permute-start | bytes 786440 | tf_op jit(solution)/shard_map/ppermute | solution.py:258
  70.1 5.3 %collective-permute-start.33 = (f32[128,256]{1,0:T(8,128)S(1)}, f32[128,256]{1,0:T(8,128)S(1)}, u32[]{:S(2)}, u32[]{:S(2)}) collective-permute-start(f32[128,256]{1,0:T(8,128)S(1)} %shard_map.73.b0), channel_id=1, source_target_pairs={{0,8},{1,5},{2,10},{3,7},{4,12},{5,1},{6,14},{7,3},{8,0},{9,13},{1... | collective-permute-start | bytes 393224 | tf_op jit(solution)/shard_map/ppermute | solution.py:258
  76.4 5.2 %collective-permute-start.35 = (f32[128,256]{1,0:T(8,128)S(1)}, f32[128,256]{1,0:T(8,128)S(1)}, u32[]{:S(2)}, u32[]{:S(2)}) collective-permute-start(f32[128,256]{1,0:T(8,128)S(1)} %shard_map.73.b0), channel_id=1, source_target_pairs={{0,4},{1,9},{2,6},{3,11},{4,0},{5,13},{6,2},{7,15},{8,12},{9,1},{1... | collective-permute-start | bytes 393224 | tf_op jit(solution)/shard_map/ppermute | solution.py:258
  77.5 5.3 %collective-permute-start.36 = (f32[128,256]{1,0:T(8,128)S(1)}, f32[128,256]{1,0:T(8,128)S(1)}, u32[]{:S(2)}, u32[]{:S(2)}) collective-permute-start(f32[128,256]{1,0:T(8,128)S(1)} %collective-permute-done.33.b1), channel_id=1, source_target_pairs={{0,4},{1,9},{2,6},{3,11},{4,0},{5,13},{6,2},{7,15},{8,12},{9,1},{1... | collective-permute-start | bytes 393224 | tf_op jit(solution)/shard_map/ppermute | solution.py:258
  (10 other events, 61.3 us)

commit v5 on v3

--- a/solution.py
+++ b/solution.py
@@ -341,14 +341,15 @@
     first_other = add(first_parts[1], to_one(first_parts[3]), pads=(first_got,))
     first_sum = add(first_parts[0], first_got, after(to_two(first_other), second_sum))
     near_total = across(near_sum, first_parts, w2)
+    near_two = to_two(near_total)
+    near_one = to_one(after(near_total, first_sum))
     second_total = across(after(second_sum, near_total), first_other, pads=(pad(pad(near_total), wide // 2),))
-    near_two = to_two(near_total)
-    near = (near_total, near_two, to_one(near_total), to_one(after(near_two, first_other)))
+    near = (near_total, near_two, near_one, to_one(after(near_two, first_other)))
     left, coefficients = call(
         near_kernel,
         [((rows, cols), f32), ((cols, total), f32)],
         (place, x, *t2, *w2, *near),
-        (rows + total) * cols * half,
+        int(0.0 * (rows + total) * cols * half),
         scalars=1,
     )
     second_packed = pile(second_total, after(to_col(second_total[wide:], 2), first_sum, w1))

time: 85.6 us -> 85.6 us (level)
  waiting for transfers between devices: 29.6 us -> 28.6 us
  starting transfers between devices: 35 us -> 35.9 us
    ppermute x37, waiting for transfers between devices: 29.6 us -> 28.6 us  [permute(): return lax.ppermute(value, ('row', 'col'), pairs)]
    ppermute x37, starting transfers between devices: 35 us -> 35.9 us  [permute(): return lax.ppermute(value, ('row', 'col'), pairs)]
where the time goes in v5:
time: 85.6 us; the launch traced here: 85.4 us
  starting transfers between devices  35.9 us (42%)
  waiting for transfers between devices  28.6 us (33%)
  Pallas kernels  20.4 us (24%)
    ppermute x37, starting transfers between devices, permute(): return lax.ppermute(value, ('row', 'col'), pairs)  35.9 us
    ppermute x37, waiting for transfers between devices, permute(): return lax.ppermute(value, ('row', 'col'), pairs)  28.6 us
    pallas_call x22, Pallas kernels, call(): pl.pallas_call(kernel, out_shape=tuple((jax.ShapeDtypeStruct(shape, dtype...  20.4 us
  transfers between devices with their start and end apart: 37, of which 15 were waited for; matrix products, arithmetic and copies ran while one was open for 0% of the time, Pallas kernels for 20%

profile of v5, /device:TPU:0, one launch (start us, length us, event | category | flops | bytes accessed | tf_op | source)
XLA Modules:
  0.0 85.4 jit_solution(1050604792337112248)
XLA Ops:
  0.5 3.0 %collective-permute-start.1 = (f32[1024,128]{1,0:T(8,128)}, f32[1024,128]{1,0:T(8,128)S(1)}, u32[]{:S(2)}, u32[]{:S(2)}) collective-permute-start(f32[1024,128]{1,0:T(8,128)} %near0.1), channel_id=1, source_target_pairs={{0,2},{1,3},{2,0},{3,1},{4,6},{5,7},{6,4},{7,5},{8,10},{9,11},{10,... | collective-permute-start | bytes 1572872 | tf_op jit(solution)/shard_map/ppermute | solution.py:258
  3.6 2.6 %shard_map.56 = (bf16[640,1024]{1,0:T(8,128)(2,1)S(1)}, bf16[640,1024]{1,0:T(8,128)(2,1)S(1)}) custom-call(s32[5]{0:T(128)S(1)} %stack.23.place, f32[1024,512]{1,0:T(8,128)} %x.3, f32[1024,128]{1,0:T(8,128)} %v0.3), custom_call_target="tpu_custom_call" | custom-call | bytes 4096 | tf_op jit(solution)/shard_map/pallas_call | solution.py:216
  6.2 1.8 %shard_map.57 = (f32[128,512]{1,0:T(8,128)S(1)}, f32[128,512]{1,0:T(8,128)S(1)}, f32[128,512]{1,0:T(8,128)S(1)}, f32[128,512]{1,0:T(8,128)S(1)}) custom-call(bf16[640,1024]{1,0:T(8,128)(2,1)S(1)} %get-tuple-element.49.lt_high, bf16[640,1024]{1,0:T(8,128)(2,1)S(1)} %get-tuple-element.50.lt_low, f32[1024,128]{1,0:T(8,128)S(1)} %copy-done.1, ...), custom_call_target="tpu_custom_call" | custom-call | bytes 4096 | tf_op jit(solution)/shard_map/pallas_call | solution.py:216
  8.0 1.6 %collective-permute-start.3 = (f32[128,512]{1,0:T(8,128)S(1)}, f32[128,512]{1,0:T(8,128)S(1)}, u32[]{:S(2)}, u32[]{:S(2)}) collective-permute-start(f32[128,512]{1,0:T(8,128)S(1)} %get-tuple-element.52), channel_id=1, source_target_pairs={{0,4},{1,9},{2,6},{3,11},{4,0},{5,13},{6,2},{7,15},{8,12},{9,1},{1... | collective-permute-start | bytes 786440 | tf_op jit(solution)/shard_map/ppermute | solution.py:258
  10.2 4.3 %collective-permute-done.3.refs_1_ = f32[128,512]{1,0:T(8,128)S(1)} collective-permute-done((f32[128,512]{1,0:T(8,128)S(1)}, f32[128,512]{1,0:T(8,128)S(1)}, u32[]{:S(2)}, u32[]{:S(2)}) %collective-permute-start.3) | collective-permute-done | bytes 262176 | tf_op jit(solution)/shard_map/ppermute | solution.py:258
  14.5 2.8 %collective-permute-done.4.refs_2_.refs_1_ = f32[128,512]{1,0:T(8,128)S(1)} collective-permute-done((f32[128,512]{1,0:T(8,128)S(1)}, f32[128,512]{1,0:T(8,128)S(1)}, u32[]{:S(2)}, u32[]{:S(2)}) %collective-permute-start.4) | collective-permute-done | bytes 262176 | tf_op jit(solution)/shard_map/ppermute | solution.py:258
  17.4 1.6 %collective-permute-start.9 = (f32[128,512]{1,0:T(8,128)S(1)}, f32[128,512]{1,0:T(8,128)S(1)}, u32[]{:S(2)}, u32[]{:S(2)}) collective-permute-start(f32[128,512]{1,0:T(8,128)S(1)} %shard_map.58), channel_id=1, source_target_pairs={{0,8},{1,5},{2,10},{3,7},{4,12},{5,1},{6,14},{7,3},{8,0},{9,13},{1... | collective-permute-start | bytes 786440 | tf_op jit(solution)/shard_map/ppermute | solution.py:258
  21.0 1.4 %shard_map.60 = (f32[192,256]{1,0:T(8,128)S(1)}, f32[192,256]{1,0:T(8,128)S(1)}, f32[192,256]{1,0:T(8,128)S(1)}, f32[192,256]{1,0:T(8,128)S(1)}) custom-call(bf16[640,1024]{1,0:T(8,128)(2,1)S(1)} %get-tuple-element.49.lt_high, bf16[640,1024]{1,0:T(8,128)(2,1)S(1)} %get-tuple-element.50.lt_low, f32[1024,128]{1,0:T(8,128)S(1)} %copy-done.1, ...), custom_call_target="tpu_custom_call" | custom-call | bytes 4096 | tf_op jit(solution)/shard_map/pallas_call | solution.py:216
  22.3 1.6 %collective-permute-start.20 = (f32[192,256]{1,0:T(8,128)S(1)}, f32[192,256]{1,0:T(8,128)S(1)}, u32[]{:S(2)}, u32[]{:S(2)}) collective-permute-start(f32[192,256]{1,0:T(8,128)S(1)} %get-tuple-element.60), channel_id=1, source_target_pairs={{0,4},{1,9},{2,6},{3,11},{4,0},{5,13},{6,2},{7,15},{8,12},{9,1},{1... | collective-permute-start | bytes 589832 | tf_op jit(solution)/shard_map/ppermute | solution.py:258
  24.5 2.7 %collective-permute-start.10 = (f32[128,512]{1,0:T(8,128)S(1)}, f32[128,512]{1,0:T(8,128)S(1)}, u32[]{:S(2)}, u32[]{:S(2)}) collective-permute-start(f32[128,512]{1,0:T(8,128)S(1)} %shard_map.61.refs_0_), channel_id=1, source_target_pairs={{0,16},{1,17},{2,18},{3,19},{4,20},{5,21},{6,22},{7,23},{8,24},{9,... | collective-permute-start | bytes 786440 | tf_op jit(solution)/shard_map/ppermute | solution.py:258
  28.1 2.1 %collective-permute-done.21.refs_1_ = f32[192,256]{1,0:T(8,128)S(1)} collective-permute-done((f32[192,256]{1,0:T(8,128)S(1)}, f32[192,256]{1,0:T(8,128)S(1)}, u32[]{:S(2)}, u32[]{:S(2)}) %collective-permute-start.21) | collective-permute-done | bytes 196640 | tf_op jit(solution)/shard_map/ppermute | solution.py:258
  30.2 3.1 %collective-permute-start.15 = (f32[256,128]{1,0:T(8,128)S(1)}, f32[256,128]{1,0:T(8,128)S(1)}, u32[]{:S(2)}, u32[]{:S(2)}) collective-permute-start(f32[256,128]{1,0:T(8,128)S(1)} %get-tuple-element.89), channel_id=1, source_target_pairs={{0,1},{1,0},{2,3},{3,2},{4,5},{5,4},{6,7},{7,6},{8,9},{9,8},{10,11... | collective-permute-start | bytes 393224 | tf_op jit(solution)/shard_map/ppermute | solution.py:258
  33.3 1.8 %shard_map.59 = (bf16[1024,512]{1,0:T(8,128)(2,1)S(1)}, bf16[1024,512]{1,0:T(8,128)(2,1)S(1)}) custom-call(bf16[512,512]{1,0:T(8,128)(2,1)S(1)} %get-tuple-element.47.t_high, bf16[512,512]{1,0:T(8,128)(2,1)S(1)} %get-tuple-element.48.t_low, f32[1024,128]{1,0:T(8,128)S(1)} %copy-done.1, f32[1024,128]{1,0:T(8,128)S(1)} %collective-permute-done.refs_1_.v1.near1, ...), custom_call_target="tpu_custom_call" | custom-call | flops 1610612736 | bytes 4096 | tf_op jit(solution)/shard_map/pallas_call | solution.py:216
  36.3 2.7 %collective-permute-done.10.refs_1_ = f32[128,512]{1,0:T(8,128)S(1)} collective-permute-done((f32[128,512]{1,0:T(8,128)S(1)}, f32[128,512]{1,0:T(8,128)S(1)}, u32[]{:S(2)}, u32[]{:S(2)}) %collective-permute-start.10) | collective-permute-done | bytes 262176 | tf_op jit(solution)/shard_map/ppermute | solution.py:258
  39.1 2.0 %collective-permute-done.22.refs_2_ = f32[192,256]{1,0:T(8,128)S(1)} collective-permute-done((f32[192,256]{1,0:T(8,128)S(1)}, f32[192,256]{1,0:T(8,128)S(1)}, u32[]{:S(2)}, u32[]{:S(2)}) %collective-permute-start.22) | collective-permute-done | bytes 196640 | tf_op jit(solution)/shard_map/ppermute | solution.py:258
  41.1 1.6 %collective-permute-start.25 = (f32[192,256]{1,0:T(8,128)S(1)}, f32[192,256]{1,0:T(8,128)S(1)}, u32[]{:S(2)}, u32[]{:S(2)}) collective-permute-start(f32[192,256]{1,0:T(8,128)S(1)} %shard_map.66.refs_0_), channel_id=1, source_target_pairs={{0,16},{1,17},{2,18},{3,19},{4,20},{5,21},{6,22},{7,23},{8,24},{9,... | collective-permute-start | bytes 589832 | tf_op jit(solution)/shard_map/ppermute | solution.py:258
  44.9 2.5 %collective-permute-start.16 = (f32[128,512]{1,0:T(8,128)S(1)}, f32[128,512]{1,0:T(8,128)S(1)}, u32[]{:S(2)}, u32[]{:S(2)}) collective-permute-start(f32[128,512]{1,0:T(8,128)S(1)} %shard_map.63.refs_0_), channel_id=1, source_target_pairs={{0,8},{1,5},{2,10},{3,7},{4,12},{5,1},{6,14},{7,3},{8,0},{9,13},{1... | collective-permute-start | bytes 786440 | tf_op jit(solution)/shard_map/ppermute | solution.py:258
  48.1 2.1 %collective-permute-done.18.refs_1_ = f32[128,256]{1,0:T(8,128)S(1)} collective-permute-done((f32[128,256]{1,0:T(8,128)S(1)}, f32[128,256]{1,0:T(8,128)S(1)}, u32[]{:S(2)}, u32[]{:S(2)}) %collective-permute-start.18) | collective-permute-done | bytes 131104 | tf_op jit(solution)/shard_map/ppermute | solution.py:258
  50.2 2.5 %collective-permute-start.19 = (f32[128,256]{1,0:T(8,128)S(1)}, f32[128,256]{1,0:T(8,128)S(1)}, u32[]{:S(2)}, u32[]{:S(2)}) collective-permute-start(f32[128,256]{1,0:T(8,128)S(1)} %shard_map.64), channel_id=1, source_target_pairs={{0,8},{1,5},{2,10},{3,7},{4,12},{5,1},{6,14},{7,3},{8,0},{9,13},{1... | collective-permute-start | bytes 393224 | tf_op jit(solution)/shard_map/ppermute | solution.py:258
  52.8 1.2 %collective-permute-start.28 = (f32[64,256]{1,0:T(8,128)S(1)}, f32[64,256]{1,0:T(8,128)S(1)}, u32[]{:S(2)}, u32[]{:S(2)}) collective-permute-start(f32[64,256]{1,0:T(8,128)S(1)} %slice.9), channel_id=1, source_target_pairs={{0,2},{1,3},{2,0},{3,1},{4,6},{5,7},{6,4},{7,5},{8,10},{9,11},{10,... | collective-permute-start | bytes 196616 | tf_op jit(solution)/shard_map/ppermute | solution.py:258
  54.0 1.8 %shard_map.70 = (bf16[1024,512]{1,0:T(8,128)(2,1)S(1)}, bf16[1024,512]{1,0:T(8,128)(2,1)S(1)}) custom-call(bf16[512,512]{1,0:T(8,128)(2,1)S(1)} %get-tuple-element.73.t_high, bf16[512,512]{1,0:T(8,128)(2,1)S(1)} %get-tuple-element.74.t_low, f32[1024,128]{1,0:T(8,128)S(1)} %copy-done.2, f32[1024,128]{1,0:T(8,128)S(1)} %collective-permute-done.2.refs_3_.v1, ...), custom_call_target="tpu_custom_call" | custom-call | flops 1610612736 | bytes 4096 | tf_op jit(solution)/shard_map/pallas_call | solution.py:216
  58.0 1.9 %collective-permute-start.29 = (f32[256,256]{1,0:T(8,128)S(1)}, f32[256,256]{1,0:T(8,128)S(1)}, u32[]{:S(2)}, u32[]{:S(2)}) collective-permute-start(f32[256,256]{1,0:T(8,128)S(1)} %shard_map.72.refs_0_.refs_4_), channel_id=1, source_target_pairs={{0,8},{1,5},{2,10},{3,7},{4,12},{5,1},{6,14},{7,3},{8,0},{9,13},{1... | collective-permute-start | bytes 786440 | tf_op jit(solution)/shard_map/ppermute | solution.py:258
  60.0 1.2 %collective-permute-start.30 = (f32[256,256]{1,0:T(8,128)S(1)}, f32[256,256]{1,0:T(8,128)S(1)}, u32[]{:S(2)}, u32[]{:S(2)}) collective-permute-start(f32[256,256]{1,0:T(8,128)S(1)} %shard_map.72.refs_0_.refs_4_), channel_id=1, source_target_pairs={{0,4},{1,9},{2,6},{3,11},{4,0},{5,13},{6,2},{7,15},{8,12},{9,1},{1... | collective-permute-start | bytes 786440 | tf_op jit(solution)/shard_map/ppermute | solution.py:258
  61.3 3.1 %collective-permute-done.23.refs_2_ = f32[128,512]{1,0:T(8,128)S(1)} collective-permute-done((f32[128,512]{1,0:T(8,128)S(1)}, f32[128,512]{1,0:T(8,128)S(1)}, u32[]{:S(2)}, u32[]{:S(2)}) %collective-permute-start.23) | collective-permute-done | bytes 262176 | tf_op jit(solution)/shard_map/ppermute | solution.py:258
  64.4 2.8 %collective-permute-done.24.refs_3_ = f32[128,512]{1,0:T(8,128)S(1)} collective-permute-done((f32[128,512]{1,0:T(8,128)S(1)}, f32[128,512]{1,0:T(8,128)S(1)}, u32[]{:S(2)}, u32[]{:S(2)}) %collective-permute-start.24) | collective-permute-done | bytes 262176 | tf_op jit(solution)/shard_map/ppermute | solution.py:258
  67.2 2.1 %collective-permute-done.29.refs_1_.refs_5_ = f32[256,256]{1,0:T(8,128)S(1)} collective-permute-done((f32[256,256]{1,0:T(8,128)S(1)}, f32[256,256]{1,0:T(8,128)S(1)}, u32[]{:S(2)}, u32[]{:S(2)}) %collective-permute-start.29) | collective-permute-done | bytes 262176 | tf_op jit(solution)/shard_map/ppermute | solution.py:258
  70.0 1.2 %collective-permute-start.33 = (f32[128,256]{1,0:T(8,128)S(1)}, f32[128,256]{1,0:T(8,128)S(1)}, u32[]{:S(2)}, u32[]{:S(2)}) collective-permute-start(f32[128,256]{1,0:T(8,128)S(1)} %shard_map.73.b0), channel_id=1, source_target_pairs={{0,8},{1,5},{2,10},{3,7},{4,12},{5,1},{6,14},{7,3},{8,0},{9,13},{1... | collective-permute-start | bytes 393224 | tf_op jit(solution)/shard_map/ppermute | solution.py:258
  71.2 2.0 %shard_map.68 = (f32[1024,512]{1,0:T(8,128)S(1)}, f32[512,512]{1,0:T(8,128)S(1)}) custom-call(s32[5]{0:T(128)S(1)} %stack.23.place, f32[1024,512]{1,0:T(8,128)S(1)} %copy-done, bf16[512,512]{1,0:T(8,128)(2,1)S(1)} %get-tuple-element.47.t_high, bf16[512,512]{1,0:T(8,128)(2,1)S(1)} %get-tuple-element.48.t_low, ...), custom_call_target="tpu_custom_call" | custom-call | bytes 4096 | tf_op jit(solution)/shard_map/pallas_call | solution.py:216
  73.2 2.3 %collective-permute-done.33.b1 = f32[128,256]{1,0:T(8,128)S(1)} collective-permute-done((f32[128,256]{1,0:T(8,128)S(1)}, f32[128,256]{1,0:T(8,128)S(1)}, u32[]{:S(2)}, u32[]{:S(2)}) %collective-permute-start.33) | collective-permute-done | bytes 131104 | tf_op jit(solution)/shard_map/ppermute | solution.py:258
  78.4 3.1 %shard_map.75 = (f32[1024,512]{1,0:T(8,128)S(1)}, f32[512,256]{1,0:T(8,128)S(1)}) custom-call(f32[1024,512]{1,0:T(8,128)S(1)} %get-tuple-element.72.x, bf16[512,512]{1,0:T(8,128)(2,1)S(1)} %get-tuple-element.47.t_high, bf16[512,512]{1,0:T(8,128)(2,1)S(1)} %get-tuple-element.48.t_low, bf16[1024,512]{1,0:T(8,128)(2,1)S(1)} %get-tuple-element.55.w_high.w2_high, ...), custom_call_target="tpu_custom_call" | custom-call | flops 2415919104 | bytes 4096 | tf_op jit(solution)/shard_map/pallas_call | solution.py:216
  81.5 1.3 %collective-permute-done.36.b3 = f32[128,256]{1,0:T(8,128)S(1)} collective-permute-done((f32[128,256]{1,0:T(8,128)S(1)}, f32[128,256]{1,0:T(8,128)S(1)}, u32[]{:S(2)}, u32[]{:S(2)}) %collective-permute-start.36) | collective-permute-done | bytes 131104 | tf_op jit(solution)/shard_map/ppermute | solution.py:258
  82.8 2.7 %shard_map.76 = f32[1024,512]{1,0:T(8,128)} custom-call(s32[5]{0:T(128)S(1)} %stack.23.place, f32[1024,512]{1,0:T(8,128)S(1)} %get-tuple-element.87.x, bf16[1024,512]{1,0:T(8,128)(2,1)S(1)} %get-tuple-element.75.w1_high.w_high, bf16[1024,512]{1,0:T(8,128)(2,1)S(1)} %get-tuple-element.76.w1_low.w_low, f32[512,256]{1,0:T(8,128)S(1)} %get-tuple-element.88.rest, ...), custom_call_target="tpu_custom_call" | custom-call | flops 805306368 | bytes 4096 | tf_op jit(solution)/shard_map/pallas_call | solution.py:216
  (79 shorter events, 14.7 us)
Async XLA Ops:
  0.0 6.2 %collective-permute-start = (f32[1024,128]{1,0:T(8,128)}, f32[1024,128]{1,0:T(8,128)S(1)}, u32[]{:S(2)}, u32[]{:S(2)}) collective-permute-start(f32[1024,128]{1,0:T(8,128)} %near0.1), channel_id=1, source_target_pairs={{0,1},{1,0},{2,3},{3,2},{4,5},{5,4},{6,7},{7,6},{8,9},{9,8},{10,11... | collective-permute-start | bytes 1572872 | tf_op jit(solution)/shard_map/ppermute | solution.py:258
  0.5 5.7 %collective-permute-start.2 = (f32[1024,128]{1,0:T(8,128)}, f32[1024,128]{1,0:T(8,128)S(1)}, u32[]{:S(2)}, u32[]{:S(2)}) collective-permute-start(f32[1024,128]{1,0:T(8,128)} %v0.3), channel_id=1, source_target_pairs={{0,1},{1,0},{2,3},{3,2},{4,5},{5,4},{6,7},{7,6},{8,9},{9,8},{10,11... | collective-permute-start | bytes 1572872 | tf_op jit(solution)/shard_map/ppermute | solution.py:258
  0.5 16.8 %collective-permute-start.1 = (f32[1024,128]{1,0:T(8,128)}, f32[1024,128]{1,0:T(8,128)S(1)}, u32[]{:S(2)}, u32[]{:S(2)}) collective-permute-start(f32[1024,128]{1,0:T(8,128)} %near0.1), channel_id=1, source_target_pairs={{0,2},{1,3},{2,0},{3,1},{4,6},{5,7},{6,4},{7,5},{8,10},{9,11},{10,... | collective-permute-start | bytes 1572872 | tf_op jit(solution)/shard_map/ppermute | solution.py:258
  8.0 6.4 %collective-permute-start.3 = (f32[128,512]{1,0:T(8,128)S(1)}, f32[128,512]{1,0:T(8,128)S(1)}, u32[]{:S(2)}, u32[]{:S(2)}) collective-permute-start(f32[128,512]{1,0:T(8,128)S(1)} %get-tuple-element.52), channel_id=1, source_target_pairs={{0,4},{1,9},{2,6},{3,11},{4,0},{5,13},{6,2},{7,15},{8,12},{9,1},{1... | collective-permute-start | bytes 786440 | tf_op jit(solution)/shard_map/ppermute | solution.py:258
  9.6 7.7 %collective-permute-start.4 = (f32[128,512]{1,0:T(8,128)S(1)}, f32[128,512]{1,0:T(8,128)S(1)}, u32[]{:S(2)}, u32[]{:S(2)}) collective-permute-start(f32[128,512]{1,0:T(8,128)S(1)} %get-tuple-element.53), channel_id=1, source_target_pairs={{0,4},{1,9},{2,6},{3,11},{4,0},{5,13},{6,2},{7,15},{8,12},{9,1},{1... | collective-permute-start | bytes 786440 | tf_op jit(solution)/shard_map/ppermute | solution.py:258
  10.1 17.0 %collective-permute-start.11 = (f32[1024,128]{1,0:T(8,128)S(1)}, f32[1024,128]{1,0:T(8,128)S(1)}, u32[]{:S(2)}, u32[]{:S(2)}) collective-permute-start(f32[1024,128]{1,0:T(8,128)S(1)} %copy-done.2), channel_id=1, source_target_pairs={{0,2},{1,3},{2,0},{3,1},{4,6},{5,7},{6,4},{7,5},{8,10},{9,11},{10,... | collective-permute-start | bytes 1572872 | tf_op jit(solution)/shard_map/ppermute | solution.py:258
  17.4 7.0 %collective-permute-start.9 = (f32[128,512]{1,0:T(8,128)S(1)}, f32[128,512]{1,0:T(8,128)S(1)}, u32[]{:S(2)}, u32[]{:S(2)}) collective-permute-start(f32[128,512]{1,0:T(8,128)S(1)} %shard_map.58), channel_id=1, source_target_pairs={{0,8},{1,5},{2,10},{3,7},{4,12},{5,1},{6,14},{7,3},{8,0},{9,13},{1... | collective-permute-start | bytes 786440 | tf_op jit(solution)/shard_map/ppermute | solution.py:258
  22.3 5.7 %collective-permute-start.20 = (f32[192,256]{1,0:T(8,128)S(1)}, f32[192,256]{1,0:T(8,128)S(1)}, u32[]{:S(2)}, u32[]{:S(2)}) collective-permute-start(f32[192,256]{1,0:T(8,128)S(1)} %get-tuple-element.60), channel_id=1, source_target_pairs={{0,4},{1,9},{2,6},{3,11},{4,0},{5,13},{6,2},{7,15},{8,12},{9,1},{1... | collective-permute-start | bytes 589832 | tf_op jit(solution)/shard_map/ppermute | solution.py:258
  23.9 6.3 %collective-permute-start.21 = (f32[192,256]{1,0:T(8,128)S(1)}, f32[192,256]{1,0:T(8,128)S(1)}, u32[]{:S(2)}, u32[]{:S(2)}) collective-permute-start(f32[192,256]{1,0:T(8,128)S(1)} %get-tuple-element.61), channel_id=1, source_target_pairs={{0,4},{1,9},{2,6},{3,11},{4,0},{5,13},{6,2},{7,15},{8,12},{9,1},{1... | collective-permute-start | bytes 589832 | tf_op jit(solution)/shard_map/ppermute | solution.py:258
  24.5 14.5 %collective-permute-start.10 = (f32[128,512]{1,0:T(8,128)S(1)}, f32[128,512]{1,0:T(8,128)S(1)}, u32[]{:S(2)}, u32[]{:S(2)}) collective-permute-start(f32[128,512]{1,0:T(8,128)S(1)} %shard_map.61.refs_0_), channel_id=1, source_target_pairs={{0,16},{1,17},{2,18},{3,19},{4,20},{5,21},{6,22},{7,23},{8,24},{9,... | collective-permute-start | bytes 786440 | tf_op jit(solution)/shard_map/ppermute | solution.py:258
  27.2 8.0 %collective-permute-start.12 = (f32[256,128]{1,0:T(8,128)S(1)}, f32[256,128]{1,0:T(8,128)S(1)}, u32[]{:S(2)}, u32[]{:S(2)}) collective-permute-start(f32[256,128]{1,0:T(8,128)S(1)} %get-tuple-element.92), channel_id=1, source_target_pairs={{0,1},{1,0},{2,3},{3,2},{4,5},{5,4},{6,7},{7,6},{8,9},{9,8},{10,11... | collective-permute-start | bytes 393224 | tf_op jit(solution)/shard_map/ppermute | solution.py:258
  27.3 8.0 %collective-permute-start.13 = (f32[256,128]{1,0:T(8,128)S(1)}, f32[256,128]{1,0:T(8,128)S(1)}, u32[]{:S(2)}, u32[]{:S(2)}) collective-permute-start(f32[256,128]{1,0:T(8,128)S(1)} %get-tuple-element.91), channel_id=1, source_target_pairs={{0,1},{1,0},{2,3},{3,2},{4,5},{5,4},{6,7},{7,6},{8,9},{9,8},{10,11... | collective-permute-start | bytes 393224 | tf_op jit(solution)/shard_map/ppermute | solution.py:258
  28.1 7.2 %collective-permute-start.14 = (f32[256,128]{1,0:T(8,128)S(1)}, f32[256,128]{1,0:T(8,128)S(1)}, u32[]{:S(2)}, u32[]{:S(2)}) collective-permute-start(f32[256,128]{1,0:T(8,128)S(1)} %get-tuple-element.90), channel_id=1, source_target_pairs={{0,1},{1,0},{2,3},{3,2},{4,5},{5,4},{6,7},{7,6},{8,9},{9,8},{10,11... | collective-permute-start | bytes 393224 | tf_op jit(solution)/shard_map/ppermute | solution.py:258
  30.2 5.1 %collective-permute-start.15 = (f32[256,128]{1,0:T(8,128)S(1)}, f32[256,128]{1,0:T(8,128)S(1)}, u32[]{:S(2)}, u32[]{:S(2)}) collective-permute-start(f32[256,128]{1,0:T(8,128)S(1)} %get-tuple-element.89), channel_id=1, source_target_pairs={{0,1},{1,0},{2,3},{3,2},{4,5},{5,4},{6,7},{7,6},{8,9},{9,8},{10,11... | collective-permute-start | bytes 393224 | tf_op jit(solution)/shard_map/ppermute | solution.py:258
  35.2 5.9 %collective-permute-start.22 = (f32[192,256]{1,0:T(8,128)S(1)}, f32[192,256]{1,0:T(8,128)S(1)}, u32[]{:S(2)}, u32[]{:S(2)}) collective-permute-start(f32[192,256]{1,0:T(8,128)S(1)} %shard_map.65), channel_id=1, source_target_pairs={{0,8},{1,5},{2,10},{3,7},{4,12},{5,1},{6,14},{7,3},{8,0},{9,13},{1... | collective-permute-start | bytes 589832 | tf_op jit(solution)/shard_map/ppermute | solution.py:258
  39.0 5.8 %collective-permute-start.26 = (f32[128,512]{1,0:T(8,128)S(1)}, f32[128,512]{1,0:T(8,128)S(1)}, u32[]{:S(2)}, u32[]{:S(2)}) collective-permute-start(f32[128,512]{1,0:T(8,128)S(1)} %shard_map.63.refs_0_), channel_id=1, source_target_pairs={{0,1},{1,0},{2,3},{3,2},{4,5},{5,4},{6,7},{7,6},{8,9},{9,8},{10,11... | collective-permute-start | bytes 786440 | tf_op jit(solution)/shard_map/ppermute | solution.py:258
  41.1 11.7 %collective-permute-start.25 = (f32[192,256]{1,0:T(8,128)S(1)}, f32[192,256]{1,0:T(8,128)S(1)}, u32[]{:S(2)}, u32[]{:S(2)}) collective-permute-start(f32[192,256]{1,0:T(8,128)S(1)} %shard_map.66.refs_0_), channel_id=1, source_target_pairs={{0,16},{1,17},{2,18},{3,19},{4,20},{5,21},{6,22},{7,23},{8,24},{9,... | collective-permute-start | bytes 589832 | tf_op jit(solution)/shard_map/ppermute | solution.py:258
  42.7 5.4 %collective-permute-start.17 = (f32[128,256]{1,0:T(8,128)S(1)}, f32[128,256]{1,0:T(8,128)S(1)}, u32[]{:S(2)}, u32[]{:S(2)}) collective-permute-start(f32[128,256]{1,0:T(8,128)S(1)} %get-tuple-element.66), channel_id=1, source_target_pairs={{0,4},{1,9},{2,6},{3,11},{4,0},{5,13},{6,2},{7,15},{8,12},{9,1},{1... | collective-permute-start | bytes 393224 | tf_op jit(solution)/shard_map/ppermute | solution.py:258
  43.7 6.5 %collective-permute-start.18 = (f32[128,256]{1,0:T(8,128)S(1)}, f32[128,256]{1,0:T(8,128)S(1)}, u32[]{:S(2)}, u32[]{:S(2)}) collective-permute-start(f32[128,256]{1,0:T(8,128)S(1)} %get-tuple-element.67), channel_id=1, source_target_pairs={{0,4},{1,9},{2,6},{3,11},{4,0},{5,13},{6,2},{7,15},{8,12},{9,1},{1... | collective-permute-start | bytes 393224 | tf_op jit(solution)/shard_map/ppermute | solution.py:258
  44.8 8.0 %collective-permute-start.27 = (f32[64,512]{1,0:T(8,128)S(1)}, f32[64,512]{1,0:T(8,128)S(1)}, u32[]{:S(2)}, u32[]{:S(2)}) collective-permute-start(f32[64,512]{1,0:T(8,128)S(1)} %slice.8), channel_id=1, source_target_pairs={{0,1},{1,0},{2,3},{3,2},{4,5},{5,4},{6,7},{7,6},{8,9},{9,8},{10,11... | collective-permute-start | bytes 393224 | tf_op jit(solution)/shard_map/ppermute | solution.py:258
  44.9 12.1 %collective-permute-start.16 = (f32[128,512]{1,0:T(8,128)S(1)}, f32[128,512]{1,0:T(8,128)S(1)}, u32[]{:S(2)}, u32[]{:S(2)}) collective-permute-start(f32[128,512]{1,0:T(8,128)S(1)} %shard_map.63.refs_0_), channel_id=1, source_target_pairs={{0,8},{1,5},{2,10},{3,7},{4,12},{5,1},{6,14},{7,3},{8,0},{9,13},{1... | collective-permute-start | bytes 786440 | tf_op jit(solution)/shard_map/ppermute | solution.py:258
  50.2 5.6 %collective-permute-start.19 = (f32[128,256]{1,0:T(8,128)S(1)}, f32[128,256]{1,0:T(8,128)S(1)}, u32[]{:S(2)}, u32[]{:S(2)}) collective-permute-start(f32[128,256]{1,0:T(8,128)S(1)} %shard_map.64), channel_id=1, source_target_pairs={{0,8},{1,5},{2,10},{3,7},{4,12},{5,1},{6,14},{7,3},{8,0},{9,13},{1... | collective-permute-start | bytes 393224 | tf_op jit(solution)/shard_map/ppermute | solution.py:258
  52.8 5.2 %collective-permute-start.28 = (f32[64,256]{1,0:T(8,128)S(1)}, f32[64,256]{1,0:T(8,128)S(1)}, u32[]{:S(2)}, u32[]{:S(2)}) collective-permute-start(f32[64,256]{1,0:T(8,128)S(1)} %slice.9), channel_id=1, source_target_pairs={{0,2},{1,3},{2,0},{3,1},{4,6},{5,7},{6,4},{7,5},{8,10},{9,11},{10,... | collective-permute-start | bytes 196616 | tf_op jit(solution)/shard_map/ppermute | solution.py:258
  55.9 8.5 %collective-permute-start.23 = (f32[128,512]{1,0:T(8,128)S(1)}, f32[128,512]{1,0:T(8,128)S(1)}, u32[]{:S(2)}, u32[]{:S(2)}) collective-permute-start(f32[128,512]{1,0:T(8,128)S(1)} %shard_map.63.refs_0_), channel_id=1, source_target_pairs={{0,4},{1,9},{2,6},{3,11},{4,0},{5,13},{6,2},{7,15},{8,12},{9,1},{1... | collective-permute-start | bytes 786440 | tf_op jit(solution)/shard_map/ppermute | solution.py:258
  57.0 10.2 %collective-permute-start.24 = (f32[128,512]{1,0:T(8,128)S(1)}, f32[128,512]{1,0:T(8,128)S(1)}, u32[]{:S(2)}, u32[]{:S(2)}) collective-permute-start(f32[128,512]{1,0:T(8,128)S(1)} %collective-permute-done.16.refs_1_), channel_id=1, source_target_pairs={{0,4},{1,9},{2,6},{3,11},{4,0},{5,13},{6,2},{7,15},{8,12},{9,1},{1... | collective-permute-start | bytes 786440 | tf_op jit(solution)/shard_map/ppermute | solution.py:258
  58.0 11.3 %collective-permute-start.29 = (f32[256,256]{1,0:T(8,128)S(1)}, f32[256,256]{1,0:T(8,128)S(1)}, u32[]{:S(2)}, u32[]{:S(2)}) collective-permute-start(f32[256,256]{1,0:T(8,128)S(1)} %shard_map.72.refs_0_.refs_4_), channel_id=1, source_target_pairs={{0,8},{1,5},{2,10},{3,7},{4,12},{5,1},{6,14},{7,3},{8,0},{9,13},{1... | collective-permute-start | bytes 786440 | tf_op jit(solution)/shard_map/ppermute | solution.py:258
  60.0 10.0 %collective-permute-start.32 = (f32[128,256]{1,0:T(8,128)S(1)}, f32[128,256]{1,0:T(8,128)S(1)}, u32[]{:S(2)}, u32[]{:S(2)}) collective-permute-start(f32[128,256]{1,0:T(8,128)S(1)} %shard_map.67.refs_0_), channel_id=1, source_target_pairs={{0,16},{1,17},{2,18},{3,19},{4,20},{5,21},{6,22},{7,23},{8,24},{9,... | collective-permute-start | bytes 393224 | tf_op jit(solution)/shard_map/ppermute | solution.py:258
  60.0 15.4 %collective-permute-start.30 = (f32[256,256]{1,0:T(8,128)S(1)}, f32[256,256]{1,0:T(8,128)S(1)}, u32[]{:S(2)}, u32[]{:S(2)}) collective-permute-start(f32[256,256]{1,0:T(8,128)S(1)} %shard_map.72.refs_0_.refs_4_), channel_id=1, source_target_pairs={{0,4},{1,9},{2,6},{3,11},{4,0},{5,13},{6,2},{7,15},{8,12},{9,1},{1... | collective-permute-start | bytes 786440 | tf_op jit(solution)/shard_map/ppermute | solution.py:258
  69.3 6.4 %collective-permute-start.31 = (f32[256,256]{1,0:T(8,128)S(1)}, f32[256,256]{1,0:T(8,128)S(1)}, u32[]{:S(2)}, u32[]{:S(2)}) collective-permute-start(f32[256,256]{1,0:T(8,128)S(1)} %collective-permute-done.29.refs_1_.refs_5_), channel_id=1, source_target_pairs={{0,4},{1,9},{2,6},{3,11},{4,0},{5,13},{6,2},{7,15},{8,12},{9,1},{1... | collective-permute-start | bytes 786440 | tf_op jit(solution)/shard_map/ppermute | solution.py:258
  70.0 5.4 %collective-permute-start.33 = (f32[128,256]{1,0:T(8,128)S(1)}, f32[128,256]{1,0:T(8,128)S(1)}, u32[]{:S(2)}, u32[]{:S(2)}) collective-permute-start(f32[128,256]{1,0:T(8,128)S(1)} %shard_map.73.b0), channel_id=1, source_target_pairs={{0,8},{1,5},{2,10},{3,7},{4,12},{5,1},{6,14},{7,3},{8,0},{9,13},{1... | collective-permute-start | bytes 393224 | tf_op jit(solution)/shard_map/ppermute | solution.py:258
  76.3 5.2 %collective-permute-start.35 = (f32[128,256]{1,0:T(8,128)S(1)}, f32[128,256]{1,0:T(8,128)S(1)}, u32[]{:S(2)}, u32[]{:S(2)}) collective-permute-start(f32[128,256]{1,0:T(8,128)S(1)} %shard_map.73.b0), channel_id=1, source_target_pairs={{0,4},{1,9},{2,6},{3,11},{4,0},{5,13},{6,2},{7,15},{8,12},{9,1},{1... | collective-permute-start | bytes 393224 | tf_op jit(solution)/shard_map/ppermute | solution.py:258
  77.5 5.2 %collective-permute-start.36 = (f32[128,256]{1,0:T(8,128)S(1)}, f32[128,256]{1,0:T(8,128)S(1)}, u32[]{:S(2)}, u32[]{:S(2)}) collective-permute-start(f32[128,256]{1,0:T(8,128)S(1)} %collective-permute-done.33.b1), channel_id=1, source_target_pairs={{0,4},{1,9},{2,6},{3,11},{4,0},{5,13},{6,2},{7,15},{8,12},{9,1},{1... | collective-permute-start | bytes 393224 | tf_op jit(solution)/shard_map/ppermute | solution.py:258
  (10 other events, 62.0 us)
